TPU v7x, 32 devices: a whole 2x2x4 slice. The times are simulated.
32 devices in a mesh: grp: 4 (over y, core), dev: 8 (over z, x).
Axes of the slice: x: 2, y: 2, z: 4, core: 2. Of those that a mesh axis runs over, the one named last changes fastest.
Arguments:
- tiles: bfloat16 [16384, 128, 128], P(('grp', 'dev')), may hold values from -0.125 to 0.125
- tile_ray: int32 [16384], P(('grp', 'dev')), may hold values from 0 to 31, as said below
- tile_col: int32 [16384], P(('grp', 'dev')), may hold values from 0 to 23, as said below
- touched: int32 [768], P(('grp', 'dev')), may hold values from 0 to 2047, as said below
- home: int32 [2048], replicated, may hold values from 0 to 2047, as said below
- sketch: bfloat16 [262144, 128], P(('grp', 'dev')), may hold values from -6 to 6
Outputs:
- basis: float32 [262144, 128], P(('grp', 'dev'))
- r_factor: float32 [128, 128], replicated
Inputs may be any that keep to these rules, and one draw needn't show every extreme that they name: `home`: A permutation that maps each region of 512 consecutive voxel blocks, g * 512 to (g + 1) * 512 - 1, onto the same range of positions. The 24 entries of device i along grp+dev are distinct voxel blocks whose positions home[v] lie in the region of its group g = i // 8; at most 3 of them have positions stored on any one device (position // 64), and in every group one device stores 3 of the touched blocks of every device of the group. On each device the pairs (tile_ray, tile_col) are distinct. `tile_col`: indexes the device's own 24 entries of touched.
All inputs are finite; a program needn't handle non-finite values.
Results may differ from a plain program's by a relative error of at most 0.0017.
Values may be sent and summed in bfloat16 or wider, within the bound.
No kernel may reach another device: no remote copies, remote signals or barrier semaphores. Data moves between devices by JAX's collectives and lax.ppermute only.
A program may use at most 192 MiB of HBM per device.

v0:
```python
import jax
import jax.numpy as jnp
from jax import lax
from jax.sharding import PartitionSpec as P

CAP = 3
RB_DEV = 32


gram_shift = 0.001


def factor_lower(gram_matrix):
    width = gram_matrix.shape[0]
    indices = jnp.arange(width, dtype=jnp.int32)

    def column_step(column, lower):
        pick = (indices == column).astype(jnp.float32)
        row_part = jnp.dot(pick, lower, precision=lax.Precision.HIGHEST)
        target = jnp.dot(gram_matrix, pick, precision=lax.Precision.HIGHEST)
        rest = target - jnp.dot(lower, row_part, precision=lax.Precision.HIGHEST)
        diagonal = jnp.sqrt(jnp.sum(rest * pick))
        fresh = jnp.where(
            indices > column, rest / diagonal, jnp.where(indices == column, diagonal, 0.0)
        )
        return lower + fresh[:, None] * pick[None, :]

    return lax.fori_loop(0, width, column_step, jnp.zeros((width, width), jnp.float32))


def invert_lower(lower):
    width = lower.shape[0]
    indices = jnp.arange(width, dtype=jnp.int32)

    def row_step(row, inverse):
        pick = (indices == row).astype(jnp.float32)
        row_part = jnp.dot(pick, lower, precision=lax.Precision.HIGHEST)
        diagonal = jnp.sum(row_part * pick)
        fresh = (pick - jnp.dot(row_part, inverse, precision=lax.Precision.HIGHEST)) / diagonal
        return inverse + pick[:, None] * fresh[None, :]

    return lax.fori_loop(0, width, row_step, jnp.zeros((width, width), jnp.float32))


def local(tiles, tile_ray, tile_col, touched, home, sketch):
    group_size = lax.axis_size("dev")
    tile_size = tiles.shape[1]
    width = sketch.shape[1]
    block_count = sketch.shape[0] // tile_size
    ntouch = touched.shape[0]
    slot_count = group_size * CAP
    matches = touched[:, None] == jnp.arange(home.shape[0], dtype=jnp.int32)[None, :]
    stored = jnp.sum(jnp.where(matches, home[None, :], 0), axis=1)
    holder = stored // block_count % group_size
    local_row = stored % block_count
    counter = jnp.arange(ntouch, dtype=jnp.int32)
    earlier = (holder[:, None] == holder[None, :]) & (counter[:, None] > counter[None, :])
    position = holder * CAP + jnp.sum(earlier, axis=1)
    placing = position[:, None] == jnp.arange(slot_count, dtype=jnp.int32)[None, :]
    request = (jnp.sum(jnp.where(placing, local_row[:, None] + 1, 0), axis=0) - 1).reshape(
        group_size, CAP
    )
    incoming = lax.all_to_all(request, "dev", split_axis=0, concat_axis=0, tiled=True)
    own_blocks = sketch.reshape(block_count, tile_size, width)
    flat_requests = incoming.reshape(-1)
    served = jnp.take(own_blocks, jnp.maximum(flat_requests, 0), axis=0)
    served = jnp.where((flat_requests >= 0)[:, None, None], served, jnp.zeros_like(served))
    replies = lax.all_to_all(
        served.reshape(group_size, CAP, tile_size, width),
        "dev",
        split_axis=0,
        concat_axis=0,
        tiled=True,
    )
    touched_rows = jnp.take(replies.reshape(slot_count, tile_size, width), position, axis=0)
    batch_rows = min(128, tiles.shape[0])
    rounds = tiles.shape[0] // batch_rows
    tile_steps = tiles.reshape(rounds, batch_rows, tile_size, tile_size)
    ray_steps = tile_ray.reshape(rounds, batch_rows)
    col_steps = tile_col.reshape(rounds, batch_rows)

    def image_step(running, inputs):
        tile_block, ray_block, col_block = inputs
        gathered = jnp.take(touched_rows, col_block, axis=0)
        product = jnp.einsum(
            "tab,tbk->tak", tile_block, gathered, preferred_element_type=jnp.float32
        )
        return (running.at[ray_block].add(product), None)

    images, _ = lax.scan(
        image_step,
        jnp.zeros((RB_DEV, tile_size, width), jnp.float32),
        (tile_steps, ray_steps, col_steps),
    )
    images = images.astype(jnp.bfloat16)

    def normal_step(running, inputs):
        tile_block, ray_block, col_block = inputs
        gathered = jnp.take(images, ray_block, axis=0)
        product = jnp.einsum(
            "tab,tak->tbk", tile_block, gathered, preferred_element_type=jnp.float32
        )
        return (running.at[col_block].add(product), None)

    partial_value, _ = lax.scan(
        normal_step,
        jnp.zeros((ntouch, tile_size, width), jnp.float32),
        (tile_steps, ray_steps, col_steps),
    )
    slot_of = jnp.sum(
        jnp.where(placing, jnp.arange(slot_count, dtype=jnp.int32)[None, :], 0), axis=1
    )
    outgoing = jnp.zeros((slot_count, tile_size, width), jnp.float32).at[slot_of].set(partial_value)
    arrived = lax.all_to_all(
        outgoing.reshape(group_size, CAP, tile_size, width),
        "dev",
        split_axis=0,
        concat_axis=0,
        tiled=True,
    )
    target = incoming.reshape(-1)
    safe_target = jnp.where(target >= 0, target, block_count)
    normal = (
        jnp.zeros((block_count + 1, tile_size, width), jnp.float32)
        .at[safe_target]
        .add(arrived.reshape(slot_count, tile_size, width))
    )
    normal = normal[:block_count].reshape(block_count * tile_size, width)
    gram_matrix = lax.psum(
        jnp.dot(normal.T, normal, precision=lax.Precision.HIGHEST), ("grp", "dev")
    )
    voxels = normal.shape[0] * lax.axis_size("grp") * group_size
    gram_matrix = gram_matrix / voxels + gram_shift * jnp.eye(width, dtype=jnp.float32)
    lower = factor_lower(gram_matrix)
    r_factor = lower.T
    inverse = invert_lower(lower).T
    basis_out = jnp.dot(normal, inverse, precision=lax.Precision.HIGHEST)
    return (basis_out, r_factor)


def solution(mesh):
    in_specs = (
        P(("grp", "dev"), None, None),
        P(("grp", "dev")),
        P(("grp", "dev")),
        P(("grp", "dev")),
        P(),
        P(("grp", "dev"), None),
    )
    out_specs = (P(("grp", "dev"), None), P())
    return jax.shard_map(local, mesh=mesh, in_specs=in_specs, out_specs=out_specs, check_vma=False)
```

profile of v0, /device:TPU:0, one launch (start us, length us, event | category | flops | bytes accessed | tf_op | source)
XLA Modules:
  0.0 966.2 jit_solution(5539494399410684175)
XLA Ops:
  7.2 1.0 select_reduce_fusion
  8.7 13.5 %all_to_all.16 = s32[8,1,3]{2,1,0:T(1,128)S(1)} all-to-all(s32[8,1,3]{2,1,0:T(1,128)S(1)} %bitcast.162), channel_id=1, replica_groups=mesh['grp'=4,'dev'=8] {'dev'}, dimensions={0} | all-to-all | bytes 192 | tf_op jit(solution)/shard_map/all_to_all | solution.py:63
  25.0 1.1 select_select_fusion
  26.1 3.5 all-to-all-start.1
  29.7 22.4 %copy.52 = bf16[512,128,128]{1,2,0:T(8,128)(2,1)} copy(bf16[512,128,128]{2,1,0:T(8,128)(2,1)} %param.14) | data formatting | bytes 33554432 | tf_op args[0]
  53.3 112.9 %while.49 = (s32[]{:T(128)}, f32[32,128,128]{2,1,0:T(8,128)S(1)}, s32[4,128]{1,0:T(4,128)S(1)}, bf16[4,128,128,128]{3,2,1,0:T(8,128)(2,1)}, s32[4,128]{1,0:T(4,1...) while((s32[]{:T(128)}, f32[32,128,128]{2,1,0:T(8,128)S(1)}, s32[4,128]{1,0:T(4,128)S(1)}, ...), condition=%wide.region_6.7_spmd, body=%wide.region_4.6_spmd.sunk | while | flops 541067776 | bytes 50340692 | solution.py:90
  53.3 3.1 gather_fusion
  56.4 8.0 fusion.96
  64.4 17.0 %scatter_fusion = f32[32,128,128]{2,1,0:T(8,128)S(1)} fusion(f32[32,128,128]{2,1,0:T(8,128)S(1)} %get-tuple-element.497, s32[128]{0:T(128)S(1)} %get-tuple-element.469, f32[128,128,128]{2,1,0:T(8,128)} %fusion.96), kind=kCustom, calls=%fused_computation.4.clone.1 | custom fusion | flops 2097152 | bytes 25166336 | tf_op jit(solution)/shard_map/while/body/eval_jaxpr/scatter-add | solution.py:88
  81.5 3.1 gather_fusion
  84.7 8.0 fusion.96
  92.7 17.1 %scatter_fusion = f32[32,128,128]{2,1,0:T(8,128)S(1)} fusion(f32[32,128,128]{2,1,0:T(8,128)S(1)} %get-tuple-element.497, s32[128]{0:T(128)S(1)} %get-tuple-element.469, f32[128,128,128]{2,1,0:T(8,128)} %fusion.96), kind=kCustom, calls=%fused_computation.4.clone.1 | custom fusion | flops 2097152 | bytes 25166336 | tf_op jit(solution)/shard_map/while/body/eval_jaxpr/scatter-add | solution.py:88
  109.8 3.1 gather_fusion
  112.9 8.0 fusion.96
  120.9 17.0 %scatter_fusion = f32[32,128,128]{2,1,0:T(8,128)S(1)} fusion(f32[32,128,128]{2,1,0:T(8,128)S(1)} %get-tuple-element.497, s32[128]{0:T(128)S(1)} %get-tuple-element.469, f32[128,128,128]{2,1,0:T(8,128)} %fusion.96), kind=kCustom, calls=%fused_computation.4.clone.1 | custom fusion | flops 2097152 | bytes 25166336 | tf_op jit(solution)/shard_map/while/body/eval_jaxpr/scatter-add | solution.py:88
  138.0 3.1 gather_fusion
  141.1 8.0 fusion.96
  149.1 17.1 %scatter_fusion = f32[32,128,128]{2,1,0:T(8,128)S(1)} fusion(f32[32,128,128]{2,1,0:T(8,128)S(1)} %get-tuple-element.497, s32[128]{0:T(128)S(1)} %get-tuple-element.469, f32[128,128,128]{2,1,0:T(8,128)} %fusion.96), kind=kCustom, calls=%fused_computation.4.clone.1 | custom fusion | flops 2097152 | bytes 25166336 | tf_op jit(solution)/shard_map/while/body/eval_jaxpr/scatter-add | solution.py:88
  166.6 112.9 %while.50 = (s32[]{:T(128)}, f32[24,128,128]{2,1,0:T(8,128)S(1)}, s32[4,128]{1,0:T(4,128)S(1)}, bf16[4,128,128,128]{2,3,1,0:T(8,128)(2,1)}, s32[4,128]{1,0:T(4,1...) while((s32[]{:T(128)}, f32[24,128,128]{2,1,0:T(8,128)S(1)}, s32[4,128]{1,0:T(4,128)S(1)}, ...), condition=%wide.region_9.10_spmd, body=%wide.region_7.9_spmd.sunk | while | flops 541067776 | bytes 50340692 | solution.py:105
  166.6 3.1 gather_fusion.1
  169.7 8.0 fusion.100
  177.7 17.1 %scatter_fusion.1 = f32[24,128,128]{2,1,0:T(8,128)S(1)} fusion(f32[24,128,128]{2,1,0:T(8,128)S(1)} %get-tuple-element.518, s32[128]{0:T(128)S(1)} %get-tuple-element.477, f32[128,128,128]{2,1,0:T(8,128)} %fusion.100), kind=kCustom, calls=%fused_computation.5.clone.1 | custom fusion | flops 2097152 | bytes 25166336 | tf_op jit(solution)/shard_map/while/body/eval_jaxpr/scatter-add | solution.py:103
  194.8 3.1 gather_fusion.1
  197.9 8.0 fusion.100
  206.0 17.0 %scatter_fusion.1 = f32[24,128,128]{2,1,0:T(8,128)S(1)} fusion(f32[24,128,128]{2,1,0:T(8,128)S(1)} %get-tuple-element.518, s32[128]{0:T(128)S(1)} %get-tuple-element.477, f32[128,128,128]{2,1,0:T(8,128)} %fusion.100), kind=kCustom, calls=%fused_computation.5.clone.1 | custom fusion | flops 2097152 | bytes 25166336 | tf_op jit(solution)/shard_map/while/body/eval_jaxpr/scatter-add | solution.py:103
  223.1 3.1 gather_fusion.1
  226.2 8.0 fusion.100
  234.2 17.1 %scatter_fusion.1 = f32[24,128,128]{2,1,0:T(8,128)S(1)} fusion(f32[24,128,128]{2,1,0:T(8,128)S(1)} %get-tuple-element.518, s32[128]{0:T(128)S(1)} %get-tuple-element.477, f32[128,128,128]{2,1,0:T(8,128)} %fusion.100), kind=kCustom, calls=%fused_computation.5.clone.1 | custom fusion | flops 2097152 | bytes 25166336 | tf_op jit(solution)/shard_map/while/body/eval_jaxpr/scatter-add | solution.py:103
  251.3 3.1 gather_fusion.1
  254.4 8.0 fusion.100
  262.4 17.0 %scatter_fusion.1 = f32[24,128,128]{2,1,0:T(8,128)S(1)} fusion(f32[24,128,128]{2,1,0:T(8,128)S(1)} %get-tuple-element.518, s32[128]{0:T(128)S(1)} %get-tuple-element.477, f32[128,128,128]{2,1,0:T(8,128)} %fusion.100), kind=kCustom, calls=%fused_computation.5.clone.1 | custom fusion | flops 2097152 | bytes 25166336 | tf_op jit(solution)/shard_map/while/body/eval_jaxpr/scatter-add | solution.py:103
  279.5 1.3 broadcast.545
  280.8 5.2 scatter_fusion.2
  286.0 41.3 %all_to_all.17 = f32[8,3,128,128]{3,2,1,0:T(8,128)S(1)} all-to-all(f32[8,3,128,128]{3,2,1,0:T(8,128)} %bitcast.157), channel_id=1, replica_groups=mesh['grp'=4,'dev'=8] {'dev'}, dimensions={0} | all-to-all | bytes 3145728 | tf_op jit(solution)/shard_map/all_to_all | solution.py:114
  327.3 2.5 broadcast_in_dim.127
  329.8 6.2 scatter_fusion.3
  336.0 10.8 %convolution_bitcast_fusion.4 = f32[128,128]{1,0:T(8,128)} fusion(f32[65,128,128]{2,1,0:T(8,128)} %scatter_fusion.3), kind=kOutput, calls=%fused_computation.85 | convolution fusion | flops 1610612736 | bytes 8519680 | tf_op jit(solution)/shard_map/dot_general | solution.py:130
  346.9 4.7 slice.12
  351.6 112.1 %all-reduce.2.cloned.1.call-done = f32[128,128]{1,0:T(8,128)} async-done(((f32[128,128]{1,0:T(8,128)}), f32[128,128]{1,0:T(8,128)}) %all-reduce.2.cloned.1.call-update) | async-done | bytes 65552 | tf_op jit(solution)/shard_map/psum | solution.py:129
  464.6 255.7 %while.52 = (s32[]{:T(128)}, f32[128,128]{1,0:T(8,128)S(1)}, f32[128,128]{1,0:T(8,128)S(1)}, s32[]{:T(128)}, s32[]{:T(128)}) while((s32[]{:T(128)}, f32[128,128]{1,0:T(8,128)S(1)}, f32[128,128]{1,0:T(8,128)S(1)}, s32[]{:T(128)}, s32[]{:T(128)}) %tuple.121), condition=%wide.region_15.16_spmd.clone.clone, body=%wide.region_13.15_spmd.clone.clone.sunk | while | flops 673410 | bytes 332909 | solution.py:28
  466.9 0.9 fusion.113
  468.9 0.9 fusion.113
  470.9 0.9 fusion.113
  472.8 0.9 fusion.113
  474.8 0.9 fusion.113
  476.8 0.9 fusion.113
  721.0 231.6 %while.51 = (s32[]{:T(128)}, f32[128,128]{1,0:T(8,128)S(1)}, f32[128,128]{1,0:T(8,128)S(1)}, s32[]{:T(128)}, s32[]{:T(128)}) while((s32[]{:T(128)}, f32[128,128]{1,0:T(8,128)S(1)}, f32[128,128]{1,0:T(8,128)S(1)}, s32[]{:T(128)}, s32[]{:T(128)}) %tuple.124), condition=%wide.region_18.19_spmd.clone, body=%wide.region_16.18_spmd.clone.sunk | while | flops 460034 | bytes 265308 | solution.py:42
  952.6 6.7 fusion.65
  (1339 shorter events, 390.8 us)
Async XLA Ops:
  7.2 17.1 %copy-start = (bf16[8192,128]{1,0:T(8,128)(2,1)S(1)}, bf16[8192,128]{1,0:T(8,128)(2,1)}, u32[]{:S(2)}) copy-start(bf16[8192,128]{1,0:T(8,128)(2,1)} %param.19) | copy-start | bytes 6291460
  26.1 26.1 %all-to-all-start.1 = ((bf16[8,3,128,128]{3,2,1,0:T(8,128)(2,1)}), bf16[8,3,128,128]{3,2,1,0:T(8,128)(2,1)S(1)}, u32[]{:S(2)}, u32[]{:S(2)}) async-start(bf16[8,3,128,128]{3,2,1,0:T(8,128)(2,1)} %select_select_fusion), calls=%async_computation.1 | async-start | bytes 1572864 | tf_op jit(solution)/shard_map/all_to_all | solution.py:68
  29.6 434.1 %all-reduce.2.cloned.1.call-start = ((), (), s32[]{:S(2)}) async-start(), calls=%async_computation.3 | async-start | bytes 131072 | tf_op jit(solution)/shard_map/psum | solution.py:129
  52.1 1.1 copy-start.2
  52.1 1.2 copy-start.3
  286.0 43.8 %copy-start.4 = (s32[24]{0:T(128)S(1)}, s32[24]{0:T(128)}, u32[]{:S(2)}) copy-start(s32[24]{0:T(128)} %get-tuple-element.358) | copy-start | bytes 292
  952.6 6.7 copy-start.1
Sparse Core Ops, SparseCore 0:
  347.0 116.6 all-reduce.1
where the time goes:
time: 973 us; the launch traced here: 966 us
  matrix products  446 us (46%)
  other arithmetic  173 us (18%)
  waiting for transfers between devices  112 us (12%)
  loops' own time  98.1 us (10%)
  local copies, waits for them, and re-layouts  64.4 us (7%)
  blocking collectives  54.8 us (6%)
  between operations  14.2 us (1%)
    dot_general x128, matrix products, column_step(): rest = target - jnp.dot(lower, row_part, precision=lax.Precision.HIGHEST)  113 us
    psum x1, waiting for transfers between devices, local(): lax.psum(jnp.dot(normal.T, normal, precision=lax.Precision.HIGHEST), ('gr...  112 us
    dot_general x128, matrix products, row_step(): jnp.dot(row_part, inverse, precision=lax.Precision.HIGHEST)  108 us
    dot_general x128, matrix products, row_step(): row_part = jnp.dot(pick, lower, precision=lax.Precision.HIGHEST)  107 us
    another operation x1, loops' own time, factor_lower(): lax.fori_loop(0, width, column_step, jnp.zeros((width, width), jnp.float32))  94 us
    scatter-add x4, other arithmetic, image_step(): return (running.at[ray_block].add(product), None)  68.2 us
    scatter-add x4, other arithmetic, normal_step(): return (running.at[col_block].add(product), None)  68.2 us
    all_to_all x1, blocking collectives, local(): lax.all_to_all(outgoing.reshape(group_size, CAP, tile_size, width), 'dev'...  41.3 us
  transfers between devices with their start and end apart: 2, of which 1 were waited for; matrix products, arithmetic and copies ran while one was open for 3% of the time, Pallas kernels for 0%

commit v1 on v0

v1 whole, which is shorter than its diff:
```python
import functools

import jax
import jax.numpy as jnp
from jax import lax
from jax.experimental import pallas as pl
from jax.experimental.pallas import tpu as pltpu
from jax.sharding import PartitionSpec as P

CAP = 3
RB_DEV = 32


gram_shift = 0.001

MIB = 2**20
SMEM = pl.BlockSpec(memory_space=pltpu.SMEM)
VMEM = pl.BlockSpec(memory_space=pltpu.VMEM)
ANY = pl.BlockSpec(memory_space=pl.ANY)


def in_vmem(shape, dtype):
    return pltpu.VMEM(shape, dtype)


def plan_kernel(block_count, touched_ref, home_ref, request_ref, position_ref, used_ref):
    group_size = request_ref.shape[0]

    @pl.loop(0, group_size)
    def _(holder):
        used_ref[holder] = 0
        for slot in range(CAP):
            request_ref[holder, slot] = -1

    @pl.loop(0, touched_ref.shape[0])
    def _(entry):
        stored = home_ref[touched_ref[entry]]
        holder = lax.rem(lax.div(stored, block_count), group_size)
        slot = used_ref[holder]
        used_ref[holder] = slot + 1
        request_ref[holder, slot] = lax.rem(stored, block_count)
        position_ref[entry] = holder * CAP + slot


def serve_kernel(asked_ref, sketch_ref, served_ref, sem):
    slots, tile_size, width = served_ref.shape

    def copy(slot):
        row = jnp.maximum(asked_ref[lax.div(slot, CAP), lax.rem(slot, CAP)], 0)
        return pltpu.make_async_copy(sketch_ref.at[row], served_ref.at[slot], sem)

    @pl.loop(0, slots)
    def _(slot):
        copy(slot).start()

    pltpu.make_async_copy(served_ref, served_ref, sem).wait()


def load_kernel(ray_ref, col_ref, place_ref, tiles_ref, dense_ref, sem):
    count, tile_size, _ = tiles_ref.shape
    rows, cols = dense_ref.shape

    @pl.loop(0, rows // tile_size)
    def _(block):
        dense_ref[pl.ds(block * tile_size, tile_size), :] = jnp.zeros((tile_size, cols), dense_ref.dtype)

    @pl.loop(0, count)
    def _(tile):
        row = pl.multiple_of(ray_ref[tile] * tile_size, tile_size)
        col = pl.multiple_of(place_ref[col_ref[tile]] * tile_size, tile_size)
        pltpu.make_async_copy(
            tiles_ref.at[tile],
            dense_ref.at[pl.ds(row, tile_size), pl.ds(col, tile_size)],
            sem,
        ).start()

    filled = dense_ref.at[:, pl.ds(0, count * tile_size * tile_size // rows)]
    pltpu.make_async_copy(filled, filled, sem).wait()


def project_kernel(dense_ref, sketch_ref, part_ref, images_ref):
    rows, cols = dense_ref.shape
    step = 256

    @pl.loop(0, rows // step)
    def _(chunk):
        at = pl.multiple_of(chunk * step, step)
        image = jnp.dot(dense_ref[pl.ds(at, step), :], sketch_ref[...], preferred_element_type=jnp.float32)
        images_ref[:, pl.ds(at, step)] = image.astype(jnp.bfloat16).T

    @pl.loop(0, cols // step)
    def _(chunk):
        at = pl.multiple_of(chunk * step, step)
        part = jnp.dot(images_ref[...], dense_ref[:, pl.ds(at, step)], preferred_element_type=jnp.float32)
        part_ref[pl.ds(at, step), :] = part.T.astype(part_ref.dtype)


def zero_kernel(out_ref, zeros_ref, sem):
    rows = zeros_ref.shape[0]
    zeros_ref[...] = jnp.zeros(zeros_ref.shape, zeros_ref.dtype)

    @pl.loop(0, out_ref.shape[0] // rows)
    def _(chunk):
        pltpu.make_async_copy(zeros_ref, out_ref.at[pl.ds(chunk * rows, rows)], sem).start()

    pltpu.make_async_copy(out_ref, out_ref, sem).wait()


def split(value):
    high = value.astype(jnp.bfloat16)
    return high, (value - high.astype(jnp.float32)).astype(jnp.bfloat16)


def gather_kernel(asked_ref, arrived_ref, normal_ref, gram_ref, block_ref, seen_ref):
    slots, tile_size, width = arrived_ref.shape

    @pl.loop(0, seen_ref.shape[0])
    def _(row):
        seen_ref[row] = -1

    normal_ref[...] = jnp.zeros(normal_ref.shape, normal_ref.dtype)

    def place(slot, filled):
        row = asked_ref[lax.div(slot, CAP), lax.rem(slot, CAP)]
        safe = jnp.maximum(row, 0)
        known = seen_ref[safe]
        fresh = jnp.logical_and(row >= 0, known < 0)
        at = jnp.where(known < 0, filled, known)
        block_ref[slot] = -1

        @pl.when(row >= 0)
        def _():
            seen_ref[safe] = at
            block_ref[at] = safe
            normal_ref[at] += arrived_ref[slot].astype(jnp.float32)

        return jnp.where(fresh, filled + 1, filled)

    lax.fori_loop(0, slots, place, 0)

    gram_ref[...] = jnp.zeros(gram_ref.shape, gram_ref.dtype)

    @pl.loop(0, slots // CAP)
    def _(chunk):
        rows = jnp.concatenate([normal_ref[chunk * CAP + i] for i in range(CAP)], axis=0)
        high, low = split(rows)
        both = lax.dot_general(
            high, jnp.concatenate([high, low], axis=1), (((0,), (0,)), ((), ())),
            preferred_element_type=jnp.float32,
        )
        cross = both[:, width:]
        gram_ref[...] += both[:, :width] + cross + cross.T


def three(value):
    high = value.astype(jnp.bfloat16).astype(jnp.float32)
    rest = value - high
    mid = rest.astype(jnp.bfloat16).astype(jnp.float32)
    return high, mid, rest - mid


def finish_kernel(voxels, block_ref, gram_ref, normal_ref, zeroed_ref, basis_ref, factor_ref, work_ref, out_ref, sem):
    width = gram_ref.shape[0]
    slots, tile_size, _ = normal_ref.shape
    panel = 8
    row_at = lax.broadcasted_iota(jnp.int32, (width, width), 0)
    col_at = lax.broadcasted_iota(jnp.int32, (width, width), 1)
    unit = jnp.where(row_at == col_at, 1.0, 0.0).astype(jnp.float32)
    work_ref[:, :width] = gram_ref[...] / voxels + gram_shift * unit
    work_ref[:, width:] = unit
    in_panel = lax.broadcasted_iota(jnp.int32, (panel, 1), 0)
    for start in range(0, width, panel):
        rows = work_ref[pl.ds(start, panel), :]
        scale = jnp.zeros((panel, 1), jnp.float32)
        for k in range(panel):
            column = rows[:, start + k : start + k + 1]
            pivot = rows[k : k + 1, start + k : start + k + 1]
            rows = rows - jnp.where(in_panel > k, column / pivot, 0.0) * rows[k : k + 1, :]
            scale = jnp.where(in_panel == k, lax.rsqrt(pivot), scale)
        rows = rows * scale
        work_ref[pl.ds(start, panel), :] = rows
        if start + panel < width:
            high, mid, low = three(rows)
            left = jnp.concatenate([high, high, mid, high, low, mid], axis=0)[:, :width]
            right = jnp.concatenate([high, mid, high, low, high, mid], axis=0)
            update = lax.dot_general(
                left.astype(jnp.bfloat16), right.astype(jnp.bfloat16), (((0,), (0,)), ((), ())),
                preferred_element_type=jnp.float32,
            )
            work_ref[pl.ds(start + panel, width - start - panel), :] -= update[start + panel :, :]
    factor_ref[...] = jnp.where(col_at >= row_at, work_ref[:, :width], 0.0)
    inverse = jnp.where(col_at <= row_at, work_ref[:, width:], 0.0).T
    high, low = split(inverse)
    weights = jnp.concatenate([high, high, low], axis=0)

    @pl.loop(0, slots)
    def _(slot):
        row_high, row_low = split(normal_ref[slot])
        out_ref[slot] = jnp.dot(
            jnp.concatenate([row_high, row_low, row_high], axis=1), weights,
            preferred_element_type=jnp.float32,
        )

        @pl.when(block_ref[slot] >= 0)
        def _():
            at = block_ref[slot] * tile_size
            pltpu.make_async_copy(out_ref.at[slot], basis_ref.at[pl.ds(at, tile_size)], sem.at[slot]).start()

    @pl.loop(0, slots)
    def _(slot):
        @pl.when(block_ref[slot] >= 0)
        def _():
            at = block_ref[slot] * tile_size
            pltpu.make_async_copy(out_ref.at[slot], basis_ref.at[pl.ds(at, tile_size)], sem.at[slot]).wait()


def summed(value, axis):
    size = lax.axis_size(axis)
    step = 1
    while step < size:
        value = value + lax.ppermute(value, axis, [(i, i ^ step) for i in range(size)])
        step *= 2
    return value


def local(tiles, tile_ray, tile_col, touched, home, sketch):
    group_size = lax.axis_size("dev")
    tile_size = tiles.shape[1]
    width = sketch.shape[1]
    block_count = sketch.shape[0] // tile_size
    ntouch = touched.shape[0]
    slots = group_size * CAP
    voxels = sketch.shape[0] * lax.axis_size("grp") * group_size

    request, position = pl.pallas_call(
        functools.partial(plan_kernel, block_count),
        out_shape=(
            jax.ShapeDtypeStruct((group_size, CAP), jnp.int32),
            jax.ShapeDtypeStruct((ntouch,), jnp.int32),
        ),
        in_specs=[SMEM, SMEM],
        out_specs=(SMEM, SMEM),
        scratch_shapes=[pltpu.SMEM((group_size,), jnp.int32)],
        name="plan",
    )(touched, home)
    asked = lax.all_to_all(request, "dev", split_axis=0, concat_axis=0, tiled=True)
    served = pl.pallas_call(
        serve_kernel,
        out_shape=jax.ShapeDtypeStruct((slots, tile_size, width), sketch.dtype),
        in_specs=[SMEM, ANY],
        out_specs=ANY,
        scratch_shapes=[pltpu.SemaphoreType.DMA],
        name="serve",
    )(asked, sketch.reshape(block_count, tile_size, width))
    replies = lax.all_to_all(
        served.reshape(group_size, CAP, tile_size, width), "dev", split_axis=0, concat_axis=0, tiled=True
    ).reshape(slots, tile_size, width)

    whole = slots == ntouch
    place = position if whole else jnp.arange(ntouch, dtype=jnp.int32)
    dense = pl.pallas_call(
        load_kernel,
        out_shape=in_vmem((RB_DEV * tile_size, ntouch * tile_size), tiles.dtype),
        in_specs=[SMEM, SMEM, SMEM, ANY],
        out_specs=VMEM,
        scratch_shapes=[pltpu.SemaphoreType.DMA],
        compiler_params=pltpu.CompilerParams(vmem_limit_bytes=8 * MIB),
        name="load",
    )(tile_ray, tile_col, place, tiles)
    columns = replies if whole else jnp.take(replies, position, axis=0)
    part = pl.pallas_call(
        project_kernel,
        out_shape=jax.ShapeDtypeStruct((ntouch * tile_size, width), jnp.bfloat16),
        in_specs=[VMEM, VMEM],
        out_specs=VMEM,
        scratch_shapes=[pltpu.VMEM((width, RB_DEV * tile_size), jnp.bfloat16)],
        compiler_params=pltpu.CompilerParams(vmem_limit_bytes=16 * MIB),
        name="project",
    )(dense, columns.reshape(ntouch * tile_size, width))
    part = part.reshape(ntouch, tile_size, width)
    if not whole:
        part = jnp.zeros((slots, tile_size, width), part.dtype).at[position].set(part)
    arrived = lax.all_to_all(
        part.reshape(group_size, CAP, tile_size, width), "dev", split_axis=0, concat_axis=0, tiled=True
    ).reshape(slots, tile_size, width)

    zeroed = pl.pallas_call(
        zero_kernel,
        out_shape=jax.ShapeDtypeStruct(sketch.shape, jnp.float32),
        in_specs=[],
        out_specs=ANY,
        scratch_shapes=[pltpu.VMEM((sketch.shape[0] // 8, width), jnp.float32), pltpu.SemaphoreType.DMA],
        name="zeros",
    )()
    normal, gram, blocks = pl.pallas_call(
        gather_kernel,
        out_shape=(
            in_vmem((slots, tile_size, width), jnp.float32),
            jax.ShapeDtypeStruct((width, width), jnp.float32),
            jax.ShapeDtypeStruct((slots,), jnp.int32),
        ),
        in_specs=[SMEM, VMEM],
        out_specs=(VMEM, VMEM, SMEM),
        scratch_shapes=[pltpu.SMEM((block_count,), jnp.int32)],
        compiler_params=pltpu.CompilerParams(vmem_limit_bytes=16 * MIB),
        name="collect",
    )(asked, arrived)
    gram = summed(summed(gram, "grp"), "dev")
    return pl.pallas_call(
        functools.partial(finish_kernel, voxels),
        out_shape=(
            jax.ShapeDtypeStruct(sketch.shape, jnp.float32),
            jax.ShapeDtypeStruct((width, width), jnp.float32),
        ),
        in_specs=[SMEM, VMEM, VMEM, ANY],
        out_specs=(ANY, VMEM),
        scratch_shapes=[
            pltpu.VMEM((width, 2 * width), jnp.float32),
            pltpu.VMEM((slots, tile_size, width), jnp.float32),
            pltpu.SemaphoreType.DMA((slots,)),
        ],
        input_output_aliases={3: 0},
        compiler_params=pltpu.CompilerParams(vmem_limit_bytes=16 * MIB),
        name="finish",
    )(blocks, gram, normal, zeroed)


def solution(mesh):
    in_specs = (
        P(("grp", "dev"), None, None),
        P(("grp", "dev")),
        P(("grp", "dev")),
        P(("grp", "dev")),
        P(),
        P(("grp", "dev"), None),
    )
    out_specs = (P(("grp", "dev"), None), P())
    return jax.shard_map(local, mesh=mesh, in_specs=in_specs, out_specs=out_specs, check_vma=False)
```

time: 973 us -> 165 us (0.17)
  matrix products: 446 us -> 0 us
  other arithmetic: 173 us -> 0.05 us
  waiting for transfers between devices: 112 us -> 12 us
  loops' own time: 98.1 us -> 0 us
  Pallas kernels: 0 us -> 82.4 us
  local copies, waits for them, and re-layouts: 64.4 us -> 22.2 us
  blocking collectives: 54.8 us -> 37.9 us
  between operations: 14.2 us -> 0.78 us
    dot_general x650 -> x0, matrix products: 446 us -> none  [the longest x128 113 us: column_step(): rest = target - jnp.dot(lower, row_part, precision=lax.Precision.HIGHEST)]
    scatter-add x9 -> x0, other arithmetic: 143 us -> none  [the longest x4 68.2 us: image_step(): return (running.at[ray_block].add(product), None)]
    psum x1 -> x0, waiting for transfers between devices: 112 us -> none  [local(): lax.psum(jnp.dot(normal.T, normal, precision=lax.Precision.HIGHEST), ('gr...]
    another operation x4 -> x0, loops' own time: 98.1 us -> none  [the longest x1 94 us: factor_lower(): lax.fori_loop(0, width, column_step, jnp.zeros((width, width), jnp.float32))]
    pallas_call x0 -> x7, Pallas kernels: none -> 82.4 us  [the longest x1 25.7 us: local(): pl.pallas_call(serve_kernel, out_shape=jax.ShapeDtypeStruct((slots, tile_...]
    gather x10 -> x0, local copies, waits for them, and re-layouts: 26.2 us -> none  [the longest x4 12.4 us: normal_step(): gathered = jnp.take(images, ray_block, axis=0)]
    add x258 -> x5, other arithmetic: 24.6 us -> 0.05 us  [summed(): value + lax.ppermute(value, axis, [(i, i ^ step) for i in range(size)])]
    all_to_all x1, blocking collectives: 41.3 us -> 24.3 us  [local(): lax.all_to_all(part.reshape(group_size, CAP, tile_size, width), 'dev', sp...]
  transfers between devices with their start and end apart: 2 -> 6, of which waited for: 1 -> 5; matrix products, arithmetic and copies ran while one was open for 3% -> 0% of each run, Pallas kernels for 0% -> 9%
where the time goes in v1:
time: 165 us; the launch traced here: 164 us
  Pallas kernels  82.4 us (50%)
  blocking collectives  37.9 us (23%)
  local copies, waits for them, and re-layouts  22.2 us (13%)
  waiting for transfers between devices  12 us (7%)
  starting transfers between devices  9.03 us (5%)
    pallas_call x1, Pallas kernels, local(): pl.pallas_call(serve_kernel, out_shape=jax.ShapeDtypeStruct((slots, tile_...  25.7 us
    all_to_all x1, blocking collectives, local(): lax.all_to_all(part.reshape(group_size, CAP, tile_size, width), 'dev', sp...  24.3 us
    unnamed x14, local copies, waits for them, and re-layouts  22.2 us
    pallas_call x1, Pallas kernels, local(): pl.pallas_call(functools.partial(finish_kernel, voxels), out_shape=(jax.S...  19 us
    pallas_call x1, Pallas kernels, local(): pl.pallas_call(project_kernel, out_shape=jax.ShapeDtypeStruct((ntouch * t...  16.8 us
    all_to_all x1, blocking collectives, local(): lax.all_to_all(request, 'dev', split_axis=0, concat_axis=0, tiled=True)  13.6 us
    pallas_call x1, Pallas kernels, local(): pl.pallas_call(load_kernel, out_shape=in_vmem((RB_DEV * tile_size, ntouch...  12.3 us
    ppermute x5, waiting for transfers between devices, summed(): lax.ppermute(value, axis, [(i, i ^ step) for i in range(size)])  12 us
  transfers between devices with their start and end apart: 6, of which 5 were waited for; matrix products, arithmetic and copies ran while one was open for 0% of the time, Pallas kernels for 9%

profile of v1, /device:TPU:0, one launch (start us, length us, event | category | flops | bytes accessed | tf_op | source)
XLA Modules:
  0.0 164.4 jit_solution(10993319058885606888)
XLA Ops:
  0.6 0.0 copy-start.4
  0.6 0.0 copy-start.5
  0.7 2.0 %plan.1 = (s32[8,3]{1,0:T(8,128)}, s32[24]{0:T(128)}) custom-call(s32[24]{0:T(128)} %touched_ref.1, s32[2048]{0:T(1024)} %home_ref.1), custom_call_target="tpu_custom_call" | custom-call | tf_op jit(solution)/shard_map/plan/pallas_call | solution.py:235
  2.7 0.0 copy-start.6
  2.7 13.6 %all_to_all.21 = s32[8,1,3]{2,1,0:T(1,128)} all-to-all(s32[8,1,3]{2,1,0:T(1,128)} %bitcast.16), channel_id=1, replica_groups=mesh['grp'=4,'dev'=8] {'dev'}, dimensions={0} | all-to-all | bytes 192 | tf_op jit(solution)/shard_map/all_to_all | solution.py:246
  16.3 25.7 %serve.1 = bf16[24,128,128]{2,1,0:T(8,128)(2,1)} custom-call(s32[8,3]{1,0:T(8,128)} %bitcast.12, bf16[64,128,128]{2,1,0:T(8,128)(2,1)} %bitcast.15), custom_call_target="tpu_custom_call" | custom-call | tf_op jit(solution)/shard_map/serve/pallas_call | solution.py:247
  42.0 3.6 %all-to-all-start.1 = ((bf16[8,3,128,128]{3,2,1,0:T(8,128)(2,1)}), bf16[8,3,128,128]{3,2,1,0:T(8,128)(2,1)S(1)}, u32[]{:S(2)}, u32[]{:S(2)}) async-start(bf16[8,3,128,128]{3,2,1,0:T(8,128)(2,1)} %bitcast.14), calls=%async_computation.1 | async-start | bytes 1572864 | tf_op jit(solution)/shard_map/all_to_all | solution.py:255
  45.5 0.0 copy-done.4
  45.5 0.0 copy-done.5
  45.6 0.0 copy-done.6
  45.6 0.0 copy-start.2
  45.6 5.8 %copy-done.2 = bf16[512,128,128]{2,1,0:T(8,128)(2,1)S(1)} copy-done((bf16[512,128,128]{2,1,0:T(8,128)(2,1)S(1)}, bf16[512,128,128]{2,1,0:T(8,128)(2,1)}, u32[]{:S(2)}) %copy-start.2) | copy-done | bytes 16777240
  51.3 12.3 %load.1.dense_ref = bf16[4096,3072]{1,0:T(8,128)(2,1)S(1)} custom-call(s32[512]{0:T(512)S(1)} %copy-done.4, s32[512]{0:T(512)S(1)} %copy-done.5, s32[24]{0:T(128)S(1)} %copy-done.6, bf16[512,128,128]{2,1,0:T(8,128)(2,1)S(1)} %copy-done.2), custom_call_target="tpu_custom_call" | custom-call | tf_op jit(solution)/shard_map/load/pallas_call | solution.py:261
  63.6 0.0 copy-start
  63.7 8.3 %copy-done = bf16[4096,3072]{1,0:T(8,128)(2,1)} copy-done((bf16[4096,3072]{1,0:T(8,128)(2,1)}, bf16[4096,3072]{1,0:T(8,128)(2,1)S(1)}, u32[]{:S(2)}) %copy-start) | copy-done | bytes 25165848
  72.0 0.0 all-to-all-done.1
  72.0 0.0 copy-start.1
  72.0 8.2 %copy-done.1 = bf16[4096,3072]{1,0:T(8,128)(2,1)S(1)} copy-done((bf16[4096,3072]{1,0:T(8,128)(2,1)S(1)}, bf16[4096,3072]{1,0:T(8,128)(2,1)}, u32[]{:S(2)}) %copy-start.1) | copy-done | bytes 25165848
  80.1 0.0 copy-start.3
  80.1 16.8 %project.1 = bf16[3072,128]{1,0:T(8,128)(2,1)S(1)} custom-call(bf16[4096,3072]{1,0:T(8,128)(2,1)S(1)} %copy-done.1, bf16[3072,128]{1,0:T(8,128)(2,1)S(1)} %bitcast.9), custom_call_target="tpu_custom_call" | custom-call | tf_op jit(solution)/shard_map/project/pallas_call | solution.py:271
  96.9 24.3 %all_to_all.22 = bf16[8,3,128,128]{3,2,1,0:T(8,128)(2,1)S(1)} all-to-all(bf16[8,3,128,128]{3,2,1,0:T(8,128)(2,1)S(1)} %bitcast.10), channel_id=1, replica_groups=mesh['grp'=4,'dev'=8] {'dev'}, dimensions={0} | all-to-all | bytes 1572864 | tf_op jit(solution)/shard_map/all_to_all | solution.py:283
  121.2 0.0 copy-done.3
  121.2 4.6 %collect.1 = (f32[24,128,128]{2,1,0:T(8,128)S(1)}, f32[128,128]{1,0:T(8,128)S(1)}, s32[24]{0:T(128)S(1)}) custom-call(s32[8,3]{1,0:T(8,128)S(1)} %bitcast.13, bf16[24,128,128]{2,1,0:T(8,128)(2,1)S(1)} %bitcast.11), custom_call_target="tpu_custom_call" | custom-call | tf_op jit(solution)/shard_map/collect/pallas_call | solution.py:295
  125.8 0.1 collective-permute-start
  125.9 1.2 collective-permute-done
  127.2 1.6 collective-permute-start.1
  128.7 2.7 %collective-permute-done.1 = f32[128,128]{1,0:T(8,128)S(1)} collective-permute-done((f32[128,128]{1,0:T(8,128)S(1)}, f32[128,128]{1,0:T(8,128)S(1)}, u32[]{:S(2)}, u32[]{:S(2)}) %collective-permute-start.1) | collective-permute-done | bytes 65568 | tf_op jit(solution)/shard_map/ppermute | solution.py:221
  131.5 1.5 collective-permute-start.2
  133.0 2.8 %collective-permute-done.2 = f32[128,128]{1,0:T(8,128)S(1)} collective-permute-done((f32[128,128]{1,0:T(8,128)S(1)}, f32[128,128]{1,0:T(8,128)S(1)}, u32[]{:S(2)}, u32[]{:S(2)}) %collective-permute-start.2) | collective-permute-done | bytes 65568 | tf_op jit(solution)/shard_map/ppermute | solution.py:221
  135.8 1.2 collective-permute-start.3
  137.0 3.2 %collective-permute-done.3 = f32[128,128]{1,0:T(8,128)S(1)} collective-permute-done((f32[128,128]{1,0:T(8,128)S(1)}, f32[128,128]{1,0:T(8,128)S(1)}, u32[]{:S(2)}, u32[]{:S(2)}) %collective-permute-start.3) | collective-permute-done | bytes 65568 | tf_op jit(solution)/shard_map/ppermute | solution.py:221
  140.2 1.1 collective-permute-start.4
  141.3 2.0 %zeros.1.zeroed_ref = f32[8192,128]{1,0:T(8,128)} custom-call(), custom_call_target="tpu_custom_call" | custom-call | tf_op jit(solution)/shard_map/zeros/pallas_call | solution.py:287
  143.4 2.1 %collective-permute-done.4 = f32[128,128]{1,0:T(8,128)S(1)} collective-permute-done((f32[128,128]{1,0:T(8,128)S(1)}, f32[128,128]{1,0:T(8,128)S(1)}, u32[]{:S(2)}, u32[]{:S(2)}) %collective-permute-start.4) | collective-permute-done | bytes 65568 | tf_op jit(solution)/shard_map/ppermute | solution.py:221
  145.4 19.0 %finish.1 = (f32[8192,128]{1,0:T(8,128)}, f32[128,128]{1,0:T(8,128)}) custom-call(s32[24]{0:T(128)S(1)} %get-tuple-element.9.block_ref, f32[128,128]{1,0:T(8,128)S(1)} %add.19.gram_ref, f32[24,128,128]{2,1,0:T(8,128)S(1)} %get-tuple-element.11.normal_ref, f32[8192,128]{1,0:T(8,128)} %zeros.1.zeroed_ref), custom_call_target="tpu_custom_call", output_to_operand_aliasing={{0}: (3, {})} | custom-call | tf_op jit(solution)/shard_map/finish/pallas_call | solution.py:309
  (5 shorter events, 0.0 us)
Async XLA Ops:
  0.6 44.9 %copy-start.4 = (s32[512]{0:T(512)S(1)}, s32[512]{0:T(512)}, u32[]{:S(2)}) copy-start(s32[512]{0:T(512)} %ray_ref.1) | copy-start | bytes 6148
  0.6 44.9 %copy-start.5 = (s32[512]{0:T(512)S(1)}, s32[512]{0:T(512)}, u32[]{:S(2)}) copy-start(s32[512]{0:T(512)} %col_ref.1) | copy-start | bytes 6148
  2.7 42.9 %copy-start.6 = (s32[24]{0:T(128)S(1)}, s32[24]{0:T(128)}, u32[]{:S(2)}) copy-start(s32[24]{0:T(128)} %get-tuple-element.8.place_ref) | copy-start | bytes 292
  42.0 30.0 %all-to-all-start.1 = ((bf16[8,3,128,128]{3,2,1,0:T(8,128)(2,1)}), bf16[8,3,128,128]{3,2,1,0:T(8,128)(2,1)S(1)}, u32[]{:S(2)}, u32[]{:S(2)}) async-start(bf16[8,3,128,128]{3,2,1,0:T(8,128)(2,1)} %bitcast.14), calls=%async_computation.1 | async-start | bytes 1572864 | tf_op jit(solution)/shard_map/all_to_all | solution.py:255
  45.6 5.8 %copy-start.2 = (bf16[512,128,128]{2,1,0:T(8,128)(2,1)S(1)}, bf16[512,128,128]{2,1,0:T(8,128)(2,1)}, u32[]{:S(2)}) copy-start(bf16[512,128,128]{2,1,0:T(8,128)(2,1)} %tiles_ref.1) | copy-start | bytes 50331652
  63.6 8.3 %copy-start = (bf16[4096,3072]{1,0:T(8,128)(2,1)}, bf16[4096,3072]{1,0:T(8,128)(2,1)S(1)}, u32[]{:S(2)}) copy-start(bf16[4096,3072]{1,0:T(8,128)(2,1)S(1)} %load.1.dense_ref) | copy-start | bytes 75497472
  72.0 8.2 %copy-start.1 = (bf16[4096,3072]{1,0:T(8,128)(2,1)S(1)}, bf16[4096,3072]{1,0:T(8,128)(2,1)}, u32[]{:S(2)}) copy-start(bf16[4096,3072]{1,0:T(8,128)(2,1)} %copy-done) | copy-start | bytes 75497472
  80.1 41.1 %copy-start.3 = (s32[8,1,3]{2,1,0:T(1,128)S(1)}, s32[8,1,3]{2,1,0:T(1,128)}, u32[]{:S(2)}) copy-start(s32[8,1,3]{2,1,0:T(1,128)} %all_to_all.21) | copy-start | bytes 292
  125.8 1.3 collective-permute-start
  127.2 4.3 %collective-permute-start.1 = (f32[128,128]{1,0:T(8,128)S(1)}, f32[128,128]{1,0:T(8,128)S(1)}, u32[]{:S(2)}, u32[]{:S(2)}) collective-permute-start(f32[128,128]{1,0:T(8,128)S(1)} %add.15), channel_id=1, source_target_pairs={{0,16},{8,24},{16,0},{24,8},{1,17},{9,25},{17,1},{25,9},{2,18},{10... | collective-permute-start | bytes 196616 | tf_op jit(solution)/shard_map/ppermute | solution.py:221
  131.5 4.3 %collective-permute-start.2 = (f32[128,128]{1,0:T(8,128)S(1)}, f32[128,128]{1,0:T(8,128)S(1)}, u32[]{:S(2)}, u32[]{:S(2)}) collective-permute-start(f32[128,128]{1,0:T(8,128)S(1)} %add.16), channel_id=1, source_target_pairs={{0,1},{1,0},{2,3},{3,2},{4,5},{5,4},{6,7},{7,6},{8,9},{9,8},{10,11... | collective-permute-start | bytes 196616 | tf_op jit(solution)/shard_map/ppermute | solution.py:221
  135.8 4.3 %collective-permute-start.3 = (f32[128,128]{1,0:T(8,128)S(1)}, f32[128,128]{1,0:T(8,128)S(1)}, u32[]{:S(2)}, u32[]{:S(2)}) collective-permute-start(f32[128,128]{1,0:T(8,128)S(1)} %add.17), channel_id=1, source_target_pairs={{0,2},{1,3},{2,0},{3,1},{4,6},{5,7},{6,4},{7,5},{8,10},{9,11},{10,... | collective-permute-start | bytes 196616 | tf_op jit(solution)/shard_map/ppermute | solution.py:221
  140.2 5.2 %collective-permute-start.4 = (f32[128,128]{1,0:T(8,128)S(1)}, f32[128,128]{1,0:T(8,128)S(1)}, u32[]{:S(2)}, u32[]{:S(2)}) collective-permute-start(f32[128,128]{1,0:T(8,128)S(1)} %add.18), channel_id=1, source_target_pairs={{0,4},{1,5},{2,6},{3,7},{4,0},{5,1},{6,2},{7,3},{8,12},{9,13},{10,... | collective-permute-start | bytes 196616 | tf_op jit(solution)/shard_map/ppermute | solution.py:221

commit v2 on v1

--- a/solution.py
+++ b/solution.py
@@ -21,6 +21,14 @@
 
 def in_vmem(shape, dtype):
     return pltpu.VMEM(shape, dtype)
+
+
+def held(value):
+    return pltpu.with_memory_space_constraint(value, pltpu.VMEM)
+
+
+def in_hbm(value):
+    return pltpu.with_memory_space_constraint(value, pltpu.HBM)
 
 
 def plan_kernel(block_count, touched_ref, home_ref, request_ref, position_ref, used_ref):
@@ -152,44 +160,68 @@
         gram_ref[...] += both[:, :width] + cross + cross.T
 
 
-def three(value):
-    high = value.astype(jnp.bfloat16).astype(jnp.float32)
-    rest = value - high
-    mid = rest.astype(jnp.bfloat16).astype(jnp.float32)
-    return high, mid, rest - mid
+def spread(value, like):
+    return jnp.broadcast_to(value, like.shape)
+
+
+def factor(gram, inverse_ref):
+    panel, width = gram[0].shape
+    gram = list(gram)
+    row_at = lax.broadcasted_iota(jnp.int32, (panel, width), 0)
+    lane = lax.broadcasted_iota(jnp.int32, (panel, width), 1)
+    right = [jnp.where(lane == row_at + panel * i, 1.0, 0.0) for i in range(len(gram))]
+    upper = []
+    for p in range(len(gram)):
+        start = panel * p
+        columns = [
+            [spread(rows[:, start + k : start + k + 1], rows) for k in range(panel)] for rows in gram[p:]
+        ]
+        corner = list(columns[0])
+        left_rows, right_rows = gram[p], right[p]
+        upper_rows, inverse_rows = jnp.zeros_like(left_rows), jnp.zeros_like(left_rows)
+        for k in range(panel):
+            pivot = spread(corner[k][k : k + 1], left_rows)
+            reciprocal, root = 1.0 / pivot, lax.rsqrt(pivot)
+            here = row_at == k
+            left_row, right_row = spread(left_rows[k : k + 1], left_rows), spread(right_rows[k : k + 1], left_rows)
+            upper_rows = jnp.where(here, left_row * root, upper_rows)
+            inverse_rows = jnp.where(here, right_row * root, inverse_rows)
+            by = jnp.where(here, -1.0, corner[k])
+            for j in range(k + 1, panel):
+                scaled = spread(corner[j][k : k + 1], left_rows) * reciprocal
+                corner[j] = jnp.where(here, 0.0, corner[j]) - by * scaled
+            left_rows = jnp.where(here, 0.0, left_rows) - by * (left_row * reciprocal)
+            right_rows = jnp.where(here, 0.0, right_rows) - by * (right_row * reciprocal)
+        upper.append(jnp.where(lane >= row_at + start, upper_rows, 0.0))
+        inverse_ref[pl.ds(start, panel), :] = jnp.where(lane <= row_at + start, inverse_rows, 0.0)
+        left_each = [spread(left_rows[k : k + 1], left_rows) for k in range(panel)]
+        right_each = [spread(right_rows[k : k + 1], left_rows) for k in range(panel)]
+        for i in range(p + 1, len(gram)):
+            by = columns[i - p]
+            gram[i] = gram[i] - total([b * row for b, row in zip(by, left_each)])
+            right[i] = right[i] - total([b * row for b, row in zip(by, right_each)])
+    return upper
+
+
+def total(terms):
+    while len(terms) > 1:
+        terms = [sum(terms[i + 1 : i + 2], terms[i]) for i in range(0, len(terms), 2)]
+    return terms[0]
 
 
 def finish_kernel(voxels, block_ref, gram_ref, normal_ref, zeroed_ref, basis_ref, factor_ref, work_ref, out_ref, sem):
     width = gram_ref.shape[0]
     slots, tile_size, _ = normal_ref.shape
     panel = 8
-    row_at = lax.broadcasted_iota(jnp.int32, (width, width), 0)
-    col_at = lax.broadcasted_iota(jnp.int32, (width, width), 1)
-    unit = jnp.where(row_at == col_at, 1.0, 0.0).astype(jnp.float32)
-    work_ref[:, :width] = gram_ref[...] / voxels + gram_shift * unit
-    work_ref[:, width:] = unit
-    in_panel = lax.broadcasted_iota(jnp.int32, (panel, 1), 0)
+    row_at = lax.broadcasted_iota(jnp.int32, (panel, width), 0)
+    lane = lax.broadcasted_iota(jnp.int32, (panel, width), 1)
+    gram = []
     for start in range(0, width, panel):
-        rows = work_ref[pl.ds(start, panel), :]
-        scale = jnp.zeros((panel, 1), jnp.float32)
-        for k in range(panel):
-            column = rows[:, start + k : start + k + 1]
-            pivot = rows[k : k + 1, start + k : start + k + 1]
-            rows = rows - jnp.where(in_panel > k, column / pivot, 0.0) * rows[k : k + 1, :]
-            scale = jnp.where(in_panel == k, lax.rsqrt(pivot), scale)
-        rows = rows * scale
-        work_ref[pl.ds(start, panel), :] = rows
-        if start + panel < width:
-            high, mid, low = three(rows)
-            left = jnp.concatenate([high, high, mid, high, low, mid], axis=0)[:, :width]
-            right = jnp.concatenate([high, mid, high, low, high, mid], axis=0)
-            update = lax.dot_general(
-                left.astype(jnp.bfloat16), right.astype(jnp.bfloat16), (((0,), (0,)), ((), ())),
-                preferred_element_type=jnp.float32,
-            )
-            work_ref[pl.ds(start + panel, width - start - panel), :] -= update[start + panel :, :]
-    factor_ref[...] = jnp.where(col_at >= row_at, work_ref[:, :width], 0.0)
-    inverse = jnp.where(col_at <= row_at, work_ref[:, width:], 0.0).T
+        shift = jnp.where(lane == row_at + start, gram_shift, 0.0)
+        gram.append(gram_ref[pl.ds(start, panel), :] / voxels + shift)
+    for i, rows in enumerate(factor(gram, work_ref)):
+        factor_ref[pl.ds(panel * i, panel), :] = rows
+    inverse = work_ref[...].T
     high, low = split(inverse)
     weights = jnp.concatenate([high, high, low], axis=0)
 
@@ -248,10 +280,10 @@
         serve_kernel,
         out_shape=jax.ShapeDtypeStruct((slots, tile_size, width), sketch.dtype),
         in_specs=[SMEM, ANY],
-        out_specs=ANY,
+        out_specs=VMEM,
         scratch_shapes=[pltpu.SemaphoreType.DMA],
         name="serve",
-    )(asked, sketch.reshape(block_count, tile_size, width))
+    )(asked, in_hbm(sketch.reshape(block_count, tile_size, width)))
     replies = lax.all_to_all(
         served.reshape(group_size, CAP, tile_size, width), "dev", split_axis=0, concat_axis=0, tiled=True
     ).reshape(slots, tile_size, width)
@@ -266,7 +298,7 @@
         scratch_shapes=[pltpu.SemaphoreType.DMA],
         compiler_params=pltpu.CompilerParams(vmem_limit_bytes=8 * MIB),
         name="load",
-    )(tile_ray, tile_col, place, tiles)
+    )(tile_ray, tile_col, place, in_hbm(tiles))
     columns = replies if whole else jnp.take(replies, position, axis=0)
     part = pl.pallas_call(
         project_kernel,
@@ -276,7 +308,7 @@
         scratch_shapes=[pltpu.VMEM((width, RB_DEV * tile_size), jnp.bfloat16)],
         compiler_params=pltpu.CompilerParams(vmem_limit_bytes=16 * MIB),
         name="project",
-    )(dense, columns.reshape(ntouch * tile_size, width))
+    )(held(dense), columns.reshape(ntouch * tile_size, width))
     part = part.reshape(ntouch, tile_size, width)
     if not whole:
         part = jnp.zeros((slots, tile_size, width), part.dtype).at[position].set(part)
@@ -315,14 +347,14 @@
         in_specs=[SMEM, VMEM, VMEM, ANY],
         out_specs=(ANY, VMEM),
         scratch_shapes=[
-            pltpu.VMEM((width, 2 * width), jnp.float32),
+            pltpu.VMEM((width, width), jnp.float32),
             pltpu.VMEM((slots, tile_size, width), jnp.float32),
             pltpu.SemaphoreType.DMA((slots,)),
         ],
         input_output_aliases={3: 0},
         compiler_params=pltpu.CompilerParams(vmem_limit_bytes=16 * MIB),
         name="finish",
-    )(blocks, gram, normal, zeroed)
+    )(blocks, gram, held(normal), zeroed)
 
 
 def solution(mesh):

time: 165 us -> 125 us (0.76)
  Pallas kernels: 82.4 us -> 47.7 us
  local copies, waits for them, and re-layouts: 22.2 us -> 16.5 us
    pallas_call x1, Pallas kernels: 25.7 us -> 2.82 us  [local(): pl.pallas_call(serve_kernel, out_shape=jax.ShapeDtypeStruct((slots, tile_...]
    pallas_call x1, Pallas kernels: 19 us -> 10.4 us  [local(): pl.pallas_call(functools.partial(finish_kernel, voxels), out_shape=(jax.S...]
    unnamed x14 -> x12, local copies, waits for them, and re-layouts: 22.2 us -> 16.5 us
    pallas_call x1, Pallas kernels: 12.3 us -> 9.01 us  [local(): pl.pallas_call(load_kernel, out_shape=in_vmem((RB_DEV * tile_size, ntouch...]
  transfers between devices with their start and end apart: 6 -> 6, of which waited for: 5 -> 6; matrix products, arithmetic and copies ran while one was open for 0% -> 0% of each run, Pallas kernels for 9% -> 9%
where the time goes in v2:
time: 125 us; the launch traced here: 124 us
  Pallas kernels  47.7 us (38%)
  blocking collectives  36.9 us (30%)
  local copies, waits for them, and re-layouts  16.5 us (13%)
  waiting for transfers between devices  13.5 us (11%)
  starting transfers between devices  9.04 us (7%)
    all_to_all x1, blocking collectives, local(): lax.all_to_all(part.reshape(group_size, CAP, tile_size, width), 'dev', sp...  23.1 us
    pallas_call x1, Pallas kernels, local(): pl.pallas_call(project_kernel, out_shape=jax.ShapeDtypeStruct((ntouch * t...  16.8 us
    unnamed x12, local copies, waits for them, and re-layouts  16.5 us
    all_to_all x1, blocking collectives, local(): lax.all_to_all(request, 'dev', split_axis=0, concat_axis=0, tiled=True)  13.8 us
    ppermute x5, waiting for transfers between devices, summed(): lax.ppermute(value, axis, [(i, i ^ step) for i in range(size)])  12 us
    pallas_call x1, Pallas kernels, local(): pl.pallas_call(functools.partial(finish_kernel, voxels), out_shape=(jax.S...  10.4 us
    pallas_call x1, Pallas kernels, local(): pl.pallas_call(load_kernel, out_shape=in_vmem((RB_DEV * tile_size, ntouch...  9.01 us
    ppermute x5, starting transfers between devices, summed(): lax.ppermute(value, axis, [(i, i ^ step) for i in range(size)])  5.48 us
  transfers between devices with their start and end apart: 6, of which 6 were waited for; matrix products, arithmetic and copies ran while one was open for 0% of the time, Pallas kernels for 9%

profile of v2, /device:TPU:0, one launch (start us, length us, event | category | flops | bytes accessed | tf_op | source)
XLA Modules:
  0.0 124.4 jit_solution(4104237485564153526)
XLA Ops:
  0.6 0.0 copy-start.3
  0.6 0.0 copy-start.4
  0.7 2.0 %plan.1 = (s32[8,3]{1,0:T(8,128)}, s32[24]{0:T(128)}) custom-call(s32[24]{0:T(128)} %touched_ref.1, s32[2048]{0:T(1024)} %home_ref.1), custom_call_target="tpu_custom_call" | custom-call | tf_op jit(solution)/shard_map/plan/pallas_call | solution.py:267
  2.7 0.0 copy-start.5
  2.7 13.8 %all_to_all.21 = s32[8,1,3]{2,1,0:T(1,128)} all-to-all(s32[8,1,3]{2,1,0:T(1,128)} %bitcast.16), channel_id=1, replica_groups=mesh['grp'=4,'dev'=8] {'dev'}, dimensions={0} | all-to-all | bytes 192 | tf_op jit(solution)/shard_map/all_to_all | solution.py:278
  16.4 2.8 %serve.1 = bf16[24,128,128]{2,1,0:T(8,128)(2,1)} custom-call(s32[8,3]{1,0:T(8,128)} %bitcast.12, bf16[64,128,128]{2,1,0:T(8,128)(2,1)} %bitcast.15), custom_call_target="tpu_custom_call" | custom-call | tf_op jit(solution)/shard_map/serve/pallas_call | solution.py:279
  19.3 3.6 %all-to-all-start.1 = ((bf16[8,3,128,128]{3,2,1,0:T(8,128)(2,1)}), bf16[8,3,128,128]{3,2,1,0:T(8,128)(2,1)S(1)}, u32[]{:S(2)}, u32[]{:S(2)}) async-start(bf16[8,3,128,128]{3,2,1,0:T(8,128)(2,1)} %bitcast.14), calls=%async_computation.1 | async-start | bytes 1572864 | tf_op jit(solution)/shard_map/all_to_all | solution.py:287
  22.8 0.0 copy-done.3
  22.9 0.0 copy-done.4
  22.9 0.0 copy-done.5
  22.9 9.0 %load.1.dense_ref = bf16[4096,3072]{1,0:T(8,128)(2,1)S(1)} custom-call(s32[512]{0:T(512)S(1)} %copy-done.3, s32[512]{0:T(512)S(1)} %copy-done.4, s32[24]{0:T(128)S(1)} %copy-done.5, bf16[512,128,128]{2,1,0:T(8,128)(2,1)} %tiles_ref.1), custom_call_target="tpu_custom_call" | custom-call | tf_op jit(solution)/shard_map/load/pallas_call | solution.py:293
  31.9 0.0 copy-start
  31.9 8.3 %copy-done = bf16[4096,3072]{1,0:T(8,128)(2,1)} copy-done((bf16[4096,3072]{1,0:T(8,128)(2,1)}, bf16[4096,3072]{1,0:T(8,128)(2,1)S(1)}, u32[]{:S(2)}) %copy-start) | copy-done | bytes 25165848
  40.2 1.5 %all-to-all-done.1 = bf16[8,3,128,128]{3,2,1,0:T(8,128)(2,1)S(1)} async-done(((bf16[8,3,128,128]{3,2,1,0:T(8,128)(2,1)}), bf16[8,3,128,128]{3,2,1,0:T(8,128)(2,1)S(1)}, u32[]{:S(2)}, u32[]{:S(2)}) %all-to-all-start.1) | async-done | bytes 786464 | tf_op jit(solution)/shard_map/all_to_all | solution.py:287
  41.7 0.0 copy-start.1
  41.7 8.2 %copy-done.1 = bf16[4096,3072]{1,0:T(8,128)(2,1)S(1)} copy-done((bf16[4096,3072]{1,0:T(8,128)(2,1)S(1)}, bf16[4096,3072]{1,0:T(8,128)(2,1)}, u32[]{:S(2)}) %copy-start.1) | copy-done | bytes 25165848
  49.9 0.0 copy-start.2
  49.9 16.8 %project.1 = bf16[3072,128]{1,0:T(8,128)(2,1)S(1)} custom-call(bf16[4096,3072]{1,0:T(8,128)(2,1)S(1)} %copy-done.1, bf16[3072,128]{1,0:T(8,128)(2,1)S(1)} %bitcast.9), custom_call_target="tpu_custom_call" | custom-call | tf_op jit(solution)/shard_map/project/pallas_call | solution.py:303
  66.7 23.1 %all_to_all.22 = bf16[8,3,128,128]{3,2,1,0:T(8,128)(2,1)S(1)} all-to-all(bf16[8,3,128,128]{3,2,1,0:T(8,128)(2,1)S(1)} %bitcast.10), channel_id=1, replica_groups=mesh['grp'=4,'dev'=8] {'dev'}, dimensions={0} | all-to-all | bytes 1572864 | tf_op jit(solution)/shard_map/all_to_all | solution.py:315
  89.8 0.0 copy-done.2
  89.8 4.6 %collect.1 = (f32[24,128,128]{2,1,0:T(8,128)S(1)}, f32[128,128]{1,0:T(8,128)S(1)}, s32[24]{0:T(128)S(1)}) custom-call(s32[8,3]{1,0:T(8,128)S(1)} %bitcast.13, bf16[24,128,128]{2,1,0:T(8,128)(2,1)S(1)} %bitcast.11), custom_call_target="tpu_custom_call" | custom-call | tf_op jit(solution)/shard_map/collect/pallas_call | solution.py:327
  94.4 0.1 collective-permute-start
  94.5 1.2 collective-permute-done
  95.7 1.6 %collective-permute-start.1 = (f32[128,128]{1,0:T(8,128)S(1)}, f32[128,128]{1,0:T(8,128)S(1)}, u32[]{:S(2)}, u32[]{:S(2)}) collective-permute-start(f32[128,128]{1,0:T(8,128)S(1)} %add.15), channel_id=1, source_target_pairs={{0,16},{8,24},{16,0},{24,8},{1,17},{9,25},{17,1},{25,9},{2,18},{10... | collective-permute-start | bytes 196616 | tf_op jit(solution)/shard_map/ppermute | solution.py:253
  97.3 2.7 %collective-permute-done.1 = f32[128,128]{1,0:T(8,128)S(1)} collective-permute-done((f32[128,128]{1,0:T(8,128)S(1)}, f32[128,128]{1,0:T(8,128)S(1)}, u32[]{:S(2)}, u32[]{:S(2)}) %collective-permute-start.1) | collective-permute-done | bytes 65568 | tf_op jit(solution)/shard_map/ppermute | solution.py:253
  100.1 1.5 %collective-permute-start.2 = (f32[128,128]{1,0:T(8,128)S(1)}, f32[128,128]{1,0:T(8,128)S(1)}, u32[]{:S(2)}, u32[]{:S(2)}) collective-permute-start(f32[128,128]{1,0:T(8,128)S(1)} %add.16), channel_id=1, source_target_pairs={{0,1},{1,0},{2,3},{3,2},{4,5},{5,4},{6,7},{7,6},{8,9},{9,8},{10,11... | collective-permute-start | bytes 196616 | tf_op jit(solution)/shard_map/ppermute | solution.py:253
  101.6 2.8 %collective-permute-done.2 = f32[128,128]{1,0:T(8,128)S(1)} collective-permute-done((f32[128,128]{1,0:T(8,128)S(1)}, f32[128,128]{1,0:T(8,128)S(1)}, u32[]{:S(2)}, u32[]{:S(2)}) %collective-permute-start.2) | collective-permute-done | bytes 65568 | tf_op jit(solution)/shard_map/ppermute | solution.py:253
  104.4 1.2 collective-permute-start.3
  105.6 3.2 %collective-permute-done.3 = f32[128,128]{1,0:T(8,128)S(1)} collective-permute-done((f32[128,128]{1,0:T(8,128)S(1)}, f32[128,128]{1,0:T(8,128)S(1)}, u32[]{:S(2)}, u32[]{:S(2)}) %collective-permute-start.3) | collective-permute-done | bytes 65568 | tf_op jit(solution)/shard_map/ppermute | solution.py:253
  108.7 1.1 collective-permute-start.4
  109.9 2.0 %zeros.1.zeroed_ref = f32[8192,128]{1,0:T(8,128)} custom-call(), custom_call_target="tpu_custom_call" | custom-call | tf_op jit(solution)/shard_map/zeros/pallas_call | solution.py:319
  111.9 2.1 %collective-permute-done.4 = f32[128,128]{1,0:T(8,128)S(1)} collective-permute-done((f32[128,128]{1,0:T(8,128)S(1)}, f32[128,128]{1,0:T(8,128)S(1)}, u32[]{:S(2)}, u32[]{:S(2)}) %collective-permute-start.4) | collective-permute-done | bytes 65568 | tf_op jit(solution)/shard_map/ppermute | solution.py:253
  114.0 10.4 %finish.1 = (f32[8192,128]{1,0:T(8,128)}, f32[128,128]{1,0:T(8,128)}) custom-call(s32[24]{0:T(128)S(1)} %get-tuple-element.9.block_ref, f32[128,128]{1,0:T(8,128)S(1)} %add.19.gram_ref, f32[24,128,128]{2,1,0:T(8,128)S(1)} %get-tuple-element.11.normal_ref, f32[8192,128]{1,0:T(8,128)} %zeros.1.zeroed_ref), custom_call_target="tpu_custom_call", output_to_operand_aliasing={{0}: (3, {})} | custom-call | tf_op jit(solution)/shard_map/finish/pallas_call | solution.py:341
  (5 shorter events, 0.0 us)
Async XLA Ops:
  0.6 22.2 %copy-start.3 = (s32[512]{0:T(512)S(1)}, s32[512]{0:T(512)}, u32[]{:S(2)}) copy-start(s32[512]{0:T(512)} %ray_ref.1) | copy-start | bytes 6148
  0.6 22.2 %copy-start.4 = (s32[512]{0:T(512)S(1)}, s32[512]{0:T(512)}, u32[]{:S(2)}) copy-start(s32[512]{0:T(512)} %col_ref.1) | copy-start | bytes 6148
  2.7 20.2 %copy-start.5 = (s32[24]{0:T(128)S(1)}, s32[24]{0:T(128)}, u32[]{:S(2)}) copy-start(s32[24]{0:T(128)} %get-tuple-element.8.place_ref) | copy-start | bytes 292
  19.3 22.4 %all-to-all-start.1 = ((bf16[8,3,128,128]{3,2,1,0:T(8,128)(2,1)}), bf16[8,3,128,128]{3,2,1,0:T(8,128)(2,1)S(1)}, u32[]{:S(2)}, u32[]{:S(2)}) async-start(bf16[8,3,128,128]{3,2,1,0:T(8,128)(2,1)} %bitcast.14), calls=%async_computation.1 | async-start | bytes 1572864 | tf_op jit(solution)/shard_map/all_to_all | solution.py:287
  31.9 8.3 %copy-start = (bf16[4096,3072]{1,0:T(8,128)(2,1)}, bf16[4096,3072]{1,0:T(8,128)(2,1)S(1)}, u32[]{:S(2)}) copy-start(bf16[4096,3072]{1,0:T(8,128)(2,1)S(1)} %load.1.dense_ref) | copy-start | bytes 75497472
  41.7 8.2 %copy-start.1 = (bf16[4096,3072]{1,0:T(8,128)(2,1)S(1)}, bf16[4096,3072]{1,0:T(8,128)(2,1)}, u32[]{:S(2)}) copy-start(bf16[4096,3072]{1,0:T(8,128)(2,1)} %copy-done) | copy-start | bytes 75497472
  49.9 39.9 %copy-start.2 = (s32[8,1,3]{2,1,0:T(1,128)S(1)}, s32[8,1,3]{2,1,0:T(1,128)}, u32[]{:S(2)}) copy-start(s32[8,1,3]{2,1,0:T(1,128)} %all_to_all.21) | copy-start | bytes 292
  94.4 1.3 %collective-permute-start = (f32[128,128]{1,0:T(8,128)S(1)}, f32[128,128]{1,0:T(8,128)S(1)}, u32[]{:S(2)}, u32[]{:S(2)}) collective-permute-start(f32[128,128]{1,0:T(8,128)S(1)} %get-tuple-element.10), channel_id=1, source_target_pairs={{0,8},{8,0},{16,24},{24,16},{1,9},{9,1},{17,25},{25,17},{2,10},{10... | collective-permute-start | bytes 196616 | tf_op jit(solution)/shard_map/ppermute | solution.py:253
  95.7 4.3 %collective-permute-start.1 = (f32[128,128]{1,0:T(8,128)S(1)}, f32[128,128]{1,0:T(8,128)S(1)}, u32[]{:S(2)}, u32[]{:S(2)}) collective-permute-start(f32[128,128]{1,0:T(8,128)S(1)} %add.15), channel_id=1, source_target_pairs={{0,16},{8,24},{16,0},{24,8},{1,17},{9,25},{17,1},{25,9},{2,18},{10... | collective-permute-start | bytes 196616 | tf_op jit(solution)/shard_map/ppermute | solution.py:253
  100.1 4.3 %collective-permute-start.2 = (f32[128,128]{1,0:T(8,128)S(1)}, f32[128,128]{1,0:T(8,128)S(1)}, u32[]{:S(2)}, u32[]{:S(2)}) collective-permute-start(f32[128,128]{1,0:T(8,128)S(1)} %add.16), channel_id=1, source_target_pairs={{0,1},{1,0},{2,3},{3,2},{4,5},{5,4},{6,7},{7,6},{8,9},{9,8},{10,11... | collective-permute-start | bytes 196616 | tf_op jit(solution)/shard_map/ppermute | solution.py:253
  104.4 4.3 %collective-permute-start.3 = (f32[128,128]{1,0:T(8,128)S(1)}, f32[128,128]{1,0:T(8,128)S(1)}, u32[]{:S(2)}, u32[]{:S(2)}) collective-permute-start(f32[128,128]{1,0:T(8,128)S(1)} %add.17), channel_id=1, source_target_pairs={{0,2},{1,3},{2,0},{3,1},{4,6},{5,7},{6,4},{7,5},{8,10},{9,11},{10,... | collective-permute-start | bytes 196616 | tf_op jit(solution)/shard_map/ppermute | solution.py:253
  108.7 5.2 %collective-permute-start.4 = (f32[128,128]{1,0:T(8,128)S(1)}, f32[128,128]{1,0:T(8,128)S(1)}, u32[]{:S(2)}, u32[]{:S(2)}) collective-permute-start(f32[128,128]{1,0:T(8,128)S(1)} %add.18), channel_id=1, source_target_pairs={{0,4},{1,5},{2,6},{3,7},{4,0},{5,1},{6,2},{7,3},{8,12},{9,13},{10,... | collective-permute-start | bytes 196616 | tf_op jit(solution)/shard_map/ppermute | solution.py:253

commit v3 on v2

--- a/solution.py
+++ b/solution.py
@@ -14,6 +14,8 @@
 gram_shift = 0.001
 
 MIB = 2**20
+IMAGE_STEP = 1024
+PART_STEP = 768
 SMEM = pl.BlockSpec(memory_space=pltpu.SMEM)
 VMEM = pl.BlockSpec(memory_space=pltpu.VMEM)
 ANY = pl.BlockSpec(memory_space=pl.ANY)
@@ -31,7 +33,7 @@
     return pltpu.with_memory_space_constraint(value, pltpu.HBM)
 
 
-def plan_kernel(block_count, touched_ref, home_ref, request_ref, position_ref, used_ref):
+def plan_kernel(block_count, me_ref, touched_ref, home_ref, request_ref, place_ref, used_ref):
     group_size = request_ref.shape[0]
 
     @pl.loop(0, group_size)
@@ -47,60 +49,122 @@
         slot = used_ref[holder]
         used_ref[holder] = slot + 1
         request_ref[holder, slot] = lax.rem(stored, block_count)
-        position_ref[entry] = holder * CAP + slot
-
-
-def serve_kernel(asked_ref, sketch_ref, served_ref, sem):
-    slots, tile_size, width = served_ref.shape
-
-    def copy(slot):
-        row = jnp.maximum(asked_ref[lax.div(slot, CAP), lax.rem(slot, CAP)], 0)
-        return pltpu.make_async_copy(sketch_ref.at[row], served_ref.at[slot], sem)
-
-    @pl.loop(0, slots)
-    def _(slot):
-        copy(slot).start()
-
-    pltpu.make_async_copy(served_ref, served_ref, sem).wait()
-
-
-def load_kernel(ray_ref, col_ref, place_ref, tiles_ref, dense_ref, sem):
-    count, tile_size, _ = tiles_ref.shape
+        place_ref[entry] = jnp.bitwise_xor(holder, me_ref[0]) * CAP + slot
+
+
+def serve_kernel(me_ref, asked_ref, _, sketch_ref, *refs):
+    served_refs, sem = refs[:-1], refs[-1]
+
+    for differs, served_ref in enumerate(served_refs):
+        for slot in range(CAP):
+            row = jnp.maximum(asked_ref[jnp.bitwise_xor(me_ref[0], differs), slot], 0)
+            pltpu.make_async_copy(sketch_ref.at[row], served_ref.at[slot], sem).start()
+
+    for served_ref in served_refs:
+        pltpu.make_async_copy(served_ref, served_ref, sem).wait()
+
+
+def table_kernel(ray_ref, col_ref, place_ref, table_ref):
+    slots = table_ref.shape[0] // RB_DEV
+
+    @pl.loop(0, table_ref.shape[0], unroll=8)
+    def _(cell):
+        table_ref[cell] = -1
+
+    @pl.loop(0, ray_ref.shape[0], unroll=8)
+    def _(tile):
+        table_ref[ray_ref[tile] * slots + place_ref[col_ref[tile]]] = tile
+
+
+def fill(first, table_ref, tiles_ref, dense_ref, blank_ref, sems):
+    tile_size = tiles_ref.shape[1]
     rows, cols = dense_ref.shape
+    some, slots = cols // tile_size, table_ref.shape[0] // (rows // tile_size)
+    blank_ref[...] = jnp.zeros(blank_ref.shape, blank_ref.dtype)
 
     @pl.loop(0, rows // tile_size)
     def _(block):
-        dense_ref[pl.ds(block * tile_size, tile_size), :] = jnp.zeros((tile_size, cols), dense_ref.dtype)
-
-    @pl.loop(0, count)
-    def _(tile):
-        row = pl.multiple_of(ray_ref[tile] * tile_size, tile_size)
-        col = pl.multiple_of(place_ref[col_ref[tile]] * tile_size, tile_size)
-        pltpu.make_async_copy(
-            tiles_ref.at[tile],
-            dense_ref.at[pl.ds(row, tile_size), pl.ds(col, tile_size)],
-            sem,
-        ).start()
-
-    filled = dense_ref.at[:, pl.ds(0, count * tile_size * tile_size // rows)]
-    pltpu.make_async_copy(filled, filled, sem).wait()
-
-
-def project_kernel(dense_ref, sketch_ref, part_ref, images_ref):
-    rows, cols = dense_ref.shape
-    step = 256
-
-    @pl.loop(0, rows // step)
+        sem = sems.at[lax.div(block, IMAGE_STEP // tile_size)]
+        row = pl.multiple_of(block * tile_size, tile_size)
+        for slot in range(some):
+            tile = table_ref[block * slots + first + slot]
+            to = dense_ref.at[pl.ds(row, tile_size), slot * tile_size : (slot + 1) * tile_size]
+
+            @pl.when(tile >= 0)
+            def _(tile=tile, to=to):
+                pltpu.make_async_copy(tiles_ref.at[tile], to, sem).start()
+
+            @pl.when(tile < 0)
+            def _(to=to):
+                pltpu.make_async_copy(blank_ref, to, sem).start()
+
+
+def filled(dense_ref, sems, chunk):
+    rows = dense_ref.at[pl.ds(pl.multiple_of(chunk * IMAGE_STEP, IMAGE_STEP), IMAGE_STEP)]
+    pltpu.make_async_copy(rows, rows, sems.at[chunk]).wait()
+
+
+def stack(refs, stacked_ref, sem):
+    copies, at = [], 0
+    for ref in refs:
+        for i in range(ref.shape[0]):
+            to = stacked_ref.at[at : at + ref.shape[1]]
+            copies.append(pltpu.make_async_copy(ref.at[i], to, sem))
+            at += ref.shape[1]
+    for copy in copies:
+        copy.start()
+
+
+def near_kernel(holders, table_ref, tiles_ref, *refs):
+    sketch_refs, (sum_ref, dense_ref, blank_ref, sems, sketch_ref, sem) = refs[:holders], refs[holders:]
+    stack(sketch_refs, sketch_ref, sem)
+    fill(0, table_ref, tiles_ref, dense_ref, blank_ref, sems)
+    pltpu.make_async_copy(sketch_ref, sketch_ref, sem).wait()
+
+    @pl.loop(0, dense_ref.shape[0] // IMAGE_STEP)
     def _(chunk):
-        at = pl.multiple_of(chunk * step, step)
-        image = jnp.dot(dense_ref[pl.ds(at, step), :], sketch_ref[...], preferred_element_type=jnp.float32)
-        images_ref[:, pl.ds(at, step)] = image.astype(jnp.bfloat16).T
-
-    @pl.loop(0, cols // step)
+        filled(dense_ref, sems, chunk)
+        rows = pl.ds(pl.multiple_of(chunk * IMAGE_STEP, IMAGE_STEP), IMAGE_STEP)
+        sum_ref[rows, :] = jnp.dot(dense_ref[rows, :], sketch_ref[...], preferred_element_type=jnp.float32)
+
+
+def parts(images_ref, dense_ref, part_refs):
+    tall = part_refs[0].shape[0]
+    each = PART_STEP // tall
+    for first in range(0, len(part_refs), each):
+        cols = dense_ref[:, first * tall : (first + each) * tall]
+        part = jnp.dot(images_ref[...], cols, preferred_element_type=jnp.float32).T
+        for i, part_ref in enumerate(part_refs[first : first + each]):
+            part_ref[...] = part[i * tall : (i + 1) * tall].astype(part_ref.dtype)
+
+
+def far_kernel(holders, table_ref, tiles_ref, sum_ref, *refs):
+    sketch_refs, (token_ref, images_ref) = refs[:holders], refs[holders : holders + 2]
+    part_refs, (dense_ref, blank_ref, sems, sketch_ref, sem) = refs[holders + 2 : -5], refs[-5:]
+    token_ref[...] = jnp.zeros(token_ref.shape, token_ref.dtype)
+    stack(sketch_refs, sketch_ref, sem)
+    fill(holders * CAP, table_ref, tiles_ref, dense_ref, blank_ref, sems)
+    pltpu.make_async_copy(sketch_ref, sketch_ref, sem).wait()
+
+    @pl.loop(0, dense_ref.shape[0] // IMAGE_STEP)
     def _(chunk):
-        at = pl.multiple_of(chunk * step, step)
-        part = jnp.dot(images_ref[...], dense_ref[:, pl.ds(at, step)], preferred_element_type=jnp.float32)
-        part_ref[pl.ds(at, step), :] = part.T.astype(part_ref.dtype)
+        filled(dense_ref, sems, chunk)
+        rows = pl.ds(pl.multiple_of(chunk * IMAGE_STEP, IMAGE_STEP), IMAGE_STEP)
+        image = sum_ref[rows, :] + jnp.dot(dense_ref[rows, :], sketch_ref[...], preferred_element_type=jnp.float32)
+        images_ref[:, rows] = image.astype(jnp.bfloat16).T
+
+    parts(images_ref, dense_ref, part_refs)
+
+
+def rest_kernel(table_ref, tiles_ref, images_ref, _, *refs):
+    part_refs, (dense_ref, blank_ref, sems) = refs[:-3], refs[-3:]
+    fill(0, table_ref, tiles_ref, dense_ref, blank_ref, sems)
+
+    @pl.loop(0, dense_ref.shape[0] // IMAGE_STEP)
+    def _(chunk):
+        filled(dense_ref, sems, chunk)
+
+    parts(images_ref, dense_ref, part_refs)
 
 
 def zero_kernel(out_ref, zeros_ref, sem):
@@ -119,32 +183,35 @@
     return high, (value - high.astype(jnp.float32)).astype(jnp.bfloat16)
 
 
-def gather_kernel(asked_ref, arrived_ref, normal_ref, gram_ref, block_ref, seen_ref):
-    slots, tile_size, width = arrived_ref.shape
+def gather_kernel(me_ref, asked_ref, *refs):
+    arrived_refs, (normal_ref, gram_ref, block_ref, seen_ref) = refs[:-4], refs[-4:]
+    slots, tile_size, width = normal_ref.shape
 
     @pl.loop(0, seen_ref.shape[0])
     def _(row):
         seen_ref[row] = -1
 
+    @pl.loop(0, slots)
+    def _(slot):
+        block_ref[slot] = -1
+
     normal_ref[...] = jnp.zeros(normal_ref.shape, normal_ref.dtype)
-
-    def place(slot, filled):
-        row = asked_ref[lax.div(slot, CAP), lax.rem(slot, CAP)]
-        safe = jnp.maximum(row, 0)
-        known = seen_ref[safe]
-        fresh = jnp.logical_and(row >= 0, known < 0)
-        at = jnp.where(known < 0, filled, known)
-        block_ref[slot] = -1
-
-        @pl.when(row >= 0)
-        def _():
-            seen_ref[safe] = at
-            block_ref[at] = safe
-            normal_ref[at] += arrived_ref[slot].astype(jnp.float32)
-
-        return jnp.where(fresh, filled + 1, filled)
-
-    lax.fori_loop(0, slots, place, 0)
+    filled = 0
+    for differs, arrived_ref in enumerate(arrived_refs):
+        for slot in range(CAP):
+            row = asked_ref[jnp.bitwise_xor(me_ref[0], differs), slot]
+            safe = jnp.maximum(row, 0)
+            known = seen_ref[safe]
+            fresh = jnp.logical_and(row >= 0, known < 0)
+            at = jnp.where(known < 0, filled, known)
+
+            @pl.when(row >= 0)
+            def _(at=at, safe=safe, arrived_ref=arrived_ref, slot=slot):
+                seen_ref[safe] = at
+                block_ref[at] = safe
+                normal_ref[at] += arrived_ref[pl.ds(slot * tile_size, tile_size), :].astype(jnp.float32)
+
+            filled = jnp.where(fresh, filled + 1, filled)
 
     gram_ref[...] = jnp.zeros(gram_ref.shape, gram_ref.dtype)
 
@@ -255,6 +322,13 @@
     return value
 
 
+def exchanged(values, first):
+    size = lax.axis_size("dev")
+    return [
+        lax.ppermute(value, "dev", [(j, j ^ (first + i)) for j in range(size)]) for i, value in enumerate(values)
+    ]
+
+
 def local(tiles, tile_ray, tile_col, touched, home, sketch):
     group_size = lax.axis_size("dev")
     tile_size = tiles.shape[1]
@@ -264,57 +338,92 @@
     slots = group_size * CAP
     voxels = sketch.shape[0] * lax.axis_size("grp") * group_size
 
-    request, position = pl.pallas_call(
+    half = group_size // 2
+    rows, tall = RB_DEV * tile_size, CAP * tile_size
+    me = lax.axis_index("dev").astype(jnp.int32).reshape(1)
+
+    request, place = pl.pallas_call(
         functools.partial(plan_kernel, block_count),
         out_shape=(
             jax.ShapeDtypeStruct((group_size, CAP), jnp.int32),
             jax.ShapeDtypeStruct((ntouch,), jnp.int32),
         ),
-        in_specs=[SMEM, SMEM],
+        in_specs=[SMEM, SMEM, SMEM],
         out_specs=(SMEM, SMEM),
         scratch_shapes=[pltpu.SMEM((group_size,), jnp.int32)],
         name="plan",
-    )(touched, home)
+    )(me, touched, home)
+    table = pl.pallas_call(
+        table_kernel,
+        out_shape=jax.ShapeDtypeStruct((RB_DEV * slots,), jnp.int32),
+        in_specs=[SMEM, SMEM, SMEM],
+        out_specs=SMEM,
+        name="table",
+    )(tile_ray, tile_col, place)
     asked = lax.all_to_all(request, "dev", split_axis=0, concat_axis=0, tiled=True)
     served = pl.pallas_call(
         serve_kernel,
-        out_shape=jax.ShapeDtypeStruct((slots, tile_size, width), sketch.dtype),
-        in_specs=[SMEM, ANY],
-        out_specs=VMEM,
+        out_shape=[jax.ShapeDtypeStruct((CAP, tile_size, width), sketch.dtype)] * group_size,
+        in_specs=[SMEM, SMEM, ANY, ANY],
+        out_specs=[VMEM] * group_size,
         scratch_shapes=[pltpu.SemaphoreType.DMA],
         name="serve",
-    )(asked, in_hbm(sketch.reshape(block_count, tile_size, width)))
-    replies = lax.all_to_all(
-        served.reshape(group_size, CAP, tile_size, width), "dev", split_axis=0, concat_axis=0, tiled=True
-    ).reshape(slots, tile_size, width)
-
-    whole = slots == ntouch
-    place = position if whole else jnp.arange(ntouch, dtype=jnp.int32)
-    dense = pl.pallas_call(
-        load_kernel,
-        out_shape=in_vmem((RB_DEV * tile_size, ntouch * tile_size), tiles.dtype),
-        in_specs=[SMEM, SMEM, SMEM, ANY],
-        out_specs=VMEM,
-        scratch_shapes=[pltpu.SemaphoreType.DMA],
-        compiler_params=pltpu.CompilerParams(vmem_limit_bytes=8 * MIB),
-        name="load",
-    )(tile_ray, tile_col, place, in_hbm(tiles))
-    columns = replies if whole else jnp.take(replies, position, axis=0)
-    part = pl.pallas_call(
-        project_kernel,
-        out_shape=jax.ShapeDtypeStruct((ntouch * tile_size, width), jnp.bfloat16),
-        in_specs=[VMEM, VMEM],
-        out_specs=VMEM,
-        scratch_shapes=[pltpu.VMEM((width, RB_DEV * tile_size), jnp.bfloat16)],
-        compiler_params=pltpu.CompilerParams(vmem_limit_bytes=16 * MIB),
-        name="project",
-    )(held(dense), columns.reshape(ntouch * tile_size, width))
-    part = part.reshape(ntouch, tile_size, width)
-    if not whole:
-        part = jnp.zeros((slots, tile_size, width), part.dtype).at[position].set(part)
-    arrived = lax.all_to_all(
-        part.reshape(group_size, CAP, tile_size, width), "dev", split_axis=0, concat_axis=0, tiled=True
-    ).reshape(slots, tile_size, width)
+    )(me, asked, table, in_hbm(sketch.reshape(block_count, tile_size, width)))
+    replies = [served[0]] + exchanged(served[1:], 1)
+
+    def with_tiles(kernel, outs, specs, operands, scratch, name, flops):
+        return pl.pallas_call(
+            kernel,
+            out_shape=outs,
+            in_specs=[SMEM, ANY] + specs,
+            out_specs=[VMEM] * len(outs),
+            scratch_shapes=[
+                pltpu.VMEM((rows, half * tall), tiles.dtype),
+                pltpu.VMEM((tile_size, tile_size), tiles.dtype),
+                pltpu.SemaphoreType.DMA((rows // IMAGE_STEP,)),
+            ]
+            + scratch,
+            compiler_params=pltpu.CompilerParams(vmem_limit_bytes=40 * MIB),
+            cost_estimate=pl.CostEstimate(flops=flops, bytes_accessed=tiles.size, transcendentals=0),
+            name=name,
+        )(in_hbm(table), in_hbm(tiles), *operands)
+
+    flops = 2 * rows * half * tall * width
+    stacked = [pltpu.VMEM((half * tall, width), sketch.dtype), pltpu.SemaphoreType.DMA]
+    (begun,) = with_tiles(
+        functools.partial(near_kernel, half),
+        [jax.ShapeDtypeStruct((rows, width), jnp.float32)],
+        [ANY] * half,
+        [in_hbm(block) for block in replies[:half]],
+        stacked,
+        "images_near",
+        flops,
+    )
+    token, images, *far_parts = with_tiles(
+        functools.partial(far_kernel, half),
+        [
+            jax.ShapeDtypeStruct((8, width), jnp.float32),
+            jax.ShapeDtypeStruct((width, rows), jnp.bfloat16),
+        ]
+        + [jax.ShapeDtypeStruct((tall, width), jnp.bfloat16)] * half,
+        [VMEM] + [ANY] * half,
+        [begun] + [in_hbm(block) for block in replies[half:]],
+        stacked,
+        "images_far",
+        2 * flops,
+    )
+    far_arrived = exchanged(far_parts, half)
+    own_part, *near_parts = with_tiles(
+        rest_kernel,
+        [jax.ShapeDtypeStruct((tall, width), jnp.float32)]
+        + [jax.ShapeDtypeStruct((tall, width), jnp.bfloat16)] * (half - 1),
+        [VMEM, ANY],
+        [images, exchanged([token], 1)[0]],
+        [],
+        "parts_near",
+        flops,
+    )
+    arrived = [own_part] + exchanged(near_parts, 1) + far_arrived
 
     zeroed = pl.pallas_call(
         zero_kernel,
@@ -331,12 +440,12 @@
             jax.ShapeDtypeStruct((width, width), jnp.float32),
             jax.ShapeDtypeStruct((slots,), jnp.int32),
         ),
-        in_specs=[SMEM, VMEM],
+        in_specs=[SMEM, SMEM] + [VMEM] * group_size,
         out_specs=(VMEM, VMEM, SMEM),
         scratch_shapes=[pltpu.SMEM((block_count,), jnp.int32)],
         compiler_params=pltpu.CompilerParams(vmem_limit_bytes=16 * MIB),
         name="collect",
-    )(asked, arrived)
+    )(me, asked, *arrived)
     gram = summed(summed(gram, "grp"), "dev")
     return pl.pallas_call(
         functools.partial(finish_kernel, voxels),

time: 125 us -> 111 us (0.89)
  blocking collectives: 36.9 us -> 0 us
  starting transfers between devices: 9.04 us -> 37 us
  local copies, waits for them, and re-layouts: 16.5 us -> 2.5 us
  Pallas kernels: 47.7 us -> 52.4 us
  waiting for transfers between devices: 13.5 us -> 17.2 us
    all_to_all x2 -> x0, blocking collectives: 36.9 us -> none  [the longest x1 23.1 us: local(): lax.all_to_all(part.reshape(group_size, CAP, tile_size, width), 'dev', sp...]
    ppermute x0 -> x15, starting transfers between devices: none -> 23 us  [exchanged(): lax.ppermute(value, 'dev', [(j, j ^ first + i) for j in range(size)])]
    unnamed x12 -> x18, local copies, waits for them, and re-layouts: 16.5 us -> 2.5 us
    pallas_call x3 -> x5, Pallas kernels: 28.6 us -> 33.6 us  [the longest x3 27.2 us: with_tiles(): pl.pallas_call(kernel, out_shape=outs, in_specs=[SMEM, ANY] + specs, out_...]
    all_to_all x1, starting transfers between devices: 3.56 us -> 7.26 us  [local(): lax.all_to_all(request, 'dev', split_axis=0, concat_axis=0, tiled=True)]
    ppermute x0 -> x15, waiting for transfers between devices: none -> 3.66 us  [exchanged(): lax.ppermute(value, 'dev', [(j, j ^ first + i) for j in range(size)])]
  transfers between devices with their start and end apart: 6 -> 21, of which waited for: 6 -> 9; matrix products, arithmetic and copies ran while one was open for 0% -> 0% of each run, Pallas kernels for 9% -> 20%
where the time goes in v3:
time: 111 us; the launch traced here: 110 us
  Pallas kernels  52.4 us (47%)
  starting transfers between devices  37 us (33%)
  waiting for transfers between devices  17.2 us (15%)
  local copies, waits for them, and re-layouts  2.5 us (2%)
    pallas_call x3, Pallas kernels, with_tiles(): pl.pallas_call(kernel, out_shape=outs, in_specs=[SMEM, ANY] + specs, out_...  27.2 us
    ppermute x15, starting transfers between devices, exchanged(): lax.ppermute(value, 'dev', [(j, j ^ first + i) for j in range(size)])  23 us
    ppermute x5, waiting for transfers between devices, summed(): lax.ppermute(value, axis, [(i, i ^ step) for i in range(size)])  10.8 us
    pallas_call x1, Pallas kernels, local(): pl.pallas_call(functools.partial(finish_kernel, voxels), out_shape=(jax.S...  10.4 us
    all_to_all x1, starting transfers between devices, local(): lax.all_to_all(request, 'dev', split_axis=0, concat_axis=0, tiled=True)  7.26 us
    ppermute x5, starting transfers between devices, summed(): lax.ppermute(value, axis, [(i, i ^ step) for i in range(size)])  6.69 us
    pallas_call x1, Pallas kernels, local(): pl.pallas_call(gather_kernel, out_shape=(in_vmem((slots, tile_size, width...  4.45 us
    ppermute x15, waiting for transfers between devices, exchanged(): lax.ppermute(value, 'dev', [(j, j ^ first + i) for j in range(size)])  3.66 us
  transfers between devices with their start and end apart: 21, of which 9 were waited for; matrix products, arithmetic and copies ran while one was open for 0% of the time, Pallas kernels for 20%

profile of v3, /device:TPU:0, one launch (start us, length us, event | category | flops | bytes accessed | tf_op | source)
XLA Modules:
  0.0 109.9 jit_solution(9617508866621332561)
XLA Ops:
  0.6 1.9 %plan.1 = (s32[8,3]{1,0:T(8,128)}, s32[24]{0:T(128)}) custom-call(s32[1]{0:T(128)} %bitcast.me_ref, s32[24]{0:T(128)} %touched_ref.1, s32[2048]{0:T(1024)} %home_ref.1), custom_call_target="tpu_custom_call" | custom-call | tf_op jit(solution)/shard_map/plan/pallas_call | solution.py:345
  2.5 7.3 %all-to-all-start = ((s32[8,1,3]{2,1,0:T(1,128)}), s32[8,1,3]{2,1,0:T(1,128)S(1)}, u32[]{:S(2)}, u32[]{:S(2)}) async-start(s32[8,1,3]{2,1,0:T(1,128)} %bitcast.9), calls=%async_computation | async-start | bytes 8192 | tf_op jit(solution)/shard_map/all_to_all | solution.py:363
  9.8 3.7 %table.1._.table_ref = s32[768]{0:T(1024)} custom-call(s32[512]{0:T(512)} %ray_ref.1, s32[512]{0:T(512)} %col_ref.1, s32[24]{0:T(128)} %get-tuple-element.26.place_ref), custom_call_target="tpu_custom_call" | custom-call | tf_op jit(solution)/shard_map/table/pallas_call | solution.py:356
  13.5 2.7 %all-to-all-done = s32[8,1,3]{2,1,0:T(1,128)S(1)} async-done(((s32[8,1,3]{2,1,0:T(1,128)}), s32[8,1,3]{2,1,0:T(1,128)S(1)}, u32[]{:S(2)}, u32[]{:S(2)}) %all-to-all-start) | async-done | bytes 128 | tf_op jit(solution)/shard_map/all_to_all | solution.py:363
  16.2 0.6 copy-done
  16.8 2.7 %serve.1 = (bf16[3,128,128]{2,1,0:T(8,128)(2,1)}, bf16[3,128,128]{2,1,0:T(8,128)(2,1)}, bf16[3,128,128]{2,1,0:T(8,128)(2,1)}, bf16[3,128,128]{2,1,0:T(8,128)(2,1...) custom-call(s32[1]{0:T(128)} %bitcast.me_ref, ...), custom_call_target="tpu_custom_call" | custom-call | tf_op jit(solution)/shard_map/serve/pallas_call | solution.py:364
  19.5 0.6 collective-permute-start
  20.1 0.6 collective-permute-start.1
  20.7 2.4 %collective-permute-start.2 = (bf16[3,128,128]{2,1,0:T(8,128)(2,1)}, bf16[3,128,128]{2,1,0:T(8,128)(2,1)S(1)}, u32[]{:S(2)}, u32[]{:S(2)}) collective-permute-start(bf16[3,128,128]{2,1,0:T(8,128)(2,1)} %get-tuple-element.30), channel_id=1, source_target_pairs={{0,3},{1,2},{2,1},{3,0},{4,7},{5,6},{6,5},{7,4},{8,11},{9,10},{10,... | collective-permute-start | bytes 294920 | tf_op jit(solution)/shard_map/ppermute | solution.py:328
  23.0 0.6 collective-permute-start.3
  23.6 2.4 %collective-permute-start.4 = (bf16[3,128,128]{2,1,0:T(8,128)(2,1)}, bf16[3,128,128]{2,1,0:T(8,128)(2,1)S(1)}, u32[]{:S(2)}, u32[]{:S(2)}) collective-permute-start(bf16[3,128,128]{2,1,0:T(8,128)(2,1)} %get-tuple-element.32), channel_id=1, source_target_pairs={{0,5},{1,4},{2,7},{3,6},{4,1},{5,0},{6,3},{7,2},{8,13},{9,12},{10,... | collective-permute-start | bytes 294920 | tf_op jit(solution)/shard_map/ppermute | solution.py:328
  26.0 2.0 %collective-permute-start.5 = (bf16[3,128,128]{2,1,0:T(8,128)(2,1)}, bf16[3,128,128]{2,1,0:T(8,128)(2,1)S(1)}, u32[]{:S(2)}, u32[]{:S(2)}) collective-permute-start(bf16[3,128,128]{2,1,0:T(8,128)(2,1)} %get-tuple-element.33), channel_id=1, source_target_pairs={{0,6},{1,7},{2,4},{3,5},{4,2},{5,3},{6,0},{7,1},{8,14},{9,15},{10,... | collective-permute-start | bytes 294920 | tf_op jit(solution)/shard_map/ppermute | solution.py:328
  28.0 0.0 collective-permute-done.1.refs_2_
  28.0 2.7 %collective-permute-start.6 = (bf16[3,128,128]{2,1,0:T(8,128)(2,1)}, bf16[3,128,128]{2,1,0:T(8,128)(2,1)S(1)}, u32[]{:S(2)}, u32[]{:S(2)}) collective-permute-start(bf16[3,128,128]{2,1,0:T(8,128)(2,1)} %get-tuple-element.34), channel_id=1, source_target_pairs={{0,7},{1,6},{2,5},{3,4},{4,3},{5,2},{6,1},{7,0},{8,15},{9,14},{10,... | collective-permute-start | bytes 294920 | tf_op jit(solution)/shard_map/ppermute | solution.py:328
  30.7 0.0 collective-permute-done.2.refs_3_
  30.7 0.6 copy-done.8
  31.3 8.6 %images_near.1.sum_ref = f32[4096,128]{1,0:T(8,128)S(1)} custom-call(s32[768]{0:T(1024)} %table.1._.table_ref, bf16[512,128,128]{2,1,0:T(8,128)(2,1)} %tiles_ref.5, bf16[3,128,128]{2,1,0:T(8,128)(2,1)} %get-tuple-element.27.refs_0_, bf16[3,128,128]{2,1,0:T(8,128)(2,1)} %copy-done.5, bf16[3,128,128]{2,1,0:T(8,128)(2,1)} %copy-done.6, ...), custom_call_target="tpu_custom_call" | custom-call | flops 1610612736 | bytes 8388608 | tf_op jit(solution)/shard_map/images_near/pallas_call | solution.py:375
  39.9 0.0 collective-permute-done.3.refs_0_
  39.9 0.0 copy-start.2
  40.0 0.6 copy-done.2
  40.6 0.0 copy-done.3
  40.6 0.0 copy-done.4
  40.6 0.6 copy-done.7
  41.3 10.9 %images_far.1 = (f32[8,128]{1,0:T(8,128)S(1)}, bf16[128,4096]{1,0:T(8,128)(2,1)S(1)}, bf16[384,128]{1,0:T(8,128)(2,1)S(1)}, bf16[384,128]{1,0:T(8,128)(2,1)S(1)}...) custom-call(s32[768]{0:T(1024)} %table.1._.table_ref, bf16[512,128,128]{2,1,0:T(8,128)(2,1)} %tiles_ref.5, ...), custom_call_target="tpu_custom_call" | custom-call | flops 3221225472 | bytes 8388608 | tf_op jit(solution)/shard_map/images_far/pallas_call | solution.py:375
  52.1 0.6 collective-permute-start.7
  52.8 2.5 %collective-permute-start.11 = (bf16[384,128]{1,0:T(8,128)(2,1)S(1)}, bf16[384,128]{1,0:T(8,128)(2,1)S(1)}, u32[]{:S(2)}, u32[]{:S(2)}) collective-permute-start(bf16[384,128]{1,0:T(8,128)(2,1)S(1)} %get-tuple-element.41), channel_id=1, source_target_pairs={{0,4},{1,5},{2,6},{3,7},{4,0},{5,1},{6,2},{7,3},{8,12},{9,13},{10,... | collective-permute-start | bytes 294920 | tf_op jit(solution)/shard_map/ppermute | solution.py:328
  55.3 1.3 %collective-permute-start.12 = (bf16[384,128]{1,0:T(8,128)(2,1)S(1)}, bf16[384,128]{1,0:T(8,128)(2,1)S(1)}, u32[]{:S(2)}, u32[]{:S(2)}) collective-permute-start(bf16[384,128]{1,0:T(8,128)(2,1)S(1)} %get-tuple-element.42), channel_id=1, source_target_pairs={{0,5},{1,4},{2,7},{3,6},{4,1},{5,0},{6,3},{7,2},{8,13},{9,12},{10,... | collective-permute-start | bytes 294920 | tf_op jit(solution)/shard_map/ppermute | solution.py:328
  56.6 1.2 %collective-permute-start.13 = (bf16[384,128]{1,0:T(8,128)(2,1)S(1)}, bf16[384,128]{1,0:T(8,128)(2,1)S(1)}, u32[]{:S(2)}, u32[]{:S(2)}) collective-permute-start(bf16[384,128]{1,0:T(8,128)(2,1)S(1)} %get-tuple-element.43), channel_id=1, source_target_pairs={{0,6},{1,7},{2,4},{3,5},{4,2},{5,3},{6,0},{7,1},{8,14},{9,15},{10,... | collective-permute-start | bytes 294920 | tf_op jit(solution)/shard_map/ppermute | solution.py:328
  57.8 2.6 %collective-permute-start.14 = (bf16[384,128]{1,0:T(8,128)(2,1)S(1)}, bf16[384,128]{1,0:T(8,128)(2,1)S(1)}, u32[]{:S(2)}, u32[]{:S(2)}) collective-permute-start(bf16[384,128]{1,0:T(8,128)(2,1)S(1)} %get-tuple-element.44), channel_id=1, source_target_pairs={{0,7},{1,6},{2,5},{3,4},{4,3},{5,2},{6,1},{7,0},{8,15},{9,14},{10,... | collective-permute-start | bytes 294920 | tf_op jit(solution)/shard_map/ppermute | solution.py:328
  60.4 7.8 %parts_near.1 = (f32[384,128]{1,0:T(8,128)S(1)}, bf16[384,128]{1,0:T(8,128)(2,1)S(1)}, bf16[384,128]{1,0:T(8,128)(2,1)S(1)}, bf16[384,128]{1,0:T(8,128)(2,1)S(1)}) custom-call(s32[768]{0:T(1024)} %table.1._.table_ref, bf16[512,128,128]{2,1,0:T(8,128)(2,1)} %tiles_ref.5, bf16[128,4096]{1,0:T(8,128)(2,1)S(1)} %get-tuple-element.35.images_ref, ...), custom_call_target="tpu_custom_call" | custom-call | flops 1610612736 | bytes 8388608 | tf_op jit(solution)/shard_map/parts_near/pallas_call | solution.py:375
  68.2 1.5 %collective-permute-start.8 = (bf16[384,128]{1,0:T(8,128)(2,1)S(1)}, bf16[384,128]{1,0:T(8,128)(2,1)S(1)}, u32[]{:S(2)}, u32[]{:S(2)}) collective-permute-start(bf16[384,128]{1,0:T(8,128)(2,1)S(1)} %get-tuple-element.38), channel_id=1, source_target_pairs={{0,1},{1,0},{2,3},{3,2},{4,5},{5,4},{6,7},{7,6},{8,9},{9,8},{10,11... | collective-permute-start | bytes 294920 | tf_op jit(solution)/shard_map/ppermute | solution.py:328
  69.7 2.0 %collective-permute-start.10 = (bf16[384,128]{1,0:T(8,128)(2,1)S(1)}, bf16[384,128]{1,0:T(8,128)(2,1)S(1)}, u32[]{:S(2)}, u32[]{:S(2)}) collective-permute-start(bf16[384,128]{1,0:T(8,128)(2,1)S(1)} %get-tuple-element.40), channel_id=1, source_target_pairs={{0,3},{1,2},{2,1},{3,0},{4,7},{5,6},{6,5},{7,4},{8,11},{9,10},{10,... | collective-permute-start | bytes 294920 | tf_op jit(solution)/shard_map/ppermute | solution.py:328
  71.8 1.1 %collective-permute-done.8.refs_1_ = bf16[384,128]{1,0:T(8,128)(2,1)S(1)} collective-permute-done((bf16[384,128]{1,0:T(8,128)(2,1)S(1)}, bf16[384,128]{1,0:T(8,128)(2,1)S(1)}, u32[]{:S(2)}, u32[]{:S(2)}) %collective-permute-start.8) | collective-permute-done | bytes 98336 | tf_op jit(solution)/shard_map/ppermute | solution.py:328
  72.9 1.4 %collective-permute-done.9.refs_2_ = bf16[384,128]{1,0:T(8,128)(2,1)S(1)} collective-permute-done((bf16[384,128]{1,0:T(8,128)(2,1)S(1)}, bf16[384,128]{1,0:T(8,128)(2,1)S(1)}, u32[]{:S(2)}, u32[]{:S(2)}) %collective-permute-start.9) | collective-permute-done | bytes 98336 | tf_op jit(solution)/shard_map/ppermute | solution.py:328
  74.3 1.1 collective-permute-done.10.refs_3_
  75.4 4.5 %collect.1 = (f32[24,128,128]{2,1,0:T(8,128)S(1)}, f32[128,128]{1,0:T(8,128)S(1)}, s32[24]{0:T(128)S(1)}) custom-call(s32[1]{0:T(128)} %bitcast.me_ref, s32[8,3]{1,0:T(8,128)S(1)} %bitcast.7, f32[384,128]{1,0:T(8,128)S(1)} %get-tuple-element.37.refs_0_, bf16[384,128]{1,0:T(8,128)(2,1)S(1)} %collective-permute-done.8.refs_1_, ...), custom_call_target="tpu_custom_call" | custom-call | tf_op jit(solution)/shard_map/collect/pallas_call | solution.py:436
  79.9 0.1 collective-permute-start.15
  79.9 1.2 %collective-permute-done.15 = f32[128,128]{1,0:T(8,128)S(1)} collective-permute-done((f32[128,128]{1,0:T(8,128)S(1)}, f32[128,128]{1,0:T(8,128)S(1)}, u32[]{:S(2)}, u32[]{:S(2)}) %collective-permute-start.15) | collective-permute-done | bytes 65568 | tf_op jit(solution)/shard_map/ppermute | solution.py:320
  81.2 1.6 %collective-permute-start.16 = (f32[128,128]{1,0:T(8,128)S(1)}, f32[128,128]{1,0:T(8,128)S(1)}, u32[]{:S(2)}, u32[]{:S(2)}) collective-permute-start(f32[128,128]{1,0:T(8,128)S(1)} %add.15), channel_id=1, source_target_pairs={{0,16},{8,24},{16,0},{24,8},{1,17},{9,25},{17,1},{25,9},{2,18},{10... | collective-permute-start | bytes 196616 | tf_op jit(solution)/shard_map/ppermute | solution.py:320
  82.8 2.7 %collective-permute-done.16 = f32[128,128]{1,0:T(8,128)S(1)} collective-permute-done((f32[128,128]{1,0:T(8,128)S(1)}, f32[128,128]{1,0:T(8,128)S(1)}, u32[]{:S(2)}, u32[]{:S(2)}) %collective-permute-start.16) | collective-permute-done | bytes 65568 | tf_op jit(solution)/shard_map/ppermute | solution.py:320
  85.5 1.5 %collective-permute-start.17 = (f32[128,128]{1,0:T(8,128)S(1)}, f32[128,128]{1,0:T(8,128)S(1)}, u32[]{:S(2)}, u32[]{:S(2)}) collective-permute-start(f32[128,128]{1,0:T(8,128)S(1)} %add.16), channel_id=1, source_target_pairs={{0,1},{1,0},{2,3},{3,2},{4,5},{5,4},{6,7},{7,6},{8,9},{9,8},{10,11... | collective-permute-start | bytes 196616 | tf_op jit(solution)/shard_map/ppermute | solution.py:320
  87.0 2.8 %collective-permute-done.17 = f32[128,128]{1,0:T(8,128)S(1)} collective-permute-done((f32[128,128]{1,0:T(8,128)S(1)}, f32[128,128]{1,0:T(8,128)S(1)}, u32[]{:S(2)}, u32[]{:S(2)}) %collective-permute-start.17) | collective-permute-done | bytes 65568 | tf_op jit(solution)/shard_map/ppermute | solution.py:320
  89.9 1.9 %collective-permute-start.18 = (f32[128,128]{1,0:T(8,128)S(1)}, f32[128,128]{1,0:T(8,128)S(1)}, u32[]{:S(2)}, u32[]{:S(2)}) collective-permute-start(f32[128,128]{1,0:T(8,128)S(1)} %add.17), channel_id=1, source_target_pairs={{0,2},{1,3},{2,0},{3,1},{4,6},{5,7},{6,4},{7,5},{8,10},{9,11},{10,... | collective-permute-start | bytes 196616 | tf_op jit(solution)/shard_map/ppermute | solution.py:320
  91.8 2.4 %collective-permute-done.18 = f32[128,128]{1,0:T(8,128)S(1)} collective-permute-done((f32[128,128]{1,0:T(8,128)S(1)}, f32[128,128]{1,0:T(8,128)S(1)}, u32[]{:S(2)}, u32[]{:S(2)}) %collective-permute-start.18) | collective-permute-done | bytes 65568 | tf_op jit(solution)/shard_map/ppermute | solution.py:320
  94.2 1.6 %collective-permute-start.19 = (f32[128,128]{1,0:T(8,128)S(1)}, f32[128,128]{1,0:T(8,128)S(1)}, u32[]{:S(2)}, u32[]{:S(2)}) collective-permute-start(f32[128,128]{1,0:T(8,128)S(1)} %add.18), channel_id=1, source_target_pairs={{0,4},{1,5},{2,6},{3,7},{4,0},{5,1},{6,2},{7,3},{8,12},{9,13},{10,... | collective-permute-start | bytes 196616 | tf_op jit(solution)/shard_map/ppermute | solution.py:320
  95.8 2.0 %zeros.1.zeroed_ref = f32[8192,128]{1,0:T(8,128)} custom-call(), custom_call_target="tpu_custom_call" | custom-call | tf_op jit(solution)/shard_map/zeros/pallas_call | solution.py:428
  97.9 1.6 %collective-permute-done.19 = f32[128,128]{1,0:T(8,128)S(1)} collective-permute-done((f32[128,128]{1,0:T(8,128)S(1)}, f32[128,128]{1,0:T(8,128)S(1)}, u32[]{:S(2)}, u32[]{:S(2)}) %collective-permute-start.19) | collective-permute-done | bytes 65568 | tf_op jit(solution)/shard_map/ppermute | solution.py:320
  99.5 10.4 %finish.1 = (f32[8192,128]{1,0:T(8,128)}, f32[128,128]{1,0:T(8,128)}) custom-call(s32[24]{0:T(128)S(1)} %get-tuple-element.45.block_ref, f32[128,128]{1,0:T(8,128)S(1)} %add.19.gram_ref, f32[24,128,128]{2,1,0:T(8,128)S(1)} %get-tuple-element.47.normal_ref, f32[8192,128]{1,0:T(8,128)} %zeros.1.zeroed_ref), custom_call_target="tpu_custom_call", output_to_operand_aliasing={{0}: (3, {})} | custom-call | tf_op jit(solution)/shard_map/finish/pallas_call | solution.py:450
  (26 shorter events, 0.1 us)
Async XLA Ops:
  2.5 13.7 %all-to-all-start = ((s32[8,1,3]{2,1,0:T(1,128)}), s32[8,1,3]{2,1,0:T(1,128)S(1)}, u32[]{:S(2)}, u32[]{:S(2)}) async-start(s32[8,1,3]{2,1,0:T(1,128)} %bitcast.9), calls=%async_computation | async-start | bytes 8192 | tf_op jit(solution)/shard_map/all_to_all | solution.py:363
  16.2 0.6 copy-start
  19.5 6.5 %collective-permute-start = (bf16[3,128,128]{2,1,0:T(8,128)(2,1)}, bf16[3,128,128]{2,1,0:T(8,128)(2,1)S(1)}, u32[]{:S(2)}, u32[]{:S(2)}) collective-permute-start(bf16[3,128,128]{2,1,0:T(8,128)(2,1)} %get-tuple-element.28), channel_id=1, source_target_pairs={{0,1},{1,0},{2,3},{3,2},{4,5},{5,4},{6,7},{7,6},{8,9},{9,8},{10,11... | collective-permute-start | bytes 294920 | tf_op jit(solution)/shard_map/ppermute | solution.py:328
  20.1 7.9 %collective-permute-start.1 = (bf16[3,128,128]{2,1,0:T(8,128)(2,1)}, bf16[3,128,128]{2,1,0:T(8,128)(2,1)S(1)}, u32[]{:S(2)}, u32[]{:S(2)}) collective-permute-start(bf16[3,128,128]{2,1,0:T(8,128)(2,1)} %get-tuple-element.29), channel_id=1, source_target_pairs={{0,2},{1,3},{2,0},{3,1},{4,6},{5,7},{6,4},{7,5},{8,10},{9,11},{10,... | collective-permute-start | bytes 294920 | tf_op jit(solution)/shard_map/ppermute | solution.py:328
  20.7 10.0 %collective-permute-start.2 = (bf16[3,128,128]{2,1,0:T(8,128)(2,1)}, bf16[3,128,128]{2,1,0:T(8,128)(2,1)S(1)}, u32[]{:S(2)}, u32[]{:S(2)}) collective-permute-start(bf16[3,128,128]{2,1,0:T(8,128)(2,1)} %get-tuple-element.30), channel_id=1, source_target_pairs={{0,3},{1,2},{2,1},{3,0},{4,7},{5,6},{6,5},{7,4},{8,11},{9,10},{10,... | collective-permute-start | bytes 294920 | tf_op jit(solution)/shard_map/ppermute | solution.py:328
  23.0 16.9 %collective-permute-start.3 = (bf16[3,128,128]{2,1,0:T(8,128)(2,1)}, bf16[3,128,128]{2,1,0:T(8,128)(2,1)S(1)}, u32[]{:S(2)}, u32[]{:S(2)}) collective-permute-start(bf16[3,128,128]{2,1,0:T(8,128)(2,1)} %get-tuple-element.31), channel_id=1, source_target_pairs={{0,4},{1,5},{2,6},{3,7},{4,0},{5,1},{6,2},{7,3},{8,12},{9,13},{10,... | collective-permute-start | bytes 294920 | tf_op jit(solution)/shard_map/ppermute | solution.py:328
  23.6 16.4 %collective-permute-start.4 = (bf16[3,128,128]{2,1,0:T(8,128)(2,1)}, bf16[3,128,128]{2,1,0:T(8,128)(2,1)S(1)}, u32[]{:S(2)}, u32[]{:S(2)}) collective-permute-start(bf16[3,128,128]{2,1,0:T(8,128)(2,1)} %get-tuple-element.32), channel_id=1, source_target_pairs={{0,5},{1,4},{2,7},{3,6},{4,1},{5,0},{6,3},{7,2},{8,13},{9,12},{10,... | collective-permute-start | bytes 294920 | tf_op jit(solution)/shard_map/ppermute | solution.py:328
  26.0 4.8 %copy-start.5 = (bf16[3,128,128]{2,1,0:T(8,128)(2,1)}, bf16[3,128,128]{2,1,0:T(8,128)(2,1)S(1)}, u32[]{:S(2)}) copy-start(bf16[3,128,128]{2,1,0:T(8,128)(2,1)S(1)} %collective-permute-done.refs_1_) | copy-start | bytes 294916
  26.0 14.0 %collective-permute-start.5 = (bf16[3,128,128]{2,1,0:T(8,128)(2,1)}, bf16[3,128,128]{2,1,0:T(8,128)(2,1)S(1)}, u32[]{:S(2)}, u32[]{:S(2)}) collective-permute-start(bf16[3,128,128]{2,1,0:T(8,128)(2,1)} %get-tuple-element.33), channel_id=1, source_target_pairs={{0,6},{1,7},{2,4},{3,5},{4,2},{5,3},{6,0},{7,1},{8,14},{9,15},{10,... | collective-permute-start | bytes 294920 | tf_op jit(solution)/shard_map/ppermute | solution.py:328
  28.0 2.7 %copy-start.6 = (bf16[3,128,128]{2,1,0:T(8,128)(2,1)}, bf16[3,128,128]{2,1,0:T(8,128)(2,1)S(1)}, u32[]{:S(2)}) copy-start(bf16[3,128,128]{2,1,0:T(8,128)(2,1)S(1)} %collective-permute-done.1.refs_2_) | copy-start | bytes 294916
  28.0 12.0 %collective-permute-start.6 = (bf16[3,128,128]{2,1,0:T(8,128)(2,1)}, bf16[3,128,128]{2,1,0:T(8,128)(2,1)S(1)}, u32[]{:S(2)}, u32[]{:S(2)}) collective-permute-start(bf16[3,128,128]{2,1,0:T(8,128)(2,1)} %get-tuple-element.34), channel_id=1, source_target_pairs={{0,7},{1,6},{2,5},{3,4},{4,3},{5,2},{6,1},{7,0},{8,15},{9,14},{10,... | collective-permute-start | bytes 294920 | tf_op jit(solution)/shard_map/ppermute | solution.py:328
  30.7 0.6 copy-start.8
  39.9 0.6 copy-start.2
  40.0 0.6 copy-start.3
  40.0 0.6 copy-start.4
  40.6 0.6 copy-start.7
  52.1 8.3 %collective-permute-start.7 = (f32[8,128]{1,0:T(8,128)S(1)}, f32[8,128]{1,0:T(8,128)S(1)}, u32[]{:S(2)}, u32[]{:S(2)}) collective-permute-start(f32[8,128]{1,0:T(8,128)S(1)} %get-tuple-element.36), channel_id=1, source_target_pairs={{0,1},{1,0},{2,3},{3,2},{4,5},{5,4},{6,7},{7,6},{8,9},{9,8},{10,11... | collective-permute-start | bytes 12296 | tf_op jit(solution)/shard_map/ppermute | solution.py:328
  52.8 16.9 %collective-permute-start.11 = (bf16[384,128]{1,0:T(8,128)(2,1)S(1)}, bf16[384,128]{1,0:T(8,128)(2,1)S(1)}, u32[]{:S(2)}, u32[]{:S(2)}) collective-permute-start(bf16[384,128]{1,0:T(8,128)(2,1)S(1)} %get-tuple-element.41), channel_id=1, source_target_pairs={{0,4},{1,5},{2,6},{3,7},{4,0},{5,1},{6,2},{7,3},{8,12},{9,13},{10,... | collective-permute-start | bytes 294920 | tf_op jit(solution)/shard_map/ppermute | solution.py:328
  55.3 14.4 %collective-permute-start.12 = (bf16[384,128]{1,0:T(8,128)(2,1)S(1)}, bf16[384,128]{1,0:T(8,128)(2,1)S(1)}, u32[]{:S(2)}, u32[]{:S(2)}) collective-permute-start(bf16[384,128]{1,0:T(8,128)(2,1)S(1)} %get-tuple-element.42), channel_id=1, source_target_pairs={{0,5},{1,4},{2,7},{3,6},{4,1},{5,0},{6,3},{7,2},{8,13},{9,12},{10,... | collective-permute-start | bytes 294920 | tf_op jit(solution)/shard_map/ppermute | solution.py:328
  56.6 15.2 %collective-permute-start.13 = (bf16[384,128]{1,0:T(8,128)(2,1)S(1)}, bf16[384,128]{1,0:T(8,128)(2,1)S(1)}, u32[]{:S(2)}, u32[]{:S(2)}) collective-permute-start(bf16[384,128]{1,0:T(8,128)(2,1)S(1)} %get-tuple-element.43), channel_id=1, source_target_pairs={{0,6},{1,7},{2,4},{3,5},{4,2},{5,3},{6,0},{7,1},{8,14},{9,15},{10,... | collective-permute-start | bytes 294920 | tf_op jit(solution)/shard_map/ppermute | solution.py:328
  57.8 14.0 %collective-permute-start.14 = (bf16[384,128]{1,0:T(8,128)(2,1)S(1)}, bf16[384,128]{1,0:T(8,128)(2,1)S(1)}, u32[]{:S(2)}, u32[]{:S(2)}) collective-permute-start(bf16[384,128]{1,0:T(8,128)(2,1)S(1)} %get-tuple-element.44), channel_id=1, source_target_pairs={{0,7},{1,6},{2,5},{3,4},{4,3},{5,2},{6,1},{7,0},{8,15},{9,14},{10,... | collective-permute-start | bytes 294920 | tf_op jit(solution)/shard_map/ppermute | solution.py:328
  60.4 15.0 %copy-start.1 = (s32[8,1,3]{2,1,0:T(1,128)S(1)}, s32[8,1,3]{2,1,0:T(1,128)}, u32[]{:S(2)}) copy-start(s32[8,1,3]{2,1,0:T(1,128)} %copy-done) | copy-start | bytes 292
  68.2 4.7 %collective-permute-start.8 = (bf16[384,128]{1,0:T(8,128)(2,1)S(1)}, bf16[384,128]{1,0:T(8,128)(2,1)S(1)}, u32[]{:S(2)}, u32[]{:S(2)}) collective-permute-start(bf16[384,128]{1,0:T(8,128)(2,1)S(1)} %get-tuple-element.38), channel_id=1, source_target_pairs={{0,1},{1,0},{2,3},{3,2},{4,5},{5,4},{6,7},{7,6},{8,9},{9,8},{10,11... | collective-permute-start | bytes 294920 | tf_op jit(solution)/shard_map/ppermute | solution.py:328
  69.7 4.6 %collective-permute-start.9 = (bf16[384,128]{1,0:T(8,128)(2,1)S(1)}, bf16[384,128]{1,0:T(8,128)(2,1)S(1)}, u32[]{:S(2)}, u32[]{:S(2)}) collective-permute-start(bf16[384,128]{1,0:T(8,128)(2,1)S(1)} %get-tuple-element.39), channel_id=1, source_target_pairs={{0,2},{1,3},{2,0},{3,1},{4,6},{5,7},{6,4},{7,5},{8,10},{9,11},{10,... | collective-permute-start | bytes 294920 | tf_op jit(solution)/shard_map/ppermute | solution.py:328
  69.7 5.7 %collective-permute-start.10 = (bf16[384,128]{1,0:T(8,128)(2,1)S(1)}, bf16[384,128]{1,0:T(8,128)(2,1)S(1)}, u32[]{:S(2)}, u32[]{:S(2)}) collective-permute-start(bf16[384,128]{1,0:T(8,128)(2,1)S(1)} %get-tuple-element.40), channel_id=1, source_target_pairs={{0,3},{1,2},{2,1},{3,0},{4,7},{5,6},{6,5},{7,4},{8,11},{9,10},{10,... | collective-permute-start | bytes 294920 | tf_op jit(solution)/shard_map/ppermute | solution.py:328
  79.9 1.3 %collective-permute-start.15 = (f32[128,128]{1,0:T(8,128)S(1)}, f32[128,128]{1,0:T(8,128)S(1)}, u32[]{:S(2)}, u32[]{:S(2)}) collective-permute-start(f32[128,128]{1,0:T(8,128)S(1)} %get-tuple-element.46), channel_id=1, source_target_pairs={{0,8},{8,0},{16,24},{24,16},{1,9},{9,1},{17,25},{25,17},{2,10},{10... | collective-permute-start | bytes 196616 | tf_op jit(solution)/shard_map/ppermute | solution.py:320
  81.2 4.3 %collective-permute-start.16 = (f32[128,128]{1,0:T(8,128)S(1)}, f32[128,128]{1,0:T(8,128)S(1)}, u32[]{:S(2)}, u32[]{:S(2)}) collective-permute-start(f32[128,128]{1,0:T(8,128)S(1)} %add.15), channel_id=1, source_target_pairs={{0,16},{8,24},{16,0},{24,8},{1,17},{9,25},{17,1},{25,9},{2,18},{10... | collective-permute-start | bytes 196616 | tf_op jit(solution)/shard_map/ppermute | solution.py:320
  85.5 4.3 %collective-permute-start.17 = (f32[128,128]{1,0:T(8,128)S(1)}, f32[128,128]{1,0:T(8,128)S(1)}, u32[]{:S(2)}, u32[]{:S(2)}) collective-permute-start(f32[128,128]{1,0:T(8,128)S(1)} %add.16), channel_id=1, source_target_pairs={{0,1},{1,0},{2,3},{3,2},{4,5},{5,4},{6,7},{7,6},{8,9},{9,8},{10,11... | collective-permute-start | bytes 196616 | tf_op jit(solution)/shard_map/ppermute | solution.py:320
  89.9 4.3 %collective-permute-start.18 = (f32[128,128]{1,0:T(8,128)S(1)}, f32[128,128]{1,0:T(8,128)S(1)}, u32[]{:S(2)}, u32[]{:S(2)}) collective-permute-start(f32[128,128]{1,0:T(8,128)S(1)} %add.17), channel_id=1, source_target_pairs={{0,2},{1,3},{2,0},{3,1},{4,6},{5,7},{6,4},{7,5},{8,10},{9,11},{10,... | collective-permute-start | bytes 196616 | tf_op jit(solution)/shard_map/ppermute | solution.py:320
  94.2 5.2 %collective-permute-start.19 = (f32[128,128]{1,0:T(8,128)S(1)}, f32[128,128]{1,0:T(8,128)S(1)}, u32[]{:S(2)}, u32[]{:S(2)}) collective-permute-start(f32[128,128]{1,0:T(8,128)S(1)} %add.18), channel_id=1, source_target_pairs={{0,4},{1,5},{2,6},{3,7},{4,0},{5,1},{6,2},{7,3},{8,12},{9,13},{10,... | collective-permute-start | bytes 196616 | tf_op jit(solution)/shard_map/ppermute | solution.py:320

commit v4 on v3

--- a/solution.py
+++ b/solution.py
@@ -16,6 +16,7 @@
 MIB = 2**20
 IMAGE_STEP = 1024
 PART_STEP = 768
+BASIS_SLOTS = 2 * CAP
 SMEM = pl.BlockSpec(memory_space=pltpu.SMEM)
 VMEM = pl.BlockSpec(memory_space=pltpu.VMEM)
 ANY = pl.BlockSpec(memory_space=pl.ANY)
@@ -52,7 +53,7 @@
         place_ref[entry] = jnp.bitwise_xor(holder, me_ref[0]) * CAP + slot
 
 
-def serve_kernel(me_ref, asked_ref, _, sketch_ref, *refs):
+def serve_kernel(me_ref, asked_ref, sketch_ref, *refs):
     served_refs, sem = refs[:-1], refs[-1]
 
     for differs, served_ref in enumerate(served_refs):
@@ -64,44 +65,83 @@
         pltpu.make_async_copy(served_ref, served_ref, sem).wait()
 
 
-def table_kernel(ray_ref, col_ref, place_ref, table_ref):
-    slots = table_ref.shape[0] // RB_DEV
-
-    @pl.loop(0, table_ref.shape[0], unroll=8)
-    def _(cell):
-        table_ref[cell] = -1
-
-    @pl.loop(0, ray_ref.shape[0], unroll=8)
+FIELD = 6
+BUNCH = 4
+
+
+def pack(tile, ray, slot):
+    return lax.shift_left(lax.shift_left(tile, FIELD) + ray, FIELD) + slot
+
+
+def unpack(entry):
+    mask = 2**FIELD - 1
+    cell = lax.shift_right_logical(entry, FIELD)
+    return lax.shift_right_logical(cell, FIELD), jnp.bitwise_and(cell, mask), jnp.bitwise_and(entry, mask)
+
+
+def list_kernel(chunks, slots, ray_ref, col_ref, place_ref, list_ref, count_ref):
+    room = list_ref.shape[0] // (2 * chunks)
+    rays, half = RB_DEV // chunks, slots // 2
+
+    @pl.loop(0, 2 * chunks)
+    def _(which):
+        count_ref[which] = 0
+
+    @pl.loop(0, ray_ref.shape[0], unroll=4)
     def _(tile):
-        table_ref[ray_ref[tile] * slots + place_ref[col_ref[tile]]] = tile
-
-
-def fill(first, table_ref, tiles_ref, dense_ref, blank_ref, sems):
+        ray, slot = ray_ref[tile], place_ref[col_ref[tile]]
+        far = (slot >= half).astype(jnp.int32)
+        which = far * chunks + lax.div(ray, rays)
+        count = count_ref[which]
+        list_ref[which * room + count] = pack(tile, ray, slot - far * half)
+        count_ref[which] = count + 1
+
+    @pl.loop(0, 2 * chunks)
+    def _(which):
+        for _ in range(BUNCH - 1):
+            count = count_ref[which]
+
+            @pl.when(jnp.bitwise_and(count, BUNCH - 1) != 0)
+            def _(count=count):
+                list_ref[which * room + count] = RB_DEV << FIELD
+                count_ref[which] = count + 1
+
+
+def fill(far, list_ref, count_ref, tiles_ref, dense_ref, sems):
     tile_size = tiles_ref.shape[1]
-    rows, cols = dense_ref.shape
-    some, slots = cols // tile_size, table_ref.shape[0] // (rows // tile_size)
-    blank_ref[...] = jnp.zeros(blank_ref.shape, blank_ref.dtype)
+    rows, cols = dense_ref.shape[0] - tile_size, dense_ref.shape[1]
+    chunks = rows // IMAGE_STEP
+    room = list_ref.shape[0] // (2 * chunks)
 
     @pl.loop(0, rows // tile_size)
     def _(block):
-        sem = sems.at[lax.div(block, IMAGE_STEP // tile_size)]
-        row = pl.multiple_of(block * tile_size, tile_size)
-        for slot in range(some):
-            tile = table_ref[block * slots + first + slot]
-            to = dense_ref.at[pl.ds(row, tile_size), slot * tile_size : (slot + 1) * tile_size]
-
-            @pl.when(tile >= 0)
-            def _(tile=tile, to=to):
-                pltpu.make_async_copy(tiles_ref.at[tile], to, sem).start()
-
-            @pl.when(tile < 0)
-            def _(to=to):
-                pltpu.make_async_copy(blank_ref, to, sem).start()
-
-
-def filled(dense_ref, sems, chunk):
-    rows = dense_ref.at[pl.ds(pl.multiple_of(chunk * IMAGE_STEP, IMAGE_STEP), IMAGE_STEP)]
-    pltpu.make_async_copy(rows, rows, sems.at[chunk]).wait()
+        at = pl.multiple_of(block * tile_size, tile_size)
+        dense_ref[pl.ds(at, tile_size), :] = jnp.zeros((tile_size, cols), dense_ref.dtype)
+
+    for chunk in range(chunks):
+        which = far * chunks + chunk
+
+        @pl.loop(0, lax.shift_right_logical(count_ref[which], BUNCH.bit_length() - 1))
+        def _(bunch, which=which, chunk=chunk):
+            entries = [list_ref[which * room + bunch * BUNCH + i] for i in range(BUNCH)]
+            for tile, ray, slot in map(unpack, entries):
+                row = pl.multiple_of(ray * tile_size, tile_size)
+                col = pl.multiple_of(slot * tile_size, tile_size)
+                to = dense_ref.at[pl.ds(row, tile_size), pl.ds(col, tile_size)]
+                pltpu.make_async_copy(tiles_ref.at[tile], to, sems.at[chunk]).start()
+
+
+def filled(far, count_ref, tiles_ref, sems, chunk):
+    count = count_ref[far * sems.shape[0] + chunk]
+    size = 1
+    while size <= tiles_ref.shape[0]:
+
+        @pl.when(jnp.bitwise_and(count, size) != 0)
+        def _(size=size):
+            some = tiles_ref.at[:size]
+            pltpu.make_async_copy(some, some, sems.at[chunk]).wait()
+
+        size *= 2
 
 
 def stack(refs, stacked_ref, sem):
@@ -115,40 +155,76 @@
         copy.start()
 
 
-def near_kernel(holders, table_ref, tiles_ref, *refs):
-    sketch_refs, (sum_ref, dense_ref, blank_ref, sems, sketch_ref, sem) = refs[:holders], refs[holders:]
+def load_kernel(ray_ref, col_ref, place_ref, tiles_ref, _, dense_ref, sem):
+    count, tile_size, _ = tiles_ref.shape
+    rows, cols = dense_ref.shape
+
+    @pl.loop(0, rows // tile_size)
+    def _(block):
+        at = pl.multiple_of(block * tile_size, tile_size)
+        dense_ref[pl.ds(at, tile_size), :] = jnp.zeros((tile_size, cols), dense_ref.dtype)
+
+    @pl.loop(0, count, unroll=8)
+    def _(tile):
+        row = pl.multiple_of(ray_ref[tile] * tile_size, tile_size)
+        col = pl.multiple_of(place_ref[col_ref[tile]] * tile_size, tile_size)
+        to = dense_ref.at[pl.ds(row, tile_size), pl.ds(col, tile_size)]
+        pltpu.make_async_copy(tiles_ref.at[tile], to, sem).start()
+
+    pltpu.make_async_copy(tiles_ref, tiles_ref, sem).wait()
+
+
+def half_of(far, kept, refs):
+    if kept:
+        dense_ref, *refs = refs
+        cols = dense_ref.shape[1] // 2
+        return dense_ref.at[:, far * cols : (far + 1) * cols], lambda chunk: None, refs
+    list_ref, count_ref, tiles_ref, *refs = refs
+    *refs, dense_ref, sems = refs
+    fill(far, list_ref, count_ref, tiles_ref, dense_ref, sems)
+    return dense_ref, functools.partial(filled, far, count_ref, tiles_ref, sems), refs
+
+
+def near_kernel(kept, *refs):
+    dense_ref, ready, refs = half_of(0, kept, refs)
+    *sketch_refs, sum_ref, sketch_ref, sem = refs
     stack(sketch_refs, sketch_ref, sem)
-    fill(0, table_ref, tiles_ref, dense_ref, blank_ref, sems)
     pltpu.make_async_copy(sketch_ref, sketch_ref, sem).wait()
 
-    @pl.loop(0, dense_ref.shape[0] // IMAGE_STEP)
+    @pl.loop(0, sum_ref.shape[0] // IMAGE_STEP)
     def _(chunk):
-        filled(dense_ref, sems, chunk)
+        ready(chunk)
         rows = pl.ds(pl.multiple_of(chunk * IMAGE_STEP, IMAGE_STEP), IMAGE_STEP)
         sum_ref[rows, :] = jnp.dot(dense_ref[rows, :], sketch_ref[...], preferred_element_type=jnp.float32)
 
 
+def hand_out(total, part_refs):
+    tall = part_refs[0].shape[0]
+    for i, part_ref in enumerate(part_refs):
+        part_ref[...] = total[:, i * tall : (i + 1) * tall].T.astype(part_ref.dtype)
+
+
 def parts(images_ref, dense_ref, part_refs):
-    tall = part_refs[0].shape[0]
+    rows, tall = images_ref.shape[1], part_refs[0].shape[0]
     each = PART_STEP // tall
     for first in range(0, len(part_refs), each):
-        cols = dense_ref[:, first * tall : (first + each) * tall]
-        part = jnp.dot(images_ref[...], cols, preferred_element_type=jnp.float32).T
-        for i, part_ref in enumerate(part_refs[first : first + each]):
-            part_ref[...] = part[i * tall : (i + 1) * tall].astype(part_ref.dtype)
-
-
-def far_kernel(holders, table_ref, tiles_ref, sum_ref, *refs):
+        cols = dense_ref[:rows, first * tall : (first + each) * tall]
+        part = jnp.dot(images_ref[...], cols, preferred_element_type=jnp.float32)
+        hand_out(part, part_refs[first : first + each])
+
+
+def far_kernel(holders, kept, *refs):
+    dense_ref, ready, refs = half_of(1, kept, refs)
+    sum_ref, *refs = refs
     sketch_refs, (token_ref, images_ref) = refs[:holders], refs[holders : holders + 2]
-    part_refs, (dense_ref, blank_ref, sems, sketch_ref, sem) = refs[holders + 2 : -5], refs[-5:]
+    *part_refs, sketch_ref, sem = refs[holders + 2 :]
     token_ref[...] = jnp.zeros(token_ref.shape, token_ref.dtype)
     stack(sketch_refs, sketch_ref, sem)
-    fill(holders * CAP, table_ref, tiles_ref, dense_ref, blank_ref, sems)
     pltpu.make_async_copy(sketch_ref, sketch_ref, sem).wait()
 
-    @pl.loop(0, dense_ref.shape[0] // IMAGE_STEP)
+    @pl.loop(0, sum_ref.shape[0] // IMAGE_STEP)
     def _(chunk):
-        filled(dense_ref, sems, chunk)
+        ready(chunk)
         rows = pl.ds(pl.multiple_of(chunk * IMAGE_STEP, IMAGE_STEP), IMAGE_STEP)
         image = sum_ref[rows, :] + jnp.dot(dense_ref[rows, :], sketch_ref[...], preferred_element_type=jnp.float32)
         images_ref[:, rows] = image.astype(jnp.bfloat16).T
@@ -156,13 +232,13 @@
     parts(images_ref, dense_ref, part_refs)
 
 
-def rest_kernel(table_ref, tiles_ref, images_ref, _, *refs):
-    part_refs, (dense_ref, blank_ref, sems) = refs[:-3], refs[-3:]
-    fill(0, table_ref, tiles_ref, dense_ref, blank_ref, sems)
-
-    @pl.loop(0, dense_ref.shape[0] // IMAGE_STEP)
+def rest_kernel(kept, *refs):
+    dense_ref, ready, refs = half_of(0, kept, refs)
+    images_ref, _, *part_refs = refs
+
+    @pl.loop(0, images_ref.shape[1] // IMAGE_STEP)
     def _(chunk):
-        filled(dense_ref, sems, chunk)
+        ready(chunk)
 
     parts(images_ref, dense_ref, part_refs)
 
@@ -184,7 +260,7 @@
 
 
 def gather_kernel(me_ref, asked_ref, *refs):
-    arrived_refs, (normal_ref, gram_ref, block_ref, seen_ref) = refs[:-4], refs[-4:]
+    arrived_refs, (split_ref, gram_ref, block_ref, normal_ref, seen_ref) = refs[:-5], refs[-5:]
     slots, tile_size, width = normal_ref.shape
 
     @pl.loop(0, seen_ref.shape[0])
@@ -214,15 +290,16 @@
             filled = jnp.where(fresh, filled + 1, filled)
 
     gram_ref[...] = jnp.zeros(gram_ref.shape, gram_ref.dtype)
-
-    @pl.loop(0, slots // CAP)
+    tall = BASIS_SLOTS * tile_size
+
+    @pl.loop(0, slots // BASIS_SLOTS)
     def _(chunk):
-        rows = jnp.concatenate([normal_ref[chunk * CAP + i] for i in range(CAP)], axis=0)
+        at = pl.multiple_of(chunk * tall, tall)
+        rows = jnp.concatenate([normal_ref[chunk * BASIS_SLOTS + i] for i in range(BASIS_SLOTS)], axis=0)
         high, low = split(rows)
-        both = lax.dot_general(
-            high, jnp.concatenate([high, low], axis=1), (((0,), (0,)), ((), ())),
-            preferred_element_type=jnp.float32,
-        )
+        both_rows = jnp.concatenate([high, low], axis=1)
+        split_ref[pl.ds(at, tall), :] = both_rows
+        both = lax.dot_general(high, both_rows, (((0,), (0,)), ((), ())), preferred_element_type=jnp.float32)
         cross = both[:, width:]
         gram_ref[...] += both[:, :width] + cross + cross.T
 
@@ -278,7 +355,7 @@
 
 def finish_kernel(voxels, block_ref, gram_ref, normal_ref, zeroed_ref, basis_ref, factor_ref, work_ref, out_ref, sem):
     width = gram_ref.shape[0]
-    slots, tile_size, _ = normal_ref.shape
+    slots, tile_size, _ = out_ref.shape
     panel = 8
     row_at = lax.broadcasted_iota(jnp.int32, (panel, width), 0)
     lane = lax.broadcasted_iota(jnp.int32, (panel, width), 1)
@@ -290,35 +367,53 @@
         factor_ref[pl.ds(panel * i, panel), :] = rows
     inverse = work_ref[...].T
     high, low = split(inverse)
-    weights = jnp.concatenate([high, high, low], axis=0)
-
-    @pl.loop(0, slots)
-    def _(slot):
-        row_high, row_low = split(normal_ref[slot])
-        out_ref[slot] = jnp.dot(
-            jnp.concatenate([row_high, row_low, row_high], axis=1), weights,
-            preferred_element_type=jnp.float32,
-        )
-
-        @pl.when(block_ref[slot] >= 0)
-        def _():
-            at = block_ref[slot] * tile_size
-            pltpu.make_async_copy(out_ref.at[slot], basis_ref.at[pl.ds(at, tile_size)], sem.at[slot]).start()
+    twice = jnp.concatenate([high, high], axis=0)
+    tall = BASIS_SLOTS * tile_size
+
+    def copy(slot):
+        at = pl.multiple_of(block_ref[slot] * tile_size, tile_size)
+        return pltpu.make_async_copy(out_ref.at[slot], basis_ref.at[pl.ds(at, tile_size)], sem.at[slot])
+
+    @pl.loop(0, slots // BASIS_SLOTS)
+    def _(chunk):
+        rows = pl.ds(pl.multiple_of(chunk * tall, tall), tall)
+        both = normal_ref[rows, :]
+        value = jnp.dot(both, twice, preferred_element_type=jnp.float32)
+        value += jnp.dot(both[:, :width], low, preferred_element_type=jnp.float32)
+        for i in range(BASIS_SLOTS):
+            slot = chunk * BASIS_SLOTS + i
+            out_ref[slot] = value[i * tile_size : (i + 1) * tile_size]
+
+            @pl.when(block_ref[slot] >= 0)
+            def _(slot=slot):
+                copy(slot).start()
 
     @pl.loop(0, slots)
     def _(slot):
         @pl.when(block_ref[slot] >= 0)
         def _():
-            at = block_ref[slot] * tile_size
-            pltpu.make_async_copy(out_ref.at[slot], basis_ref.at[pl.ds(at, tile_size)], sem.at[slot]).wait()
-
-
-def summed(value, axis):
-    size = lax.axis_size(axis)
-    step = 1
-    while step < size:
-        value = value + lax.ppermute(value, axis, [(i, i ^ step) for i in range(size)])
-        step *= 2
+            copy(slot).wait()
+
+
+def summed(value, axes):
+    outer, inner = (lax.axis_size(axis) for axis in axes)
+
+    def other(bits):
+        return lax.ppermute(value, axes, [(i, i ^ bits) for i in range(outer * inner)])
+
+    def powers(low, high):
+        return [1 << i for i in range(low.bit_length() - 1, high.bit_length() - 1)]
+
+    core, *rest = powers(inner, outer * inner)
+    near = powers(1, inner)
+    odd = len(near) % 2
+    bits = near[:odd] + rest + near[odd:]
+    value = value + other(core)
+    for i in range(0, len(bits) - 1, 2):
+        one, two = bits[i : i + 2]
+        value = (value + other(one)) + (other(two) + other(one ^ two))
+    if len(bits) % 2:
+        value = value + other(bits[-1])
     return value
 
 
@@ -353,48 +448,68 @@
         scratch_shapes=[pltpu.SMEM((group_size,), jnp.int32)],
         name="plan",
     )(me, touched, home)
-    table = pl.pallas_call(
-        table_kernel,
-        out_shape=jax.ShapeDtypeStruct((RB_DEV * slots,), jnp.int32),
-        in_specs=[SMEM, SMEM, SMEM],
-        out_specs=SMEM,
-        name="table",
-    )(tile_ray, tile_col, place)
-    asked = lax.all_to_all(request, "dev", split_axis=0, concat_axis=0, tiled=True)
+    kept = rows * slots * tile_size * tiles.dtype.itemsize <= 24 * MIB
+    chunks = rows // IMAGE_STEP
+    if not kept:
+        room = min(RB_DEV // chunks * slots // 2, tiles.shape[0] + BUNCH)
+        listed, counts = pl.pallas_call(
+            functools.partial(list_kernel, chunks, slots),
+            out_shape=(
+                jax.ShapeDtypeStruct((2 * chunks * room,), jnp.int32),
+                jax.ShapeDtypeStruct((2 * chunks,), jnp.int32),
+            ),
+            in_specs=[SMEM, SMEM, SMEM],
+            out_specs=(SMEM, SMEM),
+            name="list",
+        )(tile_ray, tile_col, place)
+        tile_operands, tile_specs = [listed, counts, in_hbm(tiles)], [SMEM, SMEM, ANY]
+        tile_scratch = [
+            pltpu.VMEM((rows + tile_size, half * tall), tiles.dtype),
+            pltpu.SemaphoreType.DMA((chunks,)),
+        ]
+    asked = held(lax.all_to_all(request, "dev", split_axis=0, concat_axis=0, tiled=True))
     served = pl.pallas_call(
         serve_kernel,
-        out_shape=[jax.ShapeDtypeStruct((CAP, tile_size, width), sketch.dtype)] * group_size,
-        in_specs=[SMEM, SMEM, ANY, ANY],
+        out_shape=[in_vmem((CAP, tile_size, width), sketch.dtype)] * group_size,
+        in_specs=[SMEM, SMEM, ANY],
         out_specs=[VMEM] * group_size,
         scratch_shapes=[pltpu.SemaphoreType.DMA],
+        compiler_params=pltpu.CompilerParams(vmem_limit_bytes=8 * MIB),
         name="serve",
-    )(me, asked, table, in_hbm(sketch.reshape(block_count, tile_size, width)))
+    )(me, asked, in_hbm(sketch.reshape(block_count, tile_size, width)))
     replies = [served[0]] + exchanged(served[1:], 1)
+
+    if kept:
+        dense = pl.pallas_call(
+            load_kernel,
+            out_shape=in_vmem((rows, slots * tile_size), tiles.dtype),
+            in_specs=[SMEM, SMEM, SMEM, ANY, ANY],
+            out_specs=VMEM,
+            scratch_shapes=[pltpu.SemaphoreType.DMA],
+            compiler_params=pltpu.CompilerParams(vmem_limit_bytes=8 * MIB),
+            name="load",
+        )(in_hbm(tile_ray), in_hbm(tile_col), in_hbm(place), in_hbm(tiles), served[0])
+        tile_operands, tile_specs, tile_scratch = [held(dense)], [VMEM], []
 
     def with_tiles(kernel, outs, specs, operands, scratch, name, flops):
         return pl.pallas_call(
-            kernel,
+            functools.partial(kernel, kept),
             out_shape=outs,
-            in_specs=[SMEM, ANY] + specs,
+            in_specs=tile_specs + specs,
             out_specs=[VMEM] * len(outs),
-            scratch_shapes=[
-                pltpu.VMEM((rows, half * tall), tiles.dtype),
-                pltpu.VMEM((tile_size, tile_size), tiles.dtype),
-                pltpu.SemaphoreType.DMA((rows // IMAGE_STEP,)),
-            ]
-            + scratch,
-            compiler_params=pltpu.CompilerParams(vmem_limit_bytes=40 * MIB),
+            scratch_shapes=scratch + tile_scratch,
+            compiler_params=pltpu.CompilerParams(vmem_limit_bytes=(12 if kept else 40) * MIB),
             cost_estimate=pl.CostEstimate(flops=flops, bytes_accessed=tiles.size, transcendentals=0),
             name=name,
-        )(in_hbm(table), in_hbm(tiles), *operands)
+        )(*tile_operands, *operands)
 
     flops = 2 * rows * half * tall * width
     stacked = [pltpu.VMEM((half * tall, width), sketch.dtype), pltpu.SemaphoreType.DMA]
     (begun,) = with_tiles(
-        functools.partial(near_kernel, half),
+        near_kernel,
         [jax.ShapeDtypeStruct((rows, width), jnp.float32)],
         [ANY] * half,
-        [in_hbm(block) for block in replies[:half]],
+        replies[:half],
         stacked,
         "images_near",
         flops,
@@ -407,7 +522,7 @@
         ]
         + [jax.ShapeDtypeStruct((tall, width), jnp.bfloat16)] * half,
         [VMEM] + [ANY] * half,
-        [begun] + [in_hbm(block) for block in replies[half:]],
+        [begun] + replies[half:],
         stacked,
         "images_far",
         2 * flops,
@@ -436,17 +551,20 @@
     normal, gram, blocks = pl.pallas_call(
         gather_kernel,
         out_shape=(
-            in_vmem((slots, tile_size, width), jnp.float32),
+            in_vmem((slots * tile_size, 2 * width), jnp.bfloat16),
             jax.ShapeDtypeStruct((width, width), jnp.float32),
             jax.ShapeDtypeStruct((slots,), jnp.int32),
         ),
         in_specs=[SMEM, SMEM] + [VMEM] * group_size,
         out_specs=(VMEM, VMEM, SMEM),
-        scratch_shapes=[pltpu.SMEM((block_count,), jnp.int32)],
+        scratch_shapes=[
+            pltpu.VMEM((slots, tile_size, width), jnp.float32),
+            pltpu.SMEM((block_count,), jnp.int32),
+        ],
         compiler_params=pltpu.CompilerParams(vmem_limit_bytes=16 * MIB),
         name="collect",
     )(me, asked, *arrived)
-    gram = summed(summed(gram, "grp"), "dev")
+    gram = summed(gram, ("grp", "dev"))
     return pl.pallas_call(
         functools.partial(finish_kernel, voxels),
         out_shape=(

time: 111 us -> 97.5 us (0.88)
  Pallas kernels: 52.4 us -> 38 us
  blocking collectives: 0 us -> 13.7 us
  starting transfers between devices: 37 us -> 28.8 us
  local copies, waits for them, and re-layouts: 2.5 us -> 0 us
  waiting for transfers between devices: 17.2 us -> 15.9 us
    all_to_all x0 -> x1, blocking collectives: none -> 13.7 us  [local(): lax.all_to_all(request, 'dev', split_axis=0, concat_axis=0, tiled=True)]
    pallas_call x6, Pallas kernels: 38 us -> 26.2 us  [the longest x3 13 us: with_tiles(): pl.pallas_call(functools.partial(kernel, kept), out_shape=outs, in_specs=...]
    all_to_all x1 -> x0, starting transfers between devices: 7.26 us -> none  [local(): lax.all_to_all(request, 'dev', split_axis=0, concat_axis=0, tiled=True)]
    ppermute x15, waiting for transfers between devices: 3.66 us -> 8.44 us  [exchanged(): lax.ppermute(value, 'dev', [(j, j ^ first + i) for j in range(size)])]
    ppermute x5 -> x7, waiting for transfers between devices: 10.8 us -> 7.48 us  [other(): lax.ppermute(value, axes, [(i, i ^ bits) for i in range(outer * inner)])]
    all_to_all x1 -> x0, waiting for transfers between devices: 2.73 us -> none  [local(): lax.all_to_all(request, 'dev', split_axis=0, concat_axis=0, tiled=True)]
    pallas_call x1, Pallas kernels: 10.4 us -> 7.87 us  [local(): pl.pallas_call(functools.partial(finish_kernel, voxels), out_shape=(jax.S...]
    unnamed x18 -> x0, local copies, waits for them, and re-layouts: 2.5 us -> none
  transfers between devices with their start and end apart: 21 -> 22, of which waited for: 9 -> 10; matrix products, arithmetic and copies ran while one was open for 0% -> 0% of each run, Pallas kernels for 20% -> 17%
where the time goes in v4:
time: 97.5 us; the launch traced here: 97.2 us
  Pallas kernels  38 us (39%)
  starting transfers between devices  28.8 us (30%)
  waiting for transfers between devices  15.9 us (16%)
  blocking collectives  13.7 us (14%)
    ppermute x15, starting transfers between devices, exchanged(): lax.ppermute(value, 'dev', [(j, j ^ first + i) for j in range(size)])  20.7 us
    all_to_all x1, blocking collectives, local(): lax.all_to_all(request, 'dev', split_axis=0, concat_axis=0, tiled=True)  13.7 us
    pallas_call x3, Pallas kernels, with_tiles(): pl.pallas_call(functools.partial(kernel, kept), out_shape=outs, in_specs=...  13 us
    ppermute x15, waiting for transfers between devices, exchanged(): lax.ppermute(value, 'dev', [(j, j ^ first + i) for j in range(size)])  8.44 us
    pallas_call x1, Pallas kernels, local(): pl.pallas_call(load_kernel, out_shape=in_vmem((rows, slots * tile_size),...  8.19 us
    ppermute x7, starting transfers between devices, other(): lax.ppermute(value, axes, [(i, i ^ bits) for i in range(outer * inner)])  8.07 us
    pallas_call x1, Pallas kernels, local(): pl.pallas_call(functools.partial(finish_kernel, voxels), out_shape=(jax.S...  7.87 us
    ppermute x7, waiting for transfers between devices, other(): lax.ppermute(value, axes, [(i, i ^ bits) for i in range(outer * inner)])  7.48 us
  transfers between devices with their start and end apart: 22, of which 10 were waited for; matrix products, arithmetic and copies ran while one was open for 0% of the time, Pallas kernels for 17%

profile of v4, /device:TPU:0, one launch (start us, length us, event | category | flops | bytes accessed | tf_op | source)
XLA Modules:
  0.0 97.2 jit_solution(3352549049338123293)
XLA Ops:
  0.6 1.9 %plan.1 = (s32[8,3]{1,0:T(8,128)}, s32[24]{0:T(128)}) custom-call(s32[1]{0:T(128)} %bitcast.me_ref, s32[24]{0:T(128)} %touched_ref.1, s32[2048]{0:T(1024)} %home_ref.1), custom_call_target="tpu_custom_call" | custom-call | tf_op jit(solution)/shard_map/plan/pallas_call | solution.py:440
  2.5 13.7 %all_to_all.11 = s32[8,1,3]{2,1,0:T(1,128)S(1)} all-to-all(s32[8,1,3]{2,1,0:T(1,128)} %bitcast.9), channel_id=1, replica_groups=mesh['grp'=4,'dev'=8] {'dev'}, dimensions={0} | all-to-all | bytes 192 | tf_op jit(solution)/shard_map/all_to_all | solution.py:470
  16.2 1.7 %serve.1 = (bf16[3,128,128]{2,1,0:T(8,128)(2,1)S(1)}, bf16[3,128,128]{2,1,0:T(8,128)(2,1)S(1)}, bf16[3,128,128]{2,1,0:T(8,128)(2,1)S(1)}, bf16[3,128,128]{2,1,0:...) custom-call(s32[1]{0:T(128)} %bitcast.me_ref, ...), custom_call_target="tpu_custom_call" | custom-call | tf_op jit(solution)/shard_map/serve/pallas_call | solution.py:471
  17.9 0.6 collective-permute-start
  18.5 0.6 collective-permute-start.1
  19.1 2.4 %collective-permute-start.2 = (bf16[3,128,128]{2,1,0:T(8,128)(2,1)S(1)}, bf16[3,128,128]{2,1,0:T(8,128)(2,1)S(1)}, u32[]{:S(2)}, u32[]{:S(2)}) collective-permute-start(bf16[3,128,128]{2,1,0:T(8,128)(2,1)S(1)} %get-tuple-element.30), channel_id=1, source_target_pairs={{0,3},{1,2},{2,1},{3,0},{4,7},{5,6},{6,5},{7,4},{8,11},{9,10},{10,... | collective-permute-start | bytes 294920 | tf_op jit(solution)/shard_map/ppermute | solution.py:423
  21.5 0.6 collective-permute-start.3
  22.0 2.4 %collective-permute-start.4 = (bf16[3,128,128]{2,1,0:T(8,128)(2,1)S(1)}, bf16[3,128,128]{2,1,0:T(8,128)(2,1)S(1)}, u32[]{:S(2)}, u32[]{:S(2)}) collective-permute-start(bf16[3,128,128]{2,1,0:T(8,128)(2,1)S(1)} %get-tuple-element.32), channel_id=1, source_target_pairs={{0,5},{1,4},{2,7},{3,6},{4,1},{5,0},{6,3},{7,2},{8,13},{9,12},{10,... | collective-permute-start | bytes 294920 | tf_op jit(solution)/shard_map/ppermute | solution.py:423
  24.4 8.2 %load.1.refs_0_ = bf16[4096,3072]{1,0:T(8,128)(2,1)S(1)} custom-call(s32[512]{0:T(512)} %ray_ref.1, s32[512]{0:T(512)} %col_ref.1, s32[24]{0:T(128)} %get-tuple-element.26.place_ref, bf16[512,128,128]{2,1,0:T(8,128)(2,1)} %tiles_ref.1, bf16[3,128,128]{2,1,0:T(8,128)(2,1)S(1)} %get-tuple-element.27._.refs_1_), custom_call_target="tpu_custom_call" | custom-call | tf_op jit(solution)/shard_map/load/pallas_call | solution.py:483
  32.6 0.0 collective-permute-done.refs_2_
  32.6 0.7 collective-permute-start.5
  33.2 4.1 %collective-permute-start.6 = (bf16[3,128,128]{2,1,0:T(8,128)(2,1)S(1)}, bf16[3,128,128]{2,1,0:T(8,128)(2,1)S(1)}, u32[]{:S(2)}, u32[]{:S(2)}) collective-permute-start(bf16[3,128,128]{2,1,0:T(8,128)(2,1)S(1)} %get-tuple-element.34), channel_id=1, source_target_pairs={{0,7},{1,6},{2,5},{3,4},{4,3},{5,2},{6,1},{7,0},{8,15},{9,14},{10,... | collective-permute-start | bytes 294920 | tf_op jit(solution)/shard_map/ppermute | solution.py:423
  37.4 0.0 collective-permute-done.2.refs_4_
  37.4 4.4 %images_near.1.refs_1_ = f32[4096,128]{1,0:T(8,128)S(1)} custom-call(bf16[4096,3072]{1,0:T(8,128)(2,1)S(1)} %load.1.refs_0_, bf16[3,128,128]{2,1,0:T(8,128)(2,1)S(1)} %get-tuple-element.27._.refs_1_, bf16[3,128,128]{2,1,0:T(8,128)(2,1)S(1)} %collective-permute-done.refs_2_, bf16[3,128,128]{2,1,0:T(8,128)(2,1)S(1)} %collective-permute-done.1.refs_3_, ...), custom_call_target="tpu_custom_call" | custom-call | flops 1610612736 | bytes 8388608 | tf_op jit(solution)/shard_map/images_near/pallas_call | solution.py:495
  41.8 0.0 collective-permute-done.4.refs_3_
  41.8 0.0 collective-permute-done.5.refs_4_
  41.8 6.6 %images_far.1 = (f32[8,128]{1,0:T(8,128)S(1)}, bf16[128,4096]{1,0:T(8,128)(2,1)S(1)}, bf16[384,128]{1,0:T(8,128)(2,1)S(1)}, bf16[384,128]{1,0:T(8,128)(2,1)S(1)}...) custom-call(bf16[4096,3072]{1,0:T(8,128)(2,1)S(1)} %load.1.refs_0_, f32[4096,128]{1,0:T(8,128)S(1)} %images_near.1.refs_1_, ...), custom_call_target="tpu_custom_call" | custom-call | flops 3221225472 | bytes 8388608 | tf_op jit(solution)/shard_map/images_far/pallas_call | solution.py:495
  48.5 0.6 collective-permute-start.7
  49.1 0.0 collective-permute-start.11
  49.1 3.8 %collective-permute-start.12 = (bf16[384,128]{1,0:T(8,128)(2,1)S(1)}, bf16[384,128]{1,0:T(8,128)(2,1)S(1)}, u32[]{:S(2)}, u32[]{:S(2)}) collective-permute-start(bf16[384,128]{1,0:T(8,128)(2,1)S(1)} %get-tuple-element.42), channel_id=1, source_target_pairs={{0,5},{1,4},{2,7},{3,6},{4,1},{5,0},{6,3},{7,2},{8,13},{9,12},{10,... | collective-permute-start | bytes 294920 | tf_op jit(solution)/shard_map/ppermute | solution.py:423
  52.9 1.9 %collective-permute-start.13 = (bf16[384,128]{1,0:T(8,128)(2,1)S(1)}, bf16[384,128]{1,0:T(8,128)(2,1)S(1)}, u32[]{:S(2)}, u32[]{:S(2)}) collective-permute-start(bf16[384,128]{1,0:T(8,128)(2,1)S(1)} %get-tuple-element.43), channel_id=1, source_target_pairs={{0,6},{1,7},{2,4},{3,5},{4,2},{5,3},{6,0},{7,1},{8,14},{9,15},{10,... | collective-permute-start | bytes 294920 | tf_op jit(solution)/shard_map/ppermute | solution.py:423
  54.9 1.9 %collective-permute-start.14 = (bf16[384,128]{1,0:T(8,128)(2,1)S(1)}, bf16[384,128]{1,0:T(8,128)(2,1)S(1)}, u32[]{:S(2)}, u32[]{:S(2)}) collective-permute-start(bf16[384,128]{1,0:T(8,128)(2,1)S(1)} %get-tuple-element.44), channel_id=1, source_target_pairs={{0,7},{1,6},{2,5},{3,4},{4,3},{5,2},{6,1},{7,0},{8,15},{9,14},{10,... | collective-permute-start | bytes 294920 | tf_op jit(solution)/shard_map/ppermute | solution.py:423
  56.8 2.0 %parts_near.1 = (f32[384,128]{1,0:T(8,128)S(1)}, bf16[384,128]{1,0:T(8,128)(2,1)S(1)}, bf16[384,128]{1,0:T(8,128)(2,1)S(1)}, bf16[384,128]{1,0:T(8,128)(2,1)S(1)}) custom-call(bf16[4096,3072]{1,0:T(8,128)(2,1)S(1)} %load.1.refs_0_, bf16[128,4096]{1,0:T(8,128)(2,1)S(1)} %get-tuple-element.35.refs_1_, f32[8,128]{1,0:T(8,128)S(1)} %collective-permute-done.7.refs_2_), custom_call_target="tpu_custom_call" | custom-call | flops 1610612736 | bytes 8388608 | tf_op jit(solution)/shard_map/parts_near/pallas_call | solution.py:495
  58.7 0.1 collective-permute-start.10
  58.8 1.7 %collective-permute-done.11.refs_4_ = bf16[384,128]{1,0:T(8,128)(2,1)S(1)} collective-permute-done((bf16[384,128]{1,0:T(8,128)(2,1)S(1)}, bf16[384,128]{1,0:T(8,128)(2,1)S(1)}, u32[]{:S(2)}, u32[]{:S(2)}) %collective-permute-start.11) | collective-permute-done | bytes 98336 | tf_op jit(solution)/shard_map/ppermute | solution.py:423
  60.5 1.1 %collective-permute-start.8 = (bf16[384,128]{1,0:T(8,128)(2,1)S(1)}, bf16[384,128]{1,0:T(8,128)(2,1)S(1)}, u32[]{:S(2)}, u32[]{:S(2)}) collective-permute-start(bf16[384,128]{1,0:T(8,128)(2,1)S(1)} %get-tuple-element.38), channel_id=1, source_target_pairs={{0,1},{1,0},{2,3},{3,2},{4,5},{5,4},{6,7},{7,6},{8,9},{9,8},{10,11... | collective-permute-start | bytes 294920 | tf_op jit(solution)/shard_map/ppermute | solution.py:423
  61.6 2.1 %collective-permute-done.12.refs_5_ = bf16[384,128]{1,0:T(8,128)(2,1)S(1)} collective-permute-done((bf16[384,128]{1,0:T(8,128)(2,1)S(1)}, bf16[384,128]{1,0:T(8,128)(2,1)S(1)}, u32[]{:S(2)}, u32[]{:S(2)}) %collective-permute-start.12) | collective-permute-done | bytes 98336 | tf_op jit(solution)/shard_map/ppermute | solution.py:423
  63.7 0.0 collective-permute-start.9
  63.7 1.1 %collective-permute-done.10.refs_3_ = bf16[384,128]{1,0:T(8,128)(2,1)S(1)} collective-permute-done((bf16[384,128]{1,0:T(8,128)(2,1)S(1)}, bf16[384,128]{1,0:T(8,128)(2,1)S(1)}, u32[]{:S(2)}, u32[]{:S(2)}) %collective-permute-start.10) | collective-permute-done | bytes 98336 | tf_op jit(solution)/shard_map/ppermute | solution.py:423
  64.8 1.0 %collective-permute-done.8.refs_1_ = bf16[384,128]{1,0:T(8,128)(2,1)S(1)} collective-permute-done((bf16[384,128]{1,0:T(8,128)(2,1)S(1)}, bf16[384,128]{1,0:T(8,128)(2,1)S(1)}, u32[]{:S(2)}, u32[]{:S(2)}) %collective-permute-start.8) | collective-permute-done | bytes 98336 | tf_op jit(solution)/shard_map/ppermute | solution.py:423
  65.8 2.5 %collective-permute-done.9.refs_2_ = bf16[384,128]{1,0:T(8,128)(2,1)S(1)} collective-permute-done((bf16[384,128]{1,0:T(8,128)(2,1)S(1)}, bf16[384,128]{1,0:T(8,128)(2,1)S(1)}, u32[]{:S(2)}, u32[]{:S(2)}) %collective-permute-start.9) | collective-permute-done | bytes 98336 | tf_op jit(solution)/shard_map/ppermute | solution.py:423
  68.3 3.3 %collect.1 = (bf16[3072,256]{1,0:T(8,128)(2,1)S(1)}, f32[128,128]{1,0:T(8,128)S(1)}, s32[24]{0:T(128)S(1)}) custom-call(s32[1]{0:T(128)} %bitcast.me_ref, s32[8,3]{1,0:T(8,128)S(1)} %bitcast.7, f32[384,128]{1,0:T(8,128)S(1)} %get-tuple-element.37.refs_0_, bf16[384,128]{1,0:T(8,128)(2,1)S(1)} %collective-permute-done.8.refs_1_, ...), custom_call_target="tpu_custom_call" | custom-call | tf_op jit(solution)/shard_map/collect/pallas_call | solution.py:551
  71.6 0.1 collective-permute-start.15
  71.7 1.2 %collective-permute-done.15 = f32[128,128]{1,0:T(8,128)S(1)} collective-permute-done((f32[128,128]{1,0:T(8,128)S(1)}, f32[128,128]{1,0:T(8,128)S(1)}, u32[]{:S(2)}, u32[]{:S(2)}) %collective-permute-start.15) | collective-permute-done | bytes 65568 | tf_op jit(solution)/shard_map/ppermute | solution.py:402
  73.0 1.4 %collective-permute-start.16 = (f32[128,128]{1,0:T(8,128)S(1)}, f32[128,128]{1,0:T(8,128)S(1)}, u32[]{:S(2)}, u32[]{:S(2)}) collective-permute-start(f32[128,128]{1,0:T(8,128)S(1)} %add.21), channel_id=1, source_target_pairs={{0,1},{1,0},{2,3},{3,2},{4,5},{5,4},{6,7},{7,6},{8,9},{9,8},{10,11... | collective-permute-start | bytes 196616 | tf_op jit(solution)/shard_map/ppermute | solution.py:402
  74.3 1.5 %collective-permute-start.17 = (f32[128,128]{1,0:T(8,128)S(1)}, f32[128,128]{1,0:T(8,128)S(1)}, u32[]{:S(2)}, u32[]{:S(2)}) collective-permute-start(f32[128,128]{1,0:T(8,128)S(1)} %add.21), channel_id=1, source_target_pairs={{0,16},{1,17},{2,18},{3,19},{4,20},{5,21},{6,22},{7,23},{8,24},{9,... | collective-permute-start | bytes 196616 | tf_op jit(solution)/shard_map/ppermute | solution.py:402
  75.8 0.7 collective-permute-start.18
  76.5 0.8 collective-permute-done.16
  77.3 1.3 %collective-permute-done.17 = f32[128,128]{1,0:T(8,128)S(1)} collective-permute-done((f32[128,128]{1,0:T(8,128)S(1)}, f32[128,128]{1,0:T(8,128)S(1)}, u32[]{:S(2)}, u32[]{:S(2)}) %collective-permute-start.17) | collective-permute-done | bytes 65568 | tf_op jit(solution)/shard_map/ppermute | solution.py:402
  78.6 2.4 %collective-permute-done.18 = f32[128,128]{1,0:T(8,128)S(1)} collective-permute-done((f32[128,128]{1,0:T(8,128)S(1)}, f32[128,128]{1,0:T(8,128)S(1)}, u32[]{:S(2)}, u32[]{:S(2)}) %collective-permute-start.18) | collective-permute-done | bytes 65568 | tf_op jit(solution)/shard_map/ppermute | solution.py:402
  81.0 0.1 collective-permute-start.19
  81.1 2.1 %collective-permute-start.20 = (f32[128,128]{1,0:T(8,128)S(1)}, f32[128,128]{1,0:T(8,128)S(1)}, u32[]{:S(2)}, u32[]{:S(2)}) collective-permute-start(f32[128,128]{1,0:T(8,128)S(1)} %add_add_fusion.1), channel_id=1, source_target_pairs={{0,4},{1,5},{2,6},{3,7},{4,0},{5,1},{6,2},{7,3},{8,12},{9,13},{10,... | collective-permute-start | bytes 196616 | tf_op jit(solution)/shard_map/ppermute | solution.py:402
  83.2 2.2 %collective-permute-start.21 = (f32[128,128]{1,0:T(8,128)S(1)}, f32[128,128]{1,0:T(8,128)S(1)}, u32[]{:S(2)}, u32[]{:S(2)}) collective-permute-start(f32[128,128]{1,0:T(8,128)S(1)} %add_add_fusion.1), channel_id=1, source_target_pairs={{0,6},{1,7},{2,4},{3,5},{4,2},{5,3},{6,0},{7,1},{8,14},{9,15},{10,... | collective-permute-start | bytes 196616 | tf_op jit(solution)/shard_map/ppermute | solution.py:402
  85.5 2.0 %zeros.1.zeroed_ref = f32[8192,128]{1,0:T(8,128)} custom-call(), custom_call_target="tpu_custom_call" | custom-call | tf_op jit(solution)/shard_map/zeros/pallas_call | solution.py:543
  87.5 0.0 collective-permute-done.19
  87.5 0.0 collective-permute-done.20
  87.6 1.8 %collective-permute-done.21 = f32[128,128]{1,0:T(8,128)S(1)} collective-permute-done((f32[128,128]{1,0:T(8,128)S(1)}, f32[128,128]{1,0:T(8,128)S(1)}, u32[]{:S(2)}, u32[]{:S(2)}) %collective-permute-start.21) | collective-permute-done | bytes 65568 | tf_op jit(solution)/shard_map/ppermute | solution.py:402
  89.3 7.9 %finish.1 = (f32[8192,128]{1,0:T(8,128)}, f32[128,128]{1,0:T(8,128)}) custom-call(s32[24]{0:T(128)S(1)} %get-tuple-element.45.block_ref, f32[128,128]{1,0:T(8,128)S(1)} %add_add_fusion.gram_ref, bf16[3072,256]{1,0:T(8,128)(2,1)S(1)} %get-tuple-element.47.normal_ref, f32[8192,128]{1,0:T(8,128)} %zeros.1.zeroed_ref), custom_call_target="tpu_custom_call", output_to_operand_aliasing={{0}: (3, {})} | custom-call | tf_op jit(solution)/shard_map/finish/pallas_call | solution.py:568
  (9 shorter events, 0.1 us)
Async XLA Ops:
  17.9 14.7 %collective-permute-start = (bf16[3,128,128]{2,1,0:T(8,128)(2,1)S(1)}, bf16[3,128,128]{2,1,0:T(8,128)(2,1)S(1)}, u32[]{:S(2)}, u32[]{:S(2)}) collective-permute-start(bf16[3,128,128]{2,1,0:T(8,128)(2,1)S(1)} %get-tuple-element.28), channel_id=1, source_target_pairs={{0,1},{1,0},{2,3},{3,2},{4,5},{5,4},{6,7},{7,6},{8,9},{9,8},{10,11... | collective-permute-start | bytes 294920 | tf_op jit(solution)/shard_map/ppermute | solution.py:423
  18.5 14.7 %collective-permute-start.1 = (bf16[3,128,128]{2,1,0:T(8,128)(2,1)S(1)}, bf16[3,128,128]{2,1,0:T(8,128)(2,1)S(1)}, u32[]{:S(2)}, u32[]{:S(2)}) collective-permute-start(bf16[3,128,128]{2,1,0:T(8,128)(2,1)S(1)} %get-tuple-element.29), channel_id=1, source_target_pairs={{0,2},{1,3},{2,0},{3,1},{4,6},{5,7},{6,4},{7,5},{8,10},{9,11},{10,... | collective-permute-start | bytes 294920 | tf_op jit(solution)/shard_map/ppermute | solution.py:423
  19.1 18.3 %collective-permute-start.2 = (bf16[3,128,128]{2,1,0:T(8,128)(2,1)S(1)}, bf16[3,128,128]{2,1,0:T(8,128)(2,1)S(1)}, u32[]{:S(2)}, u32[]{:S(2)}) collective-permute-start(bf16[3,128,128]{2,1,0:T(8,128)(2,1)S(1)} %get-tuple-element.30), channel_id=1, source_target_pairs={{0,3},{1,2},{2,1},{3,0},{4,7},{5,6},{6,5},{7,4},{8,11},{9,10},{10,... | collective-permute-start | bytes 294920 | tf_op jit(solution)/shard_map/ppermute | solution.py:423
  21.5 20.3 %collective-permute-start.3 = (bf16[3,128,128]{2,1,0:T(8,128)(2,1)S(1)}, bf16[3,128,128]{2,1,0:T(8,128)(2,1)S(1)}, u32[]{:S(2)}, u32[]{:S(2)}) collective-permute-start(bf16[3,128,128]{2,1,0:T(8,128)(2,1)S(1)} %get-tuple-element.31), channel_id=1, source_target_pairs={{0,4},{1,5},{2,6},{3,7},{4,0},{5,1},{6,2},{7,3},{8,12},{9,13},{10,... | collective-permute-start | bytes 294920 | tf_op jit(solution)/shard_map/ppermute | solution.py:423
  22.0 19.8 %collective-permute-start.4 = (bf16[3,128,128]{2,1,0:T(8,128)(2,1)S(1)}, bf16[3,128,128]{2,1,0:T(8,128)(2,1)S(1)}, u32[]{:S(2)}, u32[]{:S(2)}) collective-permute-start(bf16[3,128,128]{2,1,0:T(8,128)(2,1)S(1)} %get-tuple-element.32), channel_id=1, source_target_pairs={{0,5},{1,4},{2,7},{3,6},{4,1},{5,0},{6,3},{7,2},{8,13},{9,12},{10,... | collective-permute-start | bytes 294920 | tf_op jit(solution)/shard_map/ppermute | solution.py:423
  32.6 9.2 %collective-permute-start.5 = (bf16[3,128,128]{2,1,0:T(8,128)(2,1)S(1)}, bf16[3,128,128]{2,1,0:T(8,128)(2,1)S(1)}, u32[]{:S(2)}, u32[]{:S(2)}) collective-permute-start(bf16[3,128,128]{2,1,0:T(8,128)(2,1)S(1)} %get-tuple-element.33), channel_id=1, source_target_pairs={{0,6},{1,7},{2,4},{3,5},{4,2},{5,3},{6,0},{7,1},{8,14},{9,15},{10,... | collective-permute-start | bytes 294920 | tf_op jit(solution)/shard_map/ppermute | solution.py:423
  33.2 8.6 %collective-permute-start.6 = (bf16[3,128,128]{2,1,0:T(8,128)(2,1)S(1)}, bf16[3,128,128]{2,1,0:T(8,128)(2,1)S(1)}, u32[]{:S(2)}, u32[]{:S(2)}) collective-permute-start(bf16[3,128,128]{2,1,0:T(8,128)(2,1)S(1)} %get-tuple-element.34), channel_id=1, source_target_pairs={{0,7},{1,6},{2,5},{3,4},{4,3},{5,2},{6,1},{7,0},{8,15},{9,14},{10,... | collective-permute-start | bytes 294920 | tf_op jit(solution)/shard_map/ppermute | solution.py:423
  48.5 8.3 %collective-permute-start.7 = (f32[8,128]{1,0:T(8,128)S(1)}, f32[8,128]{1,0:T(8,128)S(1)}, u32[]{:S(2)}, u32[]{:S(2)}) collective-permute-start(f32[8,128]{1,0:T(8,128)S(1)} %get-tuple-element.36), channel_id=1, source_target_pairs={{0,1},{1,0},{2,3},{3,2},{4,5},{5,4},{6,7},{7,6},{8,9},{9,8},{10,11... | collective-permute-start | bytes 12296 | tf_op jit(solution)/shard_map/ppermute | solution.py:423
  49.1 11.4 %collective-permute-start.11 = (bf16[384,128]{1,0:T(8,128)(2,1)S(1)}, bf16[384,128]{1,0:T(8,128)(2,1)S(1)}, u32[]{:S(2)}, u32[]{:S(2)}) collective-permute-start(bf16[384,128]{1,0:T(8,128)(2,1)S(1)} %get-tuple-element.41), channel_id=1, source_target_pairs={{0,4},{1,5},{2,6},{3,7},{4,0},{5,1},{6,2},{7,3},{8,12},{9,13},{10,... | collective-permute-start | bytes 294920 | tf_op jit(solution)/shard_map/ppermute | solution.py:423
  49.1 14.6 %collective-permute-start.12 = (bf16[384,128]{1,0:T(8,128)(2,1)S(1)}, bf16[384,128]{1,0:T(8,128)(2,1)S(1)}, u32[]{:S(2)}, u32[]{:S(2)}) collective-permute-start(bf16[384,128]{1,0:T(8,128)(2,1)S(1)} %get-tuple-element.42), channel_id=1, source_target_pairs={{0,5},{1,4},{2,7},{3,6},{4,1},{5,0},{6,3},{7,2},{8,13},{9,12},{10,... | collective-permute-start | bytes 294920 | tf_op jit(solution)/shard_map/ppermute | solution.py:423
  52.9 10.8 %collective-permute-start.13 = (bf16[384,128]{1,0:T(8,128)(2,1)S(1)}, bf16[384,128]{1,0:T(8,128)(2,1)S(1)}, u32[]{:S(2)}, u32[]{:S(2)}) collective-permute-start(bf16[384,128]{1,0:T(8,128)(2,1)S(1)} %get-tuple-element.43), channel_id=1, source_target_pairs={{0,6},{1,7},{2,4},{3,5},{4,2},{5,3},{6,0},{7,1},{8,14},{9,15},{10,... | collective-permute-start | bytes 294920 | tf_op jit(solution)/shard_map/ppermute | solution.py:423
  54.9 8.8 %collective-permute-start.14 = (bf16[384,128]{1,0:T(8,128)(2,1)S(1)}, bf16[384,128]{1,0:T(8,128)(2,1)S(1)}, u32[]{:S(2)}, u32[]{:S(2)}) collective-permute-start(bf16[384,128]{1,0:T(8,128)(2,1)S(1)} %get-tuple-element.44), channel_id=1, source_target_pairs={{0,7},{1,6},{2,5},{3,4},{4,3},{5,2},{6,1},{7,0},{8,15},{9,14},{10,... | collective-permute-start | bytes 294920 | tf_op jit(solution)/shard_map/ppermute | solution.py:423
  58.7 6.1 %collective-permute-start.10 = (bf16[384,128]{1,0:T(8,128)(2,1)S(1)}, bf16[384,128]{1,0:T(8,128)(2,1)S(1)}, u32[]{:S(2)}, u32[]{:S(2)}) collective-permute-start(bf16[384,128]{1,0:T(8,128)(2,1)S(1)} %get-tuple-element.40), channel_id=1, source_target_pairs={{0,3},{1,2},{2,1},{3,0},{4,7},{5,6},{6,5},{7,4},{8,11},{9,10},{10,... | collective-permute-start | bytes 294920 | tf_op jit(solution)/shard_map/ppermute | solution.py:423
  60.5 5.3 %collective-permute-start.8 = (bf16[384,128]{1,0:T(8,128)(2,1)S(1)}, bf16[384,128]{1,0:T(8,128)(2,1)S(1)}, u32[]{:S(2)}, u32[]{:S(2)}) collective-permute-start(bf16[384,128]{1,0:T(8,128)(2,1)S(1)} %get-tuple-element.38), channel_id=1, source_target_pairs={{0,1},{1,0},{2,3},{3,2},{4,5},{5,4},{6,7},{7,6},{8,9},{9,8},{10,11... | collective-permute-start | bytes 294920 | tf_op jit(solution)/shard_map/ppermute | solution.py:423
  63.7 4.6 %collective-permute-start.9 = (bf16[384,128]{1,0:T(8,128)(2,1)S(1)}, bf16[384,128]{1,0:T(8,128)(2,1)S(1)}, u32[]{:S(2)}, u32[]{:S(2)}) collective-permute-start(bf16[384,128]{1,0:T(8,128)(2,1)S(1)} %get-tuple-element.39), channel_id=1, source_target_pairs={{0,2},{1,3},{2,0},{3,1},{4,6},{5,7},{6,4},{7,5},{8,10},{9,11},{10,... | collective-permute-start | bytes 294920 | tf_op jit(solution)/shard_map/ppermute | solution.py:423
  71.6 1.3 %collective-permute-start.15 = (f32[128,128]{1,0:T(8,128)S(1)}, f32[128,128]{1,0:T(8,128)S(1)}, u32[]{:S(2)}, u32[]{:S(2)}) collective-permute-start(f32[128,128]{1,0:T(8,128)S(1)} %get-tuple-element.46), channel_id=1, source_target_pairs={{0,8},{1,9},{2,10},{3,11},{4,12},{5,13},{6,14},{7,15},{8,0},{9,1},... | collective-permute-start | bytes 196616 | tf_op jit(solution)/shard_map/ppermute | solution.py:402
  73.0 4.3 %collective-permute-start.16 = (f32[128,128]{1,0:T(8,128)S(1)}, f32[128,128]{1,0:T(8,128)S(1)}, u32[]{:S(2)}, u32[]{:S(2)}) collective-permute-start(f32[128,128]{1,0:T(8,128)S(1)} %add.21), channel_id=1, source_target_pairs={{0,1},{1,0},{2,3},{3,2},{4,5},{5,4},{6,7},{7,6},{8,9},{9,8},{10,11... | collective-permute-start | bytes 196616 | tf_op jit(solution)/shard_map/ppermute | solution.py:402
  74.3 4.3 %collective-permute-start.17 = (f32[128,128]{1,0:T(8,128)S(1)}, f32[128,128]{1,0:T(8,128)S(1)}, u32[]{:S(2)}, u32[]{:S(2)}) collective-permute-start(f32[128,128]{1,0:T(8,128)S(1)} %add.21), channel_id=1, source_target_pairs={{0,16},{1,17},{2,18},{3,19},{4,20},{5,21},{6,22},{7,23},{8,24},{9,... | collective-permute-start | bytes 196616 | tf_op jit(solution)/shard_map/ppermute | solution.py:402
  75.8 5.2 %collective-permute-start.18 = (f32[128,128]{1,0:T(8,128)S(1)}, f32[128,128]{1,0:T(8,128)S(1)}, u32[]{:S(2)}, u32[]{:S(2)}) collective-permute-start(f32[128,128]{1,0:T(8,128)S(1)} %add.21), channel_id=1, source_target_pairs={{0,17},{1,16},{2,19},{3,18},{4,21},{5,20},{6,23},{7,22},{8,25},{9,... | collective-permute-start | bytes 196616 | tf_op jit(solution)/shard_map/ppermute | solution.py:402
  81.0 6.5 %collective-permute-start.19 = (f32[128,128]{1,0:T(8,128)S(1)}, f32[128,128]{1,0:T(8,128)S(1)}, u32[]{:S(2)}, u32[]{:S(2)}) collective-permute-start(f32[128,128]{1,0:T(8,128)S(1)} %add_add_fusion.1), channel_id=1, source_target_pairs={{0,2},{1,3},{2,0},{3,1},{4,6},{5,7},{6,4},{7,5},{8,10},{9,11},{10,... | collective-permute-start | bytes 196616 | tf_op jit(solution)/shard_map/ppermute | solution.py:402
  81.1 6.4 %collective-permute-start.20 = (f32[128,128]{1,0:T(8,128)S(1)}, f32[128,128]{1,0:T(8,128)S(1)}, u32[]{:S(2)}, u32[]{:S(2)}) collective-permute-start(f32[128,128]{1,0:T(8,128)S(1)} %add_add_fusion.1), channel_id=1, source_target_pairs={{0,4},{1,5},{2,6},{3,7},{4,0},{5,1},{6,2},{7,3},{8,12},{9,13},{10,... | collective-permute-start | bytes 196616 | tf_op jit(solution)/shard_map/ppermute | solution.py:402
  83.2 6.1 %collective-permute-start.21 = (f32[128,128]{1,0:T(8,128)S(1)}, f32[128,128]{1,0:T(8,128)S(1)}, u32[]{:S(2)}, u32[]{:S(2)}) collective-permute-start(f32[128,128]{1,0:T(8,128)S(1)} %add_add_fusion.1), channel_id=1, source_target_pairs={{0,6},{1,7},{2,4},{3,5},{4,2},{5,3},{6,0},{7,1},{8,14},{9,15},{10,... | collective-permute-start | bytes 196616 | tf_op jit(solution)/shard_map/ppermute | solution.py:402

commit v5 on v4

--- a/solution.py
+++ b/solution.py
@@ -16,6 +16,8 @@
 MIB = 2**20
 IMAGE_STEP = 1024
 PART_STEP = 768
+LATE = 2
+PACK_SPARE = 8
 BASIS_SLOTS = 2 * CAP
 SMEM = pl.BlockSpec(memory_space=pltpu.SMEM)
 VMEM = pl.BlockSpec(memory_space=pltpu.VMEM)
@@ -213,7 +215,7 @@
         hand_out(part, part_refs[first : first + each])
 
 
-def far_kernel(holders, kept, *refs):
+def far_kernel(holders, late, kept, *refs):
     dense_ref, ready, refs = half_of(1, kept, refs)
     sum_ref, *refs = refs
     sketch_refs, (token_ref, images_ref) = refs[:holders], refs[holders : holders + 2]
@@ -232,7 +234,8 @@
     parts(images_ref, dense_ref, part_refs)
 
 
-def rest_kernel(kept, *refs):
+def rest_kernel(late, kept, *refs):
+    all_ref = refs[0]
     dense_ref, ready, refs = half_of(0, kept, refs)
     images_ref, _, *part_refs = refs
 
@@ -240,7 +243,10 @@
     def _(chunk):
         ready(chunk)
 
-    parts(images_ref, dense_ref, part_refs)
+    parts(images_ref, dense_ref, part_refs[: len(part_refs) - late])
+    if late:
+        first = all_ref.shape[1] - late * part_refs[0].shape[0]
+        parts(images_ref, all_ref.at[:, first:], part_refs[len(part_refs) - late :])
 
 
 def zero_kernel(out_ref, zeros_ref, sem):
@@ -260,7 +266,7 @@
 
 
 def gather_kernel(me_ref, asked_ref, *refs):
-    arrived_refs, (split_ref, gram_ref, block_ref, normal_ref, seen_ref) = refs[:-5], refs[-5:]
+    arrived_refs, (split_ref, pack_ref, block_ref, normal_ref, gram_ref, seen_ref) = refs[:-6], refs[-6:]
     slots, tile_size, width = normal_ref.shape
 
     @pl.loop(0, seen_ref.shape[0])
@@ -302,6 +308,31 @@
         both = lax.dot_general(high, both_rows, (((0,), (0,)), ((), ())), preferred_element_type=jnp.float32)
         cross = both[:, width:]
         gram_ref[...] += both[:, :width] + cross + cross.T
+
+    pack_ref[...] = packed(gram_ref[...])
+
+
+def packed(gram):
+    half = gram.shape[0] // 2
+    top, bottom = gram[:half], pltpu.roll(gram[half:], half, 1)
+    row = lax.broadcasted_iota(jnp.int32, top.shape, 0)
+    col = lax.broadcasted_iota(jnp.int32, top.shape, 1)
+    diagonal = jnp.sum(jnp.where(col == row, bottom, 0.0), axis=0, keepdims=True)
+    last = jnp.broadcast_to(diagonal, (PACK_SPARE, gram.shape[1]))
+    return jnp.concatenate([jnp.where(col >= row, top, bottom), last], axis=0)
+
+
+def unpacked(pack):
+    half = pack.shape[0] - PACK_SPARE
+    top, diagonal = pack[:half], pack[half : half + 1]
+    row = lax.broadcasted_iota(jnp.int32, top.shape, 0)
+    col = lax.broadcasted_iota(jnp.int32, top.shape, 1)
+    low = jnp.where(col < row, top, jnp.where(col == row, diagonal, 0.0))
+    turned = jnp.concatenate([low, jnp.zeros_like(low)], axis=0).T[:half]
+    upper = jnp.concatenate([jnp.where(col >= row, top, 0.0), pltpu.roll(turned, half, 1)], axis=0)
+    row = lax.broadcasted_iota(jnp.int32, upper.shape, 0)
+    col = lax.broadcasted_iota(jnp.int32, upper.shape, 1)
+    return upper + jnp.where(col > row, upper, 0.0).T
 
 
 def spread(value, like):
@@ -353,16 +384,17 @@
     return terms[0]
 
 
-def finish_kernel(voxels, block_ref, gram_ref, normal_ref, zeroed_ref, basis_ref, factor_ref, work_ref, out_ref, sem):
-    width = gram_ref.shape[0]
+def finish_kernel(voxels, block_ref, pack_ref, normal_ref, zeroed_ref, basis_ref, factor_ref, work_ref, out_ref, sem):
+    width = factor_ref.shape[0]
     slots, tile_size, _ = out_ref.shape
     panel = 8
     row_at = lax.broadcasted_iota(jnp.int32, (panel, width), 0)
     lane = lax.broadcasted_iota(jnp.int32, (panel, width), 1)
+    whole = unpacked(pack_ref[...])
     gram = []
     for start in range(0, width, panel):
         shift = jnp.where(lane == row_at + start, gram_shift, 0.0)
-        gram.append(gram_ref[pl.ds(start, panel), :] / voxels + shift)
+        gram.append(whole[start : start + panel] / voxels + shift)
     for i, rows in enumerate(factor(gram, work_ref)):
         factor_ref[pl.ds(panel * i, panel), :] = rows
     inverse = work_ref[...].T
@@ -503,6 +535,7 @@
             name=name,
         )(*tile_operands, *operands)
 
+    late = LATE if kept else 0
     flops = 2 * rows * half * tall * width
     stacked = [pltpu.VMEM((half * tall, width), sketch.dtype), pltpu.SemaphoreType.DMA]
     (begun,) = with_tiles(
@@ -515,12 +548,12 @@
         flops,
     )
     token, images, *far_parts = with_tiles(
-        functools.partial(far_kernel, half),
+        functools.partial(far_kernel, half, late),
         [
             jax.ShapeDtypeStruct((8, width), jnp.float32),
             jax.ShapeDtypeStruct((width, rows), jnp.bfloat16),
         ]
-        + [jax.ShapeDtypeStruct((tall, width), jnp.bfloat16)] * half,
+        + [jax.ShapeDtypeStruct((tall, width), jnp.bfloat16)] * (half - late),
         [VMEM] + [ANY] * half,
         [begun] + replies[half:],
         stacked,
@@ -529,16 +562,17 @@
     )
     far_arrived = exchanged(far_parts, half)
     own_part, *near_parts = with_tiles(
-        rest_kernel,
+        functools.partial(rest_kernel, late),
         [jax.ShapeDtypeStruct((tall, width), jnp.float32)]
-        + [jax.ShapeDtypeStruct((tall, width), jnp.bfloat16)] * (half - 1),
+        + [jax.ShapeDtypeStruct((tall, width), jnp.bfloat16)] * (half - 1 + late),
         [VMEM, ANY],
         [images, exchanged([token], 1)[0]],
         [],
         "parts_near",
         flops,
     )
-    arrived = [own_part] + exchanged(near_parts, 1) + far_arrived
+    far_arrived += exchanged(near_parts[half - 1 :], group_size - late)
+    arrived = [own_part] + exchanged(near_parts[: half - 1], 1) + far_arrived
 
     zeroed = pl.pallas_call(
         zero_kernel,
@@ -552,13 +586,14 @@
         gather_kernel,
         out_shape=(
             in_vmem((slots * tile_size, 2 * width), jnp.bfloat16),
-            jax.ShapeDtypeStruct((width, width), jnp.float32),
+            jax.ShapeDtypeStruct((width // 2 + PACK_SPARE, width), jnp.float32),
             jax.ShapeDtypeStruct((slots,), jnp.int32),
         ),
         in_specs=[SMEM, SMEM] + [VMEM] * group_size,
         out_specs=(VMEM, VMEM, SMEM),
         scratch_shapes=[
             pltpu.VMEM((slots, tile_size, width), jnp.float32),
+            pltpu.VMEM((width, width), jnp.float32),
             pltpu.SMEM((block_count,), jnp.int32),
         ],
         compiler_params=pltpu.CompilerParams(vmem_limit_bytes=16 * MIB),

time: 97.5 us -> 94.3 us (0.967)
  waiting for transfers between devices: 15.9 us -> 11.6 us
    ppermute x15, waiting for transfers between devices: 8.44 us -> 4.73 us  [exchanged(): lax.ppermute(value, 'dev', [(j, j ^ first + i) for j in range(size)])]
  transfers between devices with their start and end apart: 22 -> 22, of which waited for: 10 -> 8; matrix products, arithmetic and copies ran while one was open for 0% -> 0% of each run, Pallas kernels for 17% -> 19%
where the time goes in v5:
time: 94.3 us; the launch traced here: 93.9 us
  Pallas kernels  38.3 us (41%)
  starting transfers between devices  29.6 us (31%)
  blocking collectives  13.7 us (15%)
  waiting for transfers between devices  11.6 us (12%)
    ppermute x15, starting transfers between devices, exchanged(): lax.ppermute(value, 'dev', [(j, j ^ first + i) for j in range(size)])  21.6 us
    all_to_all x1, blocking collectives, local(): lax.all_to_all(request, 'dev', split_axis=0, concat_axis=0, tiled=True)  13.7 us
    pallas_call x3, Pallas kernels, with_tiles(): pl.pallas_call(functools.partial(kernel, kept), out_shape=outs, in_specs=...  13.1 us
    pallas_call x1, Pallas kernels, local(): pl.pallas_call(load_kernel, out_shape=in_vmem((rows, slots * tile_size),...  8.19 us
    pallas_call x1, Pallas kernels, local(): pl.pallas_call(functools.partial(finish_kernel, voxels), out_shape=(jax.S...  8.08 us
    ppermute x7, starting transfers between devices, other(): lax.ppermute(value, axes, [(i, i ^ bits) for i in range(outer * inner)])  8.01 us
    ppermute x7, waiting for transfers between devices, other(): lax.ppermute(value, axes, [(i, i ^ bits) for i in range(outer * inner)])  6.85 us
    ppermute x15, waiting for transfers between devices, exchanged(): lax.ppermute(value, 'dev', [(j, j ^ first + i) for j in range(size)])  4.73 us
  transfers between devices with their start and end apart: 22, of which 8 were waited for; matrix products, arithmetic and copies ran while one was open for 0% of the time, Pallas kernels for 19%

profile of v5, /device:TPU:0, one launch (start us, length us, event | category | flops | bytes accessed | tf_op | source)
XLA Modules:
  0.0 93.9 jit_solution(5636311911733261400)
XLA Ops:
  0.6 1.9 %plan.1 = (s32[8,3]{1,0:T(8,128)}, s32[24]{0:T(128)}) custom-call(s32[1]{0:T(128)} %bitcast.me_ref, s32[24]{0:T(128)} %touched_ref.1, s32[2048]{0:T(1024)} %home_ref.1), custom_call_target="tpu_custom_call" | custom-call | tf_op jit(solution)/shard_map/plan/pallas_call | solution.py:472
  2.5 13.7 %all_to_all.11 = s32[8,1,3]{2,1,0:T(1,128)S(1)} all-to-all(s32[8,1,3]{2,1,0:T(1,128)} %bitcast.9), channel_id=1, replica_groups=mesh['grp'=4,'dev'=8] {'dev'}, dimensions={0} | all-to-all | bytes 192 | tf_op jit(solution)/shard_map/all_to_all | solution.py:502
  16.2 1.7 %serve.1 = (bf16[3,128,128]{2,1,0:T(8,128)(2,1)S(1)}, bf16[3,128,128]{2,1,0:T(8,128)(2,1)S(1)}, bf16[3,128,128]{2,1,0:T(8,128)(2,1)S(1)}, bf16[3,128,128]{2,1,0:...) custom-call(s32[1]{0:T(128)} %bitcast.me_ref, ...), custom_call_target="tpu_custom_call" | custom-call | tf_op jit(solution)/shard_map/serve/pallas_call | solution.py:503
  17.9 0.6 collective-permute-start
  18.5 0.6 collective-permute-start.1
  19.1 2.4 %collective-permute-start.2 = (bf16[3,128,128]{2,1,0:T(8,128)(2,1)S(1)}, bf16[3,128,128]{2,1,0:T(8,128)(2,1)S(1)}, u32[]{:S(2)}, u32[]{:S(2)}) collective-permute-start(bf16[3,128,128]{2,1,0:T(8,128)(2,1)S(1)} %get-tuple-element.30), channel_id=1, source_target_pairs={{0,3},{1,2},{2,1},{3,0},{4,7},{5,6},{6,5},{7,4},{8,11},{9,10},{10,... | collective-permute-start | bytes 294920 | tf_op jit(solution)/shard_map/ppermute | solution.py:455
  21.5 0.6 collective-permute-start.3
  22.0 2.4 %collective-permute-start.4 = (bf16[3,128,128]{2,1,0:T(8,128)(2,1)S(1)}, bf16[3,128,128]{2,1,0:T(8,128)(2,1)S(1)}, u32[]{:S(2)}, u32[]{:S(2)}) collective-permute-start(bf16[3,128,128]{2,1,0:T(8,128)(2,1)S(1)} %get-tuple-element.32), channel_id=1, source_target_pairs={{0,5},{1,4},{2,7},{3,6},{4,1},{5,0},{6,3},{7,2},{8,13},{9,12},{10,... | collective-permute-start | bytes 294920 | tf_op jit(solution)/shard_map/ppermute | solution.py:455
  24.4 8.2 %load.1.refs_0_ = bf16[4096,3072]{1,0:T(8,128)(2,1)S(1)} custom-call(s32[512]{0:T(512)} %ray_ref.1, s32[512]{0:T(512)} %col_ref.1, s32[24]{0:T(128)} %get-tuple-element.26.place_ref, bf16[512,128,128]{2,1,0:T(8,128)(2,1)} %tiles_ref.1, bf16[3,128,128]{2,1,0:T(8,128)(2,1)S(1)} %get-tuple-element.27._.refs_1_), custom_call_target="tpu_custom_call" | custom-call | tf_op jit(solution)/shard_map/load/pallas_call | solution.py:515
  32.6 0.0 collective-permute-done.refs_2_
  32.6 0.7 collective-permute-start.5
  33.2 0.0 collective-permute-done.1.refs_3_
  33.2 4.1 %collective-permute-start.6 = (bf16[3,128,128]{2,1,0:T(8,128)(2,1)S(1)}, bf16[3,128,128]{2,1,0:T(8,128)(2,1)S(1)}, u32[]{:S(2)}, u32[]{:S(2)}) collective-permute-start(bf16[3,128,128]{2,1,0:T(8,128)(2,1)S(1)} %get-tuple-element.34), channel_id=1, source_target_pairs={{0,7},{1,6},{2,5},{3,4},{4,3},{5,2},{6,1},{7,0},{8,15},{9,14},{10,... | collective-permute-start | bytes 294920 | tf_op jit(solution)/shard_map/ppermute | solution.py:455
  37.4 4.4 %images_near.1.refs_1_ = f32[4096,128]{1,0:T(8,128)S(1)} custom-call(bf16[4096,3072]{1,0:T(8,128)(2,1)S(1)} %load.1.refs_0_, bf16[3,128,128]{2,1,0:T(8,128)(2,1)S(1)} %get-tuple-element.27._.refs_1_, bf16[3,128,128]{2,1,0:T(8,128)(2,1)S(1)} %collective-permute-done.refs_2_, bf16[3,128,128]{2,1,0:T(8,128)(2,1)S(1)} %collective-permute-done.1.refs_3_, ...), custom_call_target="tpu_custom_call" | custom-call | flops 1610612736 | bytes 8388608 | tf_op jit(solution)/shard_map/images_near/pallas_call | solution.py:527
  41.8 0.0 collective-permute-done.3.refs_2_
  41.8 0.0 collective-permute-done.4.refs_3_
  41.8 0.0 collective-permute-done.6.refs_5_
  41.8 5.8 %images_far.1 = (f32[8,128]{1,0:T(8,128)S(1)}, bf16[128,4096]{1,0:T(8,128)(2,1)S(1)}, bf16[384,128]{1,0:T(8,128)(2,1)S(1)}, bf16[384,128]{1,0:T(8,128)(2,1)S(1)}) custom-call(bf16[4096,3072]{1,0:T(8,128)(2,1)S(1)} %load.1.refs_0_, f32[4096,128]{1,0:T(8,128)S(1)} %images_near.1.refs_1_, bf16[3,128,128]{2,1,0:T(8,128)(2,1)S(1)} %collective-permute-done.3.refs_2_, ...), custom_call_target="tpu_custom_call" | custom-call | flops 3221225472 | bytes 8388608 | tf_op jit(solution)/shard_map/images_far/pallas_call | solution.py:527
  47.7 0.6 collective-permute-start.7
  48.3 0.0 collective-permute-start.11
  48.3 3.8 %collective-permute-start.12 = (bf16[384,128]{1,0:T(8,128)(2,1)S(1)}, bf16[384,128]{1,0:T(8,128)(2,1)S(1)}, u32[]{:S(2)}, u32[]{:S(2)}) collective-permute-start(bf16[384,128]{1,0:T(8,128)(2,1)S(1)} %get-tuple-element.42), channel_id=1, source_target_pairs={{0,5},{1,4},{2,7},{3,6},{4,1},{5,0},{6,3},{7,2},{8,13},{9,12},{10,... | collective-permute-start | bytes 294920 | tf_op jit(solution)/shard_map/ppermute | solution.py:455
  52.1 2.9 %parts_near.1 = (f32[384,128]{1,0:T(8,128)S(1)}, bf16[384,128]{1,0:T(8,128)(2,1)S(1)}, bf16[384,128]{1,0:T(8,128)(2,1)S(1)}, bf16[384,128]{1,0:T(8,128)(2,1)S(1)...) custom-call(bf16[4096,3072]{1,0:T(8,128)(2,1)S(1)} %load.1.refs_0_, ...), custom_call_target="tpu_custom_call" | custom-call | flops 1610612736 | bytes 8388608 | tf_op jit(solution)/shard_map/parts_near/pallas_call | solution.py:527
  55.0 0.5 collective-permute-start.10
  55.5 1.5 %collective-permute-start.13 = (bf16[384,128]{1,0:T(8,128)(2,1)S(1)}, bf16[384,128]{1,0:T(8,128)(2,1)S(1)}, u32[]{:S(2)}, u32[]{:S(2)}) collective-permute-start(bf16[384,128]{1,0:T(8,128)(2,1)S(1)} %get-tuple-element.43), channel_id=1, source_target_pairs={{0,6},{1,7},{2,4},{3,5},{4,2},{5,3},{6,0},{7,1},{8,14},{9,15},{10,... | collective-permute-start | bytes 294920 | tf_op jit(solution)/shard_map/ppermute | solution.py:455
  57.1 3.0 %collective-permute-start.14 = (bf16[384,128]{1,0:T(8,128)(2,1)S(1)}, bf16[384,128]{1,0:T(8,128)(2,1)S(1)}, u32[]{:S(2)}, u32[]{:S(2)}) collective-permute-start(bf16[384,128]{1,0:T(8,128)(2,1)S(1)} %get-tuple-element.44), channel_id=1, source_target_pairs={{0,7},{1,6},{2,5},{3,4},{4,3},{5,2},{6,1},{7,0},{8,15},{9,14},{10,... | collective-permute-start | bytes 294920 | tf_op jit(solution)/shard_map/ppermute | solution.py:455
  60.1 0.8 collective-permute-start.8
  60.8 0.0 collective-permute-done.12.refs_5_
  60.8 2.2 %collective-permute-done.10.refs_3_ = bf16[384,128]{1,0:T(8,128)(2,1)S(1)} collective-permute-done((bf16[384,128]{1,0:T(8,128)(2,1)S(1)}, bf16[384,128]{1,0:T(8,128)(2,1)S(1)}, u32[]{:S(2)}, u32[]{:S(2)}) %collective-permute-start.10) | collective-permute-done | bytes 98336 | tf_op jit(solution)/shard_map/ppermute | solution.py:455
  63.1 0.0 collective-permute-done.13.refs_6_
  63.1 1.5 %collective-permute-done.14.refs_7_ = bf16[384,128]{1,0:T(8,128)(2,1)S(1)} collective-permute-done((bf16[384,128]{1,0:T(8,128)(2,1)S(1)}, bf16[384,128]{1,0:T(8,128)(2,1)S(1)}, u32[]{:S(2)}, u32[]{:S(2)}) %collective-permute-start.14) | collective-permute-done | bytes 98336 | tf_op jit(solution)/shard_map/ppermute | solution.py:455
  64.6 1.0 %collective-permute-done.8.refs_1_ = bf16[384,128]{1,0:T(8,128)(2,1)S(1)} collective-permute-done((bf16[384,128]{1,0:T(8,128)(2,1)S(1)}, bf16[384,128]{1,0:T(8,128)(2,1)S(1)}, u32[]{:S(2)}, u32[]{:S(2)}) %collective-permute-start.8) | collective-permute-done | bytes 98336 | tf_op jit(solution)/shard_map/ppermute | solution.py:455
  65.5 0.0 collective-permute-done.9.refs_2_
  65.5 3.3 %collect.1 = (bf16[3072,256]{1,0:T(8,128)(2,1)S(1)}, f32[72,128]{1,0:T(8,128)S(1)}, s32[24]{0:T(128)S(1)}) custom-call(s32[1]{0:T(128)} %bitcast.me_ref, s32[8,3]{1,0:T(8,128)S(1)} %bitcast.7, f32[384,128]{1,0:T(8,128)S(1)} %get-tuple-element.37.refs_0_, bf16[384,128]{1,0:T(8,128)(2,1)S(1)} %collective-permute-done.8.refs_1_, ...), custom_call_target="tpu_custom_call" | custom-call | tf_op jit(solution)/shard_map/collect/pallas_call | solution.py:585
  68.9 0.1 collective-permute-start.15
  69.0 1.2 %collective-permute-done.15 = f32[72,128]{1,0:T(8,128)S(1)} collective-permute-done((f32[72,128]{1,0:T(8,128)S(1)}, f32[72,128]{1,0:T(8,128)S(1)}, u32[]{:S(2)}, u32[]{:S(2)}) %collective-permute-start.15) | collective-permute-done | bytes 36896 | tf_op jit(solution)/shard_map/ppermute | solution.py:434
  70.2 1.2 %collective-permute-start.16 = (f32[72,128]{1,0:T(8,128)S(1)}, f32[72,128]{1,0:T(8,128)S(1)}, u32[]{:S(2)}, u32[]{:S(2)}) collective-permute-start(f32[72,128]{1,0:T(8,128)S(1)} %add.21), channel_id=1, source_target_pairs={{0,1},{1,0},{2,3},{3,2},{4,5},{5,4},{6,7},{7,6},{8,9},{9,8},{10,11... | collective-permute-start | bytes 110600 | tf_op jit(solution)/shard_map/ppermute | solution.py:434
  71.3 1.5 %collective-permute-start.17 = (f32[72,128]{1,0:T(8,128)S(1)}, f32[72,128]{1,0:T(8,128)S(1)}, u32[]{:S(2)}, u32[]{:S(2)}) collective-permute-start(f32[72,128]{1,0:T(8,128)S(1)} %add.21), channel_id=1, source_target_pairs={{0,16},{1,17},{2,18},{3,19},{4,20},{5,21},{6,22},{7,23},{8,24},{9,... | collective-permute-start | bytes 110600 | tf_op jit(solution)/shard_map/ppermute | solution.py:434
  72.8 0.8 collective-permute-start.18
  73.7 0.5 collective-permute-done.16
  74.1 1.2 %collective-permute-done.17 = f32[72,128]{1,0:T(8,128)S(1)} collective-permute-done((f32[72,128]{1,0:T(8,128)S(1)}, f32[72,128]{1,0:T(8,128)S(1)}, u32[]{:S(2)}, u32[]{:S(2)}) %collective-permute-start.17) | collective-permute-done | bytes 36896 | tf_op jit(solution)/shard_map/ppermute | solution.py:434
  75.3 2.4 %collective-permute-done.18 = f32[72,128]{1,0:T(8,128)S(1)} collective-permute-done((f32[72,128]{1,0:T(8,128)S(1)}, f32[72,128]{1,0:T(8,128)S(1)}, u32[]{:S(2)}, u32[]{:S(2)}) %collective-permute-start.18) | collective-permute-done | bytes 36896 | tf_op jit(solution)/shard_map/ppermute | solution.py:434
  77.7 0.7 collective-permute-start.19
  78.4 1.7 %collective-permute-start.20 = (f32[72,128]{1,0:T(8,128)S(1)}, f32[72,128]{1,0:T(8,128)S(1)}, u32[]{:S(2)}, u32[]{:S(2)}) collective-permute-start(f32[72,128]{1,0:T(8,128)S(1)} %add_add_fusion.1), channel_id=1, source_target_pairs={{0,4},{1,5},{2,6},{3,7},{4,0},{5,1},{6,2},{7,3},{8,12},{9,13},{10,... | collective-permute-start | bytes 110600 | tf_op jit(solution)/shard_map/ppermute | solution.py:434
  80.1 2.1 %collective-permute-start.21 = (f32[72,128]{1,0:T(8,128)S(1)}, f32[72,128]{1,0:T(8,128)S(1)}, u32[]{:S(2)}, u32[]{:S(2)}) collective-permute-start(f32[72,128]{1,0:T(8,128)S(1)} %add_add_fusion.1), channel_id=1, source_target_pairs={{0,6},{1,7},{2,4},{3,5},{4,2},{5,3},{6,0},{7,1},{8,14},{9,15},{10,... | collective-permute-start | bytes 110600 | tf_op jit(solution)/shard_map/ppermute | solution.py:434
  82.2 2.0 %zeros.1.zeroed_ref = f32[8192,128]{1,0:T(8,128)} custom-call(), custom_call_target="tpu_custom_call" | custom-call | tf_op jit(solution)/shard_map/zeros/pallas_call | solution.py:577
  84.2 0.0 collective-permute-done.20
  84.2 1.6 %collective-permute-done.21 = f32[72,128]{1,0:T(8,128)S(1)} collective-permute-done((f32[72,128]{1,0:T(8,128)S(1)}, f32[72,128]{1,0:T(8,128)S(1)}, u32[]{:S(2)}, u32[]{:S(2)}) %collective-permute-start.21) | collective-permute-done | bytes 36896 | tf_op jit(solution)/shard_map/ppermute | solution.py:434
  85.9 8.1 %finish.1 = (f32[8192,128]{1,0:T(8,128)}, f32[128,128]{1,0:T(8,128)}) custom-call(s32[24]{0:T(128)S(1)} %get-tuple-element.45.block_ref, f32[72,128]{1,0:T(8,128)S(1)} %add_add_fusion.pack_ref, bf16[3072,256]{1,0:T(8,128)(2,1)S(1)} %get-tuple-element.47.normal_ref, f32[8192,128]{1,0:T(8,128)} %zeros.1.zeroed_ref), custom_call_target="tpu_custom_call", output_to_operand_aliasing={{0}: (3, {})} | custom-call | tf_op jit(solution)/shard_map/finish/pallas_call | solution.py:603
  (9 shorter events, 0.0 us)
Async XLA Ops:
  17.9 14.7 %collective-permute-start = (bf16[3,128,128]{2,1,0:T(8,128)(2,1)S(1)}, bf16[3,128,128]{2,1,0:T(8,128)(2,1)S(1)}, u32[]{:S(2)}, u32[]{:S(2)}) collective-permute-start(bf16[3,128,128]{2,1,0:T(8,128)(2,1)S(1)} %get-tuple-element.28), channel_id=1, source_target_pairs={{0,1},{1,0},{2,3},{3,2},{4,5},{5,4},{6,7},{7,6},{8,9},{9,8},{10,11... | collective-permute-start | bytes 294920 | tf_op jit(solution)/shard_map/ppermute | solution.py:455
  18.5 14.7 %collective-permute-start.1 = (bf16[3,128,128]{2,1,0:T(8,128)(2,1)S(1)}, bf16[3,128,128]{2,1,0:T(8,128)(2,1)S(1)}, u32[]{:S(2)}, u32[]{:S(2)}) collective-permute-start(bf16[3,128,128]{2,1,0:T(8,128)(2,1)S(1)} %get-tuple-element.29), channel_id=1, source_target_pairs={{0,2},{1,3},{2,0},{3,1},{4,6},{5,7},{6,4},{7,5},{8,10},{9,11},{10,... | collective-permute-start | bytes 294920 | tf_op jit(solution)/shard_map/ppermute | solution.py:455
  19.1 18.3 %collective-permute-start.2 = (bf16[3,128,128]{2,1,0:T(8,128)(2,1)S(1)}, bf16[3,128,128]{2,1,0:T(8,128)(2,1)S(1)}, u32[]{:S(2)}, u32[]{:S(2)}) collective-permute-start(bf16[3,128,128]{2,1,0:T(8,128)(2,1)S(1)} %get-tuple-element.30), channel_id=1, source_target_pairs={{0,3},{1,2},{2,1},{3,0},{4,7},{5,6},{6,5},{7,4},{8,11},{9,10},{10,... | collective-permute-start | bytes 294920 | tf_op jit(solution)/shard_map/ppermute | solution.py:455
  21.5 20.3 %collective-permute-start.3 = (bf16[3,128,128]{2,1,0:T(8,128)(2,1)S(1)}, bf16[3,128,128]{2,1,0:T(8,128)(2,1)S(1)}, u32[]{:S(2)}, u32[]{:S(2)}) collective-permute-start(bf16[3,128,128]{2,1,0:T(8,128)(2,1)S(1)} %get-tuple-element.31), channel_id=1, source_target_pairs={{0,4},{1,5},{2,6},{3,7},{4,0},{5,1},{6,2},{7,3},{8,12},{9,13},{10,... | collective-permute-start | bytes 294920 | tf_op jit(solution)/shard_map/ppermute | solution.py:455
  22.0 19.8 %collective-permute-start.4 = (bf16[3,128,128]{2,1,0:T(8,128)(2,1)S(1)}, bf16[3,128,128]{2,1,0:T(8,128)(2,1)S(1)}, u32[]{:S(2)}, u32[]{:S(2)}) collective-permute-start(bf16[3,128,128]{2,1,0:T(8,128)(2,1)S(1)} %get-tuple-element.32), channel_id=1, source_target_pairs={{0,5},{1,4},{2,7},{3,6},{4,1},{5,0},{6,3},{7,2},{8,13},{9,12},{10,... | collective-permute-start | bytes 294920 | tf_op jit(solution)/shard_map/ppermute | solution.py:455
  32.6 9.2 %collective-permute-start.5 = (bf16[3,128,128]{2,1,0:T(8,128)(2,1)S(1)}, bf16[3,128,128]{2,1,0:T(8,128)(2,1)S(1)}, u32[]{:S(2)}, u32[]{:S(2)}) collective-permute-start(bf16[3,128,128]{2,1,0:T(8,128)(2,1)S(1)} %get-tuple-element.33), channel_id=1, source_target_pairs={{0,6},{1,7},{2,4},{3,5},{4,2},{5,3},{6,0},{7,1},{8,14},{9,15},{10,... | collective-permute-start | bytes 294920 | tf_op jit(solution)/shard_map/ppermute | solution.py:455
  33.2 8.6 %collective-permute-start.6 = (bf16[3,128,128]{2,1,0:T(8,128)(2,1)S(1)}, bf16[3,128,128]{2,1,0:T(8,128)(2,1)S(1)}, u32[]{:S(2)}, u32[]{:S(2)}) collective-permute-start(bf16[3,128,128]{2,1,0:T(8,128)(2,1)S(1)} %get-tuple-element.34), channel_id=1, source_target_pairs={{0,7},{1,6},{2,5},{3,4},{4,3},{5,2},{6,1},{7,0},{8,15},{9,14},{10,... | collective-permute-start | bytes 294920 | tf_op jit(solution)/shard_map/ppermute | solution.py:455
  47.7 4.5 %collective-permute-start.7 = (f32[8,128]{1,0:T(8,128)S(1)}, f32[8,128]{1,0:T(8,128)S(1)}, u32[]{:S(2)}, u32[]{:S(2)}) collective-permute-start(f32[8,128]{1,0:T(8,128)S(1)} %get-tuple-element.36), channel_id=1, source_target_pairs={{0,1},{1,0},{2,3},{3,2},{4,5},{5,4},{6,7},{7,6},{8,9},{9,8},{10,11... | collective-permute-start | bytes 12296 | tf_op jit(solution)/shard_map/ppermute | solution.py:455
  48.3 11.8 %collective-permute-start.11 = (bf16[384,128]{1,0:T(8,128)(2,1)S(1)}, bf16[384,128]{1,0:T(8,128)(2,1)S(1)}, u32[]{:S(2)}, u32[]{:S(2)}) collective-permute-start(bf16[384,128]{1,0:T(8,128)(2,1)S(1)} %get-tuple-element.41), channel_id=1, source_target_pairs={{0,4},{1,5},{2,6},{3,7},{4,0},{5,1},{6,2},{7,3},{8,12},{9,13},{10,... | collective-permute-start | bytes 294920 | tf_op jit(solution)/shard_map/ppermute | solution.py:455
  48.3 12.5 %collective-permute-start.12 = (bf16[384,128]{1,0:T(8,128)(2,1)S(1)}, bf16[384,128]{1,0:T(8,128)(2,1)S(1)}, u32[]{:S(2)}, u32[]{:S(2)}) collective-permute-start(bf16[384,128]{1,0:T(8,128)(2,1)S(1)} %get-tuple-element.42), channel_id=1, source_target_pairs={{0,5},{1,4},{2,7},{3,6},{4,1},{5,0},{6,3},{7,2},{8,13},{9,12},{10,... | collective-permute-start | bytes 294920 | tf_op jit(solution)/shard_map/ppermute | solution.py:455
  55.0 8.1 %collective-permute-start.10 = (bf16[384,128]{1,0:T(8,128)(2,1)S(1)}, bf16[384,128]{1,0:T(8,128)(2,1)S(1)}, u32[]{:S(2)}, u32[]{:S(2)}) collective-permute-start(bf16[384,128]{1,0:T(8,128)(2,1)S(1)} %get-tuple-element.40), channel_id=1, source_target_pairs={{0,3},{1,2},{2,1},{3,0},{4,7},{5,6},{6,5},{7,4},{8,11},{9,10},{10,... | collective-permute-start | bytes 294920 | tf_op jit(solution)/shard_map/ppermute | solution.py:455
  55.5 7.5 %collective-permute-start.13 = (bf16[384,128]{1,0:T(8,128)(2,1)S(1)}, bf16[384,128]{1,0:T(8,128)(2,1)S(1)}, u32[]{:S(2)}, u32[]{:S(2)}) collective-permute-start(bf16[384,128]{1,0:T(8,128)(2,1)S(1)} %get-tuple-element.43), channel_id=1, source_target_pairs={{0,6},{1,7},{2,4},{3,5},{4,2},{5,3},{6,0},{7,1},{8,14},{9,15},{10,... | collective-permute-start | bytes 294920 | tf_op jit(solution)/shard_map/ppermute | solution.py:455
  57.1 7.5 %collective-permute-start.14 = (bf16[384,128]{1,0:T(8,128)(2,1)S(1)}, bf16[384,128]{1,0:T(8,128)(2,1)S(1)}, u32[]{:S(2)}, u32[]{:S(2)}) collective-permute-start(bf16[384,128]{1,0:T(8,128)(2,1)S(1)} %get-tuple-element.44), channel_id=1, source_target_pairs={{0,7},{1,6},{2,5},{3,4},{4,3},{5,2},{6,1},{7,0},{8,15},{9,14},{10,... | collective-permute-start | bytes 294920 | tf_op jit(solution)/shard_map/ppermute | solution.py:455
  60.1 5.5 %collective-permute-start.8 = (bf16[384,128]{1,0:T(8,128)(2,1)S(1)}, bf16[384,128]{1,0:T(8,128)(2,1)S(1)}, u32[]{:S(2)}, u32[]{:S(2)}) collective-permute-start(bf16[384,128]{1,0:T(8,128)(2,1)S(1)} %get-tuple-element.38), channel_id=1, source_target_pairs={{0,1},{1,0},{2,3},{3,2},{4,5},{5,4},{6,7},{7,6},{8,9},{9,8},{10,11... | collective-permute-start | bytes 294920 | tf_op jit(solution)/shard_map/ppermute | solution.py:455
  60.8 4.7 %collective-permute-start.9 = (bf16[384,128]{1,0:T(8,128)(2,1)S(1)}, bf16[384,128]{1,0:T(8,128)(2,1)S(1)}, u32[]{:S(2)}, u32[]{:S(2)}) collective-permute-start(bf16[384,128]{1,0:T(8,128)(2,1)S(1)} %get-tuple-element.39), channel_id=1, source_target_pairs={{0,2},{1,3},{2,0},{3,1},{4,6},{5,7},{6,4},{7,5},{8,10},{9,11},{10,... | collective-permute-start | bytes 294920 | tf_op jit(solution)/shard_map/ppermute | solution.py:455
  68.9 1.3 %collective-permute-start.15 = (f32[72,128]{1,0:T(8,128)S(1)}, f32[72,128]{1,0:T(8,128)S(1)}, u32[]{:S(2)}, u32[]{:S(2)}) collective-permute-start(f32[72,128]{1,0:T(8,128)S(1)} %get-tuple-element.46), channel_id=1, source_target_pairs={{0,8},{1,9},{2,10},{3,11},{4,12},{5,13},{6,14},{7,15},{8,0},{9,1},... | collective-permute-start | bytes 110600 | tf_op jit(solution)/shard_map/ppermute | solution.py:434
  70.2 4.0 %collective-permute-start.16 = (f32[72,128]{1,0:T(8,128)S(1)}, f32[72,128]{1,0:T(8,128)S(1)}, u32[]{:S(2)}, u32[]{:S(2)}) collective-permute-start(f32[72,128]{1,0:T(8,128)S(1)} %add.21), channel_id=1, source_target_pairs={{0,1},{1,0},{2,3},{3,2},{4,5},{5,4},{6,7},{7,6},{8,9},{9,8},{10,11... | collective-permute-start | bytes 110600 | tf_op jit(solution)/shard_map/ppermute | solution.py:434
  71.3 4.0 %collective-permute-start.17 = (f32[72,128]{1,0:T(8,128)S(1)}, f32[72,128]{1,0:T(8,128)S(1)}, u32[]{:S(2)}, u32[]{:S(2)}) collective-permute-start(f32[72,128]{1,0:T(8,128)S(1)} %add.21), channel_id=1, source_target_pairs={{0,16},{1,17},{2,18},{3,19},{4,20},{5,21},{6,22},{7,23},{8,24},{9,... | collective-permute-start | bytes 110600 | tf_op jit(solution)/shard_map/ppermute | solution.py:434
  72.8 4.9 %collective-permute-start.18 = (f32[72,128]{1,0:T(8,128)S(1)}, f32[72,128]{1,0:T(8,128)S(1)}, u32[]{:S(2)}, u32[]{:S(2)}) collective-permute-start(f32[72,128]{1,0:T(8,128)S(1)} %add.21), channel_id=1, source_target_pairs={{0,17},{1,16},{2,19},{3,18},{4,21},{5,20},{6,23},{7,22},{8,25},{9,... | collective-permute-start | bytes 110600 | tf_op jit(solution)/shard_map/ppermute | solution.py:434
  77.7 6.5 %collective-permute-start.19 = (f32[72,128]{1,0:T(8,128)S(1)}, f32[72,128]{1,0:T(8,128)S(1)}, u32[]{:S(2)}, u32[]{:S(2)}) collective-permute-start(f32[72,128]{1,0:T(8,128)S(1)} %add_add_fusion.1), channel_id=1, source_target_pairs={{0,2},{1,3},{2,0},{3,1},{4,6},{5,7},{6,4},{7,5},{8,10},{9,11},{10,... | collective-permute-start | bytes 110600 | tf_op jit(solution)/shard_map/ppermute | solution.py:434
  78.4 5.8 %collective-permute-start.20 = (f32[72,128]{1,0:T(8,128)S(1)}, f32[72,128]{1,0:T(8,128)S(1)}, u32[]{:S(2)}, u32[]{:S(2)}) collective-permute-start(f32[72,128]{1,0:T(8,128)S(1)} %add_add_fusion.1), channel_id=1, source_target_pairs={{0,4},{1,5},{2,6},{3,7},{4,0},{5,1},{6,2},{7,3},{8,12},{9,13},{10,... | collective-permute-start | bytes 110600 | tf_op jit(solution)/shard_map/ppermute | solution.py:434
  80.1 5.8 %collective-permute-start.21 = (f32[72,128]{1,0:T(8,128)S(1)}, f32[72,128]{1,0:T(8,128)S(1)}, u32[]{:S(2)}, u32[]{:S(2)}) collective-permute-start(f32[72,128]{1,0:T(8,128)S(1)} %add_add_fusion.1), channel_id=1, source_target_pairs={{0,6},{1,7},{2,4},{3,5},{4,2},{5,3},{6,0},{7,1},{8,14},{9,15},{10,... | collective-permute-start | bytes 110600 | tf_op jit(solution)/shard_map/ppermute | solution.py:434

commit v6 on v5

--- a/solution.py
+++ b/solution.py
@@ -14,7 +14,7 @@
 gram_shift = 0.001
 
 MIB = 2**20
-IMAGE_STEP = 1024
+IMAGE_STEP = 2048
 PART_STEP = 768
 LATE = 2
 PACK_SPARE = 8

time: 94.3 us -> 94.1 us (level)
  transfers between devices with their start and end apart: 22 -> 22, of which waited for: 8 -> 10; matrix products, arithmetic and copies ran while one was open for 0% -> 0% of each run, Pallas kernels for 19% -> 18%
where the time goes in v6:
time: 94.1 us; the launch traced here: 93.7 us
  Pallas kernels  37.7 us (40%)
  starting transfers between devices  29.8 us (32%)
  blocking collectives  13.7 us (15%)
  waiting for transfers between devices  11.6 us (12%)
    ppermute x15, starting transfers between devices, exchanged(): lax.ppermute(value, 'dev', [(j, j ^ first + i) for j in range(size)])  21.8 us
    all_to_all x1, blocking collectives, local(): lax.all_to_all(request, 'dev', split_axis=0, concat_axis=0, tiled=True)  13.7 us
    pallas_call x3, Pallas kernels, with_tiles(): pl.pallas_call(functools.partial(kernel, kept), out_shape=outs, in_specs=...  12.4 us
    pallas_call x1, Pallas kernels, local(): pl.pallas_call(load_kernel, out_shape=in_vmem((rows, slots * tile_size),...  8.19 us
    ppermute x7, starting transfers between devices, other(): lax.ppermute(value, axes, [(i, i ^ bits) for i in range(outer * inner)])  8.01 us
    pallas_call x1, Pallas kernels, local(): pl.pallas_call(functools.partial(finish_kernel, voxels), out_shape=(jax.S...  7.98 us
    ppermute x7, waiting for transfers between devices, other(): lax.ppermute(value, axes, [(i, i ^ bits) for i in range(outer * inner)])  6.76 us
    ppermute x15, waiting for transfers between devices, exchanged(): lax.ppermute(value, 'dev', [(j, j ^ first + i) for j in range(size)])  4.83 us
  transfers between devices with their start and end apart: 22, of which 10 were waited for; matrix products, arithmetic and copies ran while one was open for 0% of the time, Pallas kernels for 18%

profile of v6, /device:TPU:0, one launch (start us, length us, event | category | flops | bytes accessed | tf_op | source)
XLA Modules:
  0.0 93.7 jit_solution(11060444027818458613)
XLA Ops:
  0.6 1.9 %plan.1 = (s32[8,3]{1,0:T(8,128)}, s32[24]{0:T(128)}) custom-call(s32[1]{0:T(128)} %bitcast.me_ref, s32[24]{0:T(128)} %touched_ref.1, s32[2048]{0:T(1024)} %home_ref.1), custom_call_target="tpu_custom_call" | custom-call | tf_op jit(solution)/shard_map/plan/pallas_call | solution.py:472
  2.5 13.7 %all_to_all.11 = s32[8,1,3]{2,1,0:T(1,128)S(1)} all-to-all(s32[8,1,3]{2,1,0:T(1,128)} %bitcast.9), channel_id=1, replica_groups=mesh['grp'=4,'dev'=8] {'dev'}, dimensions={0} | all-to-all | bytes 192 | tf_op jit(solution)/shard_map/all_to_all | solution.py:502
  16.2 1.7 %serve.1 = (bf16[3,128,128]{2,1,0:T(8,128)(2,1)S(1)}, bf16[3,128,128]{2,1,0:T(8,128)(2,1)S(1)}, bf16[3,128,128]{2,1,0:T(8,128)(2,1)S(1)}, bf16[3,128,128]{2,1,0:...) custom-call(s32[1]{0:T(128)} %bitcast.me_ref, ...), custom_call_target="tpu_custom_call" | custom-call | tf_op jit(solution)/shard_map/serve/pallas_call | solution.py:503
  17.9 0.6 collective-permute-start
  18.5 0.6 collective-permute-start.1
  19.1 2.4 %collective-permute-start.2 = (bf16[3,128,128]{2,1,0:T(8,128)(2,1)S(1)}, bf16[3,128,128]{2,1,0:T(8,128)(2,1)S(1)}, u32[]{:S(2)}, u32[]{:S(2)}) collective-permute-start(bf16[3,128,128]{2,1,0:T(8,128)(2,1)S(1)} %get-tuple-element.30), channel_id=1, source_target_pairs={{0,3},{1,2},{2,1},{3,0},{4,7},{5,6},{6,5},{7,4},{8,11},{9,10},{10,... | collective-permute-start | bytes 294920 | tf_op jit(solution)/shard_map/ppermute | solution.py:455
  21.5 0.6 collective-permute-start.3
  22.0 2.4 %collective-permute-start.4 = (bf16[3,128,128]{2,1,0:T(8,128)(2,1)S(1)}, bf16[3,128,128]{2,1,0:T(8,128)(2,1)S(1)}, u32[]{:S(2)}, u32[]{:S(2)}) collective-permute-start(bf16[3,128,128]{2,1,0:T(8,128)(2,1)S(1)} %get-tuple-element.32), channel_id=1, source_target_pairs={{0,5},{1,4},{2,7},{3,6},{4,1},{5,0},{6,3},{7,2},{8,13},{9,12},{10,... | collective-permute-start | bytes 294920 | tf_op jit(solution)/shard_map/ppermute | solution.py:455
  24.4 8.2 %load.1.refs_0_ = bf16[4096,3072]{1,0:T(8,128)(2,1)S(1)} custom-call(s32[512]{0:T(512)} %ray_ref.1, s32[512]{0:T(512)} %col_ref.1, s32[24]{0:T(128)} %get-tuple-element.26.place_ref, bf16[512,128,128]{2,1,0:T(8,128)(2,1)} %tiles_ref.1, bf16[3,128,128]{2,1,0:T(8,128)(2,1)S(1)} %get-tuple-element.27._.refs_1_), custom_call_target="tpu_custom_call" | custom-call | tf_op jit(solution)/shard_map/load/pallas_call | solution.py:515
  32.6 0.0 collective-permute-done.refs_2_
  32.6 0.7 collective-permute-start.5
  33.2 0.0 collective-permute-done.1.refs_3_
  33.2 4.1 %collective-permute-start.6 = (bf16[3,128,128]{2,1,0:T(8,128)(2,1)S(1)}, bf16[3,128,128]{2,1,0:T(8,128)(2,1)S(1)}, u32[]{:S(2)}, u32[]{:S(2)}) collective-permute-start(bf16[3,128,128]{2,1,0:T(8,128)(2,1)S(1)} %get-tuple-element.34), channel_id=1, source_target_pairs={{0,7},{1,6},{2,5},{3,4},{4,3},{5,2},{6,1},{7,0},{8,15},{9,14},{10,... | collective-permute-start | bytes 294920 | tf_op jit(solution)/shard_map/ppermute | solution.py:455
  37.4 0.0 collective-permute-done.2.refs_4_
  37.4 4.2 %images_near.1.refs_1_ = f32[4096,128]{1,0:T(8,128)S(1)} custom-call(bf16[4096,3072]{1,0:T(8,128)(2,1)S(1)} %load.1.refs_0_, bf16[3,128,128]{2,1,0:T(8,128)(2,1)S(1)} %get-tuple-element.27._.refs_1_, bf16[3,128,128]{2,1,0:T(8,128)(2,1)S(1)} %collective-permute-done.refs_2_, bf16[3,128,128]{2,1,0:T(8,128)(2,1)S(1)} %collective-permute-done.1.refs_3_, ...), custom_call_target="tpu_custom_call" | custom-call | flops 1610612736 | bytes 8388608 | tf_op jit(solution)/shard_map/images_near/pallas_call | solution.py:527
  41.6 0.0 collective-permute-done.3.refs_2_
  41.6 0.0 collective-permute-done.4.refs_3_
  41.6 0.0 collective-permute-done.6.refs_5_
  41.6 5.4 %images_far.1 = (f32[8,128]{1,0:T(8,128)S(1)}, bf16[128,4096]{1,0:T(8,128)(2,1)S(1)}, bf16[384,128]{1,0:T(8,128)(2,1)S(1)}, bf16[384,128]{1,0:T(8,128)(2,1)S(1)}) custom-call(bf16[4096,3072]{1,0:T(8,128)(2,1)S(1)} %load.1.refs_0_, f32[4096,128]{1,0:T(8,128)S(1)} %images_near.1.refs_1_, bf16[3,128,128]{2,1,0:T(8,128)(2,1)S(1)} %collective-permute-done.3.refs_2_, ...), custom_call_target="tpu_custom_call" | custom-call | flops 3221225472 | bytes 8388608 | tf_op jit(solution)/shard_map/images_far/pallas_call | solution.py:527
  47.0 0.6 collective-permute-start.7
  47.6 0.2 collective-permute-start.11
  47.9 3.6 %collective-permute-start.12 = (bf16[384,128]{1,0:T(8,128)(2,1)S(1)}, bf16[384,128]{1,0:T(8,128)(2,1)S(1)}, u32[]{:S(2)}, u32[]{:S(2)}) collective-permute-start(bf16[384,128]{1,0:T(8,128)(2,1)S(1)} %get-tuple-element.42), channel_id=1, source_target_pairs={{0,5},{1,4},{2,7},{3,6},{4,1},{5,0},{6,3},{7,2},{8,13},{9,12},{10,... | collective-permute-start | bytes 294920 | tf_op jit(solution)/shard_map/ppermute | solution.py:455
  51.5 0.0 collective-permute-done.7.refs_2_
  51.5 2.9 %parts_near.1 = (f32[384,128]{1,0:T(8,128)S(1)}, bf16[384,128]{1,0:T(8,128)(2,1)S(1)}, bf16[384,128]{1,0:T(8,128)(2,1)S(1)}, bf16[384,128]{1,0:T(8,128)(2,1)S(1)...) custom-call(bf16[4096,3072]{1,0:T(8,128)(2,1)S(1)} %load.1.refs_0_, ...), custom_call_target="tpu_custom_call" | custom-call | flops 1610612736 | bytes 8388608 | tf_op jit(solution)/shard_map/parts_near/pallas_call | solution.py:527
  54.3 0.8 collective-permute-start.10
  55.1 1.5 %collective-permute-start.13 = (bf16[384,128]{1,0:T(8,128)(2,1)S(1)}, bf16[384,128]{1,0:T(8,128)(2,1)S(1)}, u32[]{:S(2)}, u32[]{:S(2)}) collective-permute-start(bf16[384,128]{1,0:T(8,128)(2,1)S(1)} %get-tuple-element.43), channel_id=1, source_target_pairs={{0,6},{1,7},{2,4},{3,5},{4,2},{5,3},{6,0},{7,1},{8,14},{9,15},{10,... | collective-permute-start | bytes 294920 | tf_op jit(solution)/shard_map/ppermute | solution.py:455
  56.6 3.0 %collective-permute-start.14 = (bf16[384,128]{1,0:T(8,128)(2,1)S(1)}, bf16[384,128]{1,0:T(8,128)(2,1)S(1)}, u32[]{:S(2)}, u32[]{:S(2)}) collective-permute-start(bf16[384,128]{1,0:T(8,128)(2,1)S(1)} %get-tuple-element.44), channel_id=1, source_target_pairs={{0,7},{1,6},{2,5},{3,4},{4,3},{5,2},{6,1},{7,0},{8,15},{9,14},{10,... | collective-permute-start | bytes 294920 | tf_op jit(solution)/shard_map/ppermute | solution.py:455
  59.6 0.8 collective-permute-start.8
  60.4 0.2 collective-permute-done.12.refs_5_
  60.6 2.1 %collective-permute-done.10.refs_3_ = bf16[384,128]{1,0:T(8,128)(2,1)S(1)} collective-permute-done((bf16[384,128]{1,0:T(8,128)(2,1)S(1)}, bf16[384,128]{1,0:T(8,128)(2,1)S(1)}, u32[]{:S(2)}, u32[]{:S(2)}) %collective-permute-start.10) | collective-permute-done | bytes 98336 | tf_op jit(solution)/shard_map/ppermute | solution.py:455
  62.7 1.4 %collective-permute-done.14.refs_7_ = bf16[384,128]{1,0:T(8,128)(2,1)S(1)} collective-permute-done((bf16[384,128]{1,0:T(8,128)(2,1)S(1)}, bf16[384,128]{1,0:T(8,128)(2,1)S(1)}, u32[]{:S(2)}, u32[]{:S(2)}) %collective-permute-start.14) | collective-permute-done | bytes 98336 | tf_op jit(solution)/shard_map/ppermute | solution.py:455
  64.1 1.0 %collective-permute-done.8.refs_1_ = bf16[384,128]{1,0:T(8,128)(2,1)S(1)} collective-permute-done((bf16[384,128]{1,0:T(8,128)(2,1)S(1)}, bf16[384,128]{1,0:T(8,128)(2,1)S(1)}, u32[]{:S(2)}, u32[]{:S(2)}) %collective-permute-start.8) | collective-permute-done | bytes 98336 | tf_op jit(solution)/shard_map/ppermute | solution.py:455
  65.1 0.1 collective-permute-done.9.refs_2_
  65.2 3.5 %collect.1 = (bf16[3072,256]{1,0:T(8,128)(2,1)S(1)}, f32[72,128]{1,0:T(8,128)S(1)}, s32[24]{0:T(128)S(1)}) custom-call(s32[1]{0:T(128)} %bitcast.me_ref, s32[8,3]{1,0:T(8,128)S(1)} %bitcast.7, f32[384,128]{1,0:T(8,128)S(1)} %get-tuple-element.37.refs_0_, bf16[384,128]{1,0:T(8,128)(2,1)S(1)} %collective-permute-done.8.refs_1_, ...), custom_call_target="tpu_custom_call" | custom-call | tf_op jit(solution)/shard_map/collect/pallas_call | solution.py:585
  68.7 0.1 collective-permute-start.15
  68.8 1.2 %collective-permute-done.15 = f32[72,128]{1,0:T(8,128)S(1)} collective-permute-done((f32[72,128]{1,0:T(8,128)S(1)}, f32[72,128]{1,0:T(8,128)S(1)}, u32[]{:S(2)}, u32[]{:S(2)}) %collective-permute-start.15) | collective-permute-done | bytes 36896 | tf_op jit(solution)/shard_map/ppermute | solution.py:434
  70.0 1.1 %collective-permute-start.16 = (f32[72,128]{1,0:T(8,128)S(1)}, f32[72,128]{1,0:T(8,128)S(1)}, u32[]{:S(2)}, u32[]{:S(2)}) collective-permute-start(f32[72,128]{1,0:T(8,128)S(1)} %add.21), channel_id=1, source_target_pairs={{0,1},{1,0},{2,3},{3,2},{4,5},{5,4},{6,7},{7,6},{8,9},{9,8},{10,11... | collective-permute-start | bytes 110600 | tf_op jit(solution)/shard_map/ppermute | solution.py:434
  71.1 1.5 %collective-permute-start.17 = (f32[72,128]{1,0:T(8,128)S(1)}, f32[72,128]{1,0:T(8,128)S(1)}, u32[]{:S(2)}, u32[]{:S(2)}) collective-permute-start(f32[72,128]{1,0:T(8,128)S(1)} %add.21), channel_id=1, source_target_pairs={{0,16},{1,17},{2,18},{3,19},{4,20},{5,21},{6,22},{7,23},{8,24},{9,... | collective-permute-start | bytes 110600 | tf_op jit(solution)/shard_map/ppermute | solution.py:434
  72.6 0.9 collective-permute-start.18
  73.5 0.5 collective-permute-done.16
  74.0 1.1 %collective-permute-done.17 = f32[72,128]{1,0:T(8,128)S(1)} collective-permute-done((f32[72,128]{1,0:T(8,128)S(1)}, f32[72,128]{1,0:T(8,128)S(1)}, u32[]{:S(2)}, u32[]{:S(2)}) %collective-permute-start.17) | collective-permute-done | bytes 36896 | tf_op jit(solution)/shard_map/ppermute | solution.py:434
  75.0 2.4 %collective-permute-done.18 = f32[72,128]{1,0:T(8,128)S(1)} collective-permute-done((f32[72,128]{1,0:T(8,128)S(1)}, f32[72,128]{1,0:T(8,128)S(1)}, u32[]{:S(2)}, u32[]{:S(2)}) %collective-permute-start.18) | collective-permute-done | bytes 36896 | tf_op jit(solution)/shard_map/ppermute | solution.py:434
  77.5 0.6 collective-permute-start.19
  78.0 1.8 %collective-permute-start.20 = (f32[72,128]{1,0:T(8,128)S(1)}, f32[72,128]{1,0:T(8,128)S(1)}, u32[]{:S(2)}, u32[]{:S(2)}) collective-permute-start(f32[72,128]{1,0:T(8,128)S(1)} %add_add_fusion.1), channel_id=1, source_target_pairs={{0,4},{1,5},{2,6},{3,7},{4,0},{5,1},{6,2},{7,3},{8,12},{9,13},{10,... | collective-permute-start | bytes 110600 | tf_op jit(solution)/shard_map/ppermute | solution.py:434
  79.8 2.1 %collective-permute-start.21 = (f32[72,128]{1,0:T(8,128)S(1)}, f32[72,128]{1,0:T(8,128)S(1)}, u32[]{:S(2)}, u32[]{:S(2)}) collective-permute-start(f32[72,128]{1,0:T(8,128)S(1)} %add_add_fusion.1), channel_id=1, source_target_pairs={{0,6},{1,7},{2,4},{3,5},{4,2},{5,3},{6,0},{7,1},{8,14},{9,15},{10,... | collective-permute-start | bytes 110600 | tf_op jit(solution)/shard_map/ppermute | solution.py:434
  81.9 2.0 %zeros.1.zeroed_ref = f32[8192,128]{1,0:T(8,128)} custom-call(), custom_call_target="tpu_custom_call" | custom-call | tf_op jit(solution)/shard_map/zeros/pallas_call | solution.py:577
  84.0 1.6 %collective-permute-done.21 = f32[72,128]{1,0:T(8,128)S(1)} collective-permute-done((f32[72,128]{1,0:T(8,128)S(1)}, f32[72,128]{1,0:T(8,128)S(1)}, u32[]{:S(2)}, u32[]{:S(2)}) %collective-permute-start.21) | collective-permute-done | bytes 36896 | tf_op jit(solution)/shard_map/ppermute | solution.py:434
  85.6 8.0 %finish.1 = (f32[8192,128]{1,0:T(8,128)}, f32[128,128]{1,0:T(8,128)}) custom-call(s32[24]{0:T(128)S(1)} %get-tuple-element.45.block_ref, f32[72,128]{1,0:T(8,128)S(1)} %add_add_fusion.pack_ref, bf16[3072,256]{1,0:T(8,128)(2,1)S(1)} %get-tuple-element.47.normal_ref, f32[8192,128]{1,0:T(8,128)} %zeros.1.zeroed_ref), custom_call_target="tpu_custom_call", output_to_operand_aliasing={{0}: (3, {})} | custom-call | tf_op jit(solution)/shard_map/finish/pallas_call | solution.py:603
  (9 shorter events, 0.0 us)
Async XLA Ops:
  17.9 14.7 %collective-permute-start = (bf16[3,128,128]{2,1,0:T(8,128)(2,1)S(1)}, bf16[3,128,128]{2,1,0:T(8,128)(2,1)S(1)}, u32[]{:S(2)}, u32[]{:S(2)}) collective-permute-start(bf16[3,128,128]{2,1,0:T(8,128)(2,1)S(1)} %get-tuple-element.28), channel_id=1, source_target_pairs={{0,1},{1,0},{2,3},{3,2},{4,5},{5,4},{6,7},{7,6},{8,9},{9,8},{10,11... | collective-permute-start | bytes 294920 | tf_op jit(solution)/shard_map/ppermute | solution.py:455
  18.5 14.7 %collective-permute-start.1 = (bf16[3,128,128]{2,1,0:T(8,128)(2,1)S(1)}, bf16[3,128,128]{2,1,0:T(8,128)(2,1)S(1)}, u32[]{:S(2)}, u32[]{:S(2)}) collective-permute-start(bf16[3,128,128]{2,1,0:T(8,128)(2,1)S(1)} %get-tuple-element.29), channel_id=1, source_target_pairs={{0,2},{1,3},{2,0},{3,1},{4,6},{5,7},{6,4},{7,5},{8,10},{9,11},{10,... | collective-permute-start | bytes 294920 | tf_op jit(solution)/shard_map/ppermute | solution.py:455
  19.1 18.3 %collective-permute-start.2 = (bf16[3,128,128]{2,1,0:T(8,128)(2,1)S(1)}, bf16[3,128,128]{2,1,0:T(8,128)(2,1)S(1)}, u32[]{:S(2)}, u32[]{:S(2)}) collective-permute-start(bf16[3,128,128]{2,1,0:T(8,128)(2,1)S(1)} %get-tuple-element.30), channel_id=1, source_target_pairs={{0,3},{1,2},{2,1},{3,0},{4,7},{5,6},{6,5},{7,4},{8,11},{9,10},{10,... | collective-permute-start | bytes 294920 | tf_op jit(solution)/shard_map/ppermute | solution.py:455
  21.5 20.1 %collective-permute-start.3 = (bf16[3,128,128]{2,1,0:T(8,128)(2,1)S(1)}, bf16[3,128,128]{2,1,0:T(8,128)(2,1)S(1)}, u32[]{:S(2)}, u32[]{:S(2)}) collective-permute-start(bf16[3,128,128]{2,1,0:T(8,128)(2,1)S(1)} %get-tuple-element.31), channel_id=1, source_target_pairs={{0,4},{1,5},{2,6},{3,7},{4,0},{5,1},{6,2},{7,3},{8,12},{9,13},{10,... | collective-permute-start | bytes 294920 | tf_op jit(solution)/shard_map/ppermute | solution.py:455
  22.0 19.6 %collective-permute-start.4 = (bf16[3,128,128]{2,1,0:T(8,128)(2,1)S(1)}, bf16[3,128,128]{2,1,0:T(8,128)(2,1)S(1)}, u32[]{:S(2)}, u32[]{:S(2)}) collective-permute-start(bf16[3,128,128]{2,1,0:T(8,128)(2,1)S(1)} %get-tuple-element.32), channel_id=1, source_target_pairs={{0,5},{1,4},{2,7},{3,6},{4,1},{5,0},{6,3},{7,2},{8,13},{9,12},{10,... | collective-permute-start | bytes 294920 | tf_op jit(solution)/shard_map/ppermute | solution.py:455
  32.6 9.0 %collective-permute-start.5 = (bf16[3,128,128]{2,1,0:T(8,128)(2,1)S(1)}, bf16[3,128,128]{2,1,0:T(8,128)(2,1)S(1)}, u32[]{:S(2)}, u32[]{:S(2)}) collective-permute-start(bf16[3,128,128]{2,1,0:T(8,128)(2,1)S(1)} %get-tuple-element.33), channel_id=1, source_target_pairs={{0,6},{1,7},{2,4},{3,5},{4,2},{5,3},{6,0},{7,1},{8,14},{9,15},{10,... | collective-permute-start | bytes 294920 | tf_op jit(solution)/shard_map/ppermute | solution.py:455
  33.2 8.4 %collective-permute-start.6 = (bf16[3,128,128]{2,1,0:T(8,128)(2,1)S(1)}, bf16[3,128,128]{2,1,0:T(8,128)(2,1)S(1)}, u32[]{:S(2)}, u32[]{:S(2)}) collective-permute-start(bf16[3,128,128]{2,1,0:T(8,128)(2,1)S(1)} %get-tuple-element.34), channel_id=1, source_target_pairs={{0,7},{1,6},{2,5},{3,4},{4,3},{5,2},{6,1},{7,0},{8,15},{9,14},{10,... | collective-permute-start | bytes 294920 | tf_op jit(solution)/shard_map/ppermute | solution.py:455
  47.0 4.5 %collective-permute-start.7 = (f32[8,128]{1,0:T(8,128)S(1)}, f32[8,128]{1,0:T(8,128)S(1)}, u32[]{:S(2)}, u32[]{:S(2)}) collective-permute-start(f32[8,128]{1,0:T(8,128)S(1)} %get-tuple-element.36), channel_id=1, source_target_pairs={{0,1},{1,0},{2,3},{3,2},{4,5},{5,4},{6,7},{7,6},{8,9},{9,8},{10,11... | collective-permute-start | bytes 12296 | tf_op jit(solution)/shard_map/ppermute | solution.py:455
  47.6 12.0 %collective-permute-start.11 = (bf16[384,128]{1,0:T(8,128)(2,1)S(1)}, bf16[384,128]{1,0:T(8,128)(2,1)S(1)}, u32[]{:S(2)}, u32[]{:S(2)}) collective-permute-start(bf16[384,128]{1,0:T(8,128)(2,1)S(1)} %get-tuple-element.41), channel_id=1, source_target_pairs={{0,4},{1,5},{2,6},{3,7},{4,0},{5,1},{6,2},{7,3},{8,12},{9,13},{10,... | collective-permute-start | bytes 294920 | tf_op jit(solution)/shard_map/ppermute | solution.py:455
  47.9 12.7 %collective-permute-start.12 = (bf16[384,128]{1,0:T(8,128)(2,1)S(1)}, bf16[384,128]{1,0:T(8,128)(2,1)S(1)}, u32[]{:S(2)}, u32[]{:S(2)}) collective-permute-start(bf16[384,128]{1,0:T(8,128)(2,1)S(1)} %get-tuple-element.42), channel_id=1, source_target_pairs={{0,5},{1,4},{2,7},{3,6},{4,1},{5,0},{6,3},{7,2},{8,13},{9,12},{10,... | collective-permute-start | bytes 294920 | tf_op jit(solution)/shard_map/ppermute | solution.py:455
  54.3 8.4 %collective-permute-start.10 = (bf16[384,128]{1,0:T(8,128)(2,1)S(1)}, bf16[384,128]{1,0:T(8,128)(2,1)S(1)}, u32[]{:S(2)}, u32[]{:S(2)}) collective-permute-start(bf16[384,128]{1,0:T(8,128)(2,1)S(1)} %get-tuple-element.40), channel_id=1, source_target_pairs={{0,3},{1,2},{2,1},{3,0},{4,7},{5,6},{6,5},{7,4},{8,11},{9,10},{10,... | collective-permute-start | bytes 294920 | tf_op jit(solution)/shard_map/ppermute | solution.py:455
  55.1 7.6 %collective-permute-start.13 = (bf16[384,128]{1,0:T(8,128)(2,1)S(1)}, bf16[384,128]{1,0:T(8,128)(2,1)S(1)}, u32[]{:S(2)}, u32[]{:S(2)}) collective-permute-start(bf16[384,128]{1,0:T(8,128)(2,1)S(1)} %get-tuple-element.43), channel_id=1, source_target_pairs={{0,6},{1,7},{2,4},{3,5},{4,2},{5,3},{6,0},{7,1},{8,14},{9,15},{10,... | collective-permute-start | bytes 294920 | tf_op jit(solution)/shard_map/ppermute | solution.py:455
  56.6 7.5 %collective-permute-start.14 = (bf16[384,128]{1,0:T(8,128)(2,1)S(1)}, bf16[384,128]{1,0:T(8,128)(2,1)S(1)}, u32[]{:S(2)}, u32[]{:S(2)}) collective-permute-start(bf16[384,128]{1,0:T(8,128)(2,1)S(1)} %get-tuple-element.44), channel_id=1, source_target_pairs={{0,7},{1,6},{2,5},{3,4},{4,3},{5,2},{6,1},{7,0},{8,15},{9,14},{10,... | collective-permute-start | bytes 294920 | tf_op jit(solution)/shard_map/ppermute | solution.py:455
  59.6 5.5 %collective-permute-start.8 = (bf16[384,128]{1,0:T(8,128)(2,1)S(1)}, bf16[384,128]{1,0:T(8,128)(2,1)S(1)}, u32[]{:S(2)}, u32[]{:S(2)}) collective-permute-start(bf16[384,128]{1,0:T(8,128)(2,1)S(1)} %get-tuple-element.38), channel_id=1, source_target_pairs={{0,1},{1,0},{2,3},{3,2},{4,5},{5,4},{6,7},{7,6},{8,9},{9,8},{10,11... | collective-permute-start | bytes 294920 | tf_op jit(solution)/shard_map/ppermute | solution.py:455
  60.6 4.6 %collective-permute-start.9 = (bf16[384,128]{1,0:T(8,128)(2,1)S(1)}, bf16[384,128]{1,0:T(8,128)(2,1)S(1)}, u32[]{:S(2)}, u32[]{:S(2)}) collective-permute-start(bf16[384,128]{1,0:T(8,128)(2,1)S(1)} %get-tuple-element.39), channel_id=1, source_target_pairs={{0,2},{1,3},{2,0},{3,1},{4,6},{5,7},{6,4},{7,5},{8,10},{9,11},{10,... | collective-permute-start | bytes 294920 | tf_op jit(solution)/shard_map/ppermute | solution.py:455
  68.7 1.3 %collective-permute-start.15 = (f32[72,128]{1,0:T(8,128)S(1)}, f32[72,128]{1,0:T(8,128)S(1)}, u32[]{:S(2)}, u32[]{:S(2)}) collective-permute-start(f32[72,128]{1,0:T(8,128)S(1)} %get-tuple-element.46), channel_id=1, source_target_pairs={{0,8},{1,9},{2,10},{3,11},{4,12},{5,13},{6,14},{7,15},{8,0},{9,1},... | collective-permute-start | bytes 110600 | tf_op jit(solution)/shard_map/ppermute | solution.py:434
  70.0 4.0 %collective-permute-start.16 = (f32[72,128]{1,0:T(8,128)S(1)}, f32[72,128]{1,0:T(8,128)S(1)}, u32[]{:S(2)}, u32[]{:S(2)}) collective-permute-start(f32[72,128]{1,0:T(8,128)S(1)} %add.21), channel_id=1, source_target_pairs={{0,1},{1,0},{2,3},{3,2},{4,5},{5,4},{6,7},{7,6},{8,9},{9,8},{10,11... | collective-permute-start | bytes 110600 | tf_op jit(solution)/shard_map/ppermute | solution.py:434
  71.1 4.0 %collective-permute-start.17 = (f32[72,128]{1,0:T(8,128)S(1)}, f32[72,128]{1,0:T(8,128)S(1)}, u32[]{:S(2)}, u32[]{:S(2)}) collective-permute-start(f32[72,128]{1,0:T(8,128)S(1)} %add.21), channel_id=1, source_target_pairs={{0,16},{1,17},{2,18},{3,19},{4,20},{5,21},{6,22},{7,23},{8,24},{9,... | collective-permute-start | bytes 110600 | tf_op jit(solution)/shard_map/ppermute | solution.py:434
  72.6 4.9 %collective-permute-start.18 = (f32[72,128]{1,0:T(8,128)S(1)}, f32[72,128]{1,0:T(8,128)S(1)}, u32[]{:S(2)}, u32[]{:S(2)}) collective-permute-start(f32[72,128]{1,0:T(8,128)S(1)} %add.21), channel_id=1, source_target_pairs={{0,17},{1,16},{2,19},{3,18},{4,21},{5,20},{6,23},{7,22},{8,25},{9,... | collective-permute-start | bytes 110600 | tf_op jit(solution)/shard_map/ppermute | solution.py:434
  77.5 6.5 %collective-permute-start.19 = (f32[72,128]{1,0:T(8,128)S(1)}, f32[72,128]{1,0:T(8,128)S(1)}, u32[]{:S(2)}, u32[]{:S(2)}) collective-permute-start(f32[72,128]{1,0:T(8,128)S(1)} %add_add_fusion.1), channel_id=1, source_target_pairs={{0,2},{1,3},{2,0},{3,1},{4,6},{5,7},{6,4},{7,5},{8,10},{9,11},{10,... | collective-permute-start | bytes 110600 | tf_op jit(solution)/shard_map/ppermute | solution.py:434
  78.0 6.0 %collective-permute-start.20 = (f32[72,128]{1,0:T(8,128)S(1)}, f32[72,128]{1,0:T(8,128)S(1)}, u32[]{:S(2)}, u32[]{:S(2)}) collective-permute-start(f32[72,128]{1,0:T(8,128)S(1)} %add_add_fusion.1), channel_id=1, source_target_pairs={{0,4},{1,5},{2,6},{3,7},{4,0},{5,1},{6,2},{7,3},{8,12},{9,13},{10,... | collective-permute-start | bytes 110600 | tf_op jit(solution)/shard_map/ppermute | solution.py:434
  79.8 5.8 %collective-permute-start.21 = (f32[72,128]{1,0:T(8,128)S(1)}, f32[72,128]{1,0:T(8,128)S(1)}, u32[]{:S(2)}, u32[]{:S(2)}) collective-permute-start(f32[72,128]{1,0:T(8,128)S(1)} %add_add_fusion.1), channel_id=1, source_target_pairs={{0,6},{1,7},{2,4},{3,5},{4,2},{5,3},{6,0},{7,1},{8,14},{9,15},{10,... | collective-permute-start | bytes 110600 | tf_op jit(solution)/shard_map/ppermute | solution.py:434
